TPU v7x, 128 devices: a whole 4x4x4 slice. The times are simulated.
128 devices in a mesh: dp: 4 (over x), expert: 32 (over y, z, core).
Axes of the slice: x: 4, y: 4, z: 4, core: 2. Of those that a mesh axis runs over, the one named last changes fastest.
Arguments:
- hidden_states: bfloat16 [8192, 3584], P(('dp', 'expert')), may hold values from -6 to 6
- router_scores: float32 [8192, 8], P(('dp', 'expert')), may hold values from 0.05 to 1
- copy_route: int32 [8192, 8], P(('dp', 'expert')), may hold values from 0 to 63, all different within a row; in each aligned block of 64 rows (0 to 63, 64 to 127, ...) at most 12 rows name the same one
- slot_source: int32 [32], replicated, may hold values from 0 to 31, as said below
- gate_proj: bfloat16 [32, 3584, 2048], P('expert', None, 'dp'), may hold values from -0.09375 to 0.09375
- up_proj: bfloat16 [32, 3584, 2048], P('expert', None, 'dp'), may hold values from -0.09375 to 0.09375
- down_proj: bfloat16 [32, 2048, 3584], P('expert', 'dp'), may hold values from -0.125 to 0.125
Outputs:
- moe_output: bfloat16 [8192, 3584], P(('dp', 'expert'))
Inputs may be any that keep to these rules, and one draw needn't show every extreme that they name: `copy_route`: copies 0 to 31 are the native experts; copy 32 + s is redundant slot s, held on index s of expert. A token's 8 routes name different copies. Within the 64 rows of one device, no copy is named by more than 12 routes. `slot_source`: 8 distinct experts appear, each in exactly 4 slots.
All inputs are finite; a program needn't handle non-finite values.
Results may differ from a plain program's by a relative error of at most 0.017.
Values may be sent and summed in bfloat16 or wider, within the bound.
No kernel may reach another device: no remote copies, remote signals or barrier semaphores. Data moves between devices by JAX's collectives and lax.ppermute only.
A program may use at most 192 MiB of HBM per device.

v0:
```python
import jax
import jax.numpy as jnp
from jax import lax
from jax.sharding import PartitionSpec as P

TOP = 8


route_scale = 2.5


def slot_owners(routing, experts, capacity):
    tok_rows, top_count = routing.shape
    flat_route = routing.reshape(-1)
    copy_ids = jnp.arange(2 * experts, dtype=jnp.int32)
    matches = (flat_route[:, None] == copy_ids[None, :]).astype(jnp.int32)
    ranking = jnp.sum(jnp.cumsum(matches, axis=0) * matches, axis=1) - 1
    places = flat_route * capacity + ranking
    owner_rows = jnp.arange(tok_rows * top_count, dtype=jnp.int32) // top_count
    owners = jnp.full((2 * experts * capacity,), -1, jnp.int32).at[places].set(owner_rows)
    return (owners.reshape(2, experts, capacity), places)


def fetch_rows(tokens, owners):
    picked = tokens[jnp.maximum(owners, 0)]
    return jnp.where((owners >= 0)[..., None], picked, jnp.zeros((), tokens.dtype))


def per_device(
    hidden_states, router_scores, copy_route, slot_source, gate_proj, up_proj, down_proj
):
    experts = lax.axis_size("expert")
    tok_rows, widths = hidden_states.shape
    capacity = (3 * tok_rows * TOP + 4 * experts - 1) // (4 * experts)
    tables = (
        lax.all_to_all(gate_proj, "expert", split_axis=1, concat_axis=0, tiled=True),
        lax.all_to_all(up_proj, "expert", split_axis=1, concat_axis=0, tiled=True),
        lax.all_to_all(down_proj, "expert", split_axis=1, concat_axis=0, tiled=True),
    )
    selected = (
        jnp.take(tables[0], slot_source, axis=0),
        jnp.take(tables[1], slot_source, axis=0),
        jnp.take(tables[2], slot_source, axis=0),
    )
    slot_gate, slot_up, slot_down = (
        lax.all_to_all(selected[0], "expert", split_axis=0, concat_axis=1, tiled=True),
        lax.all_to_all(selected[1], "expert", split_axis=0, concat_axis=1, tiled=True),
        lax.all_to_all(selected[2], "expert", split_axis=0, concat_axis=1, tiled=True),
    )
    stacked_gate = jnp.concatenate((gate_proj, slot_gate), axis=0)
    stacked_up = jnp.concatenate((up_proj, slot_up), axis=0)
    stacked_down = jnp.concatenate((down_proj, slot_down), axis=0)
    owners, places = slot_owners(copy_route, experts, capacity)
    send_rows = fetch_rows(hidden_states, owners)
    arrived = lax.all_to_all(send_rows, "expert", split_axis=1, concat_axis=1, tiled=True)
    piece = lax.all_gather(arrived[:, None], "dp", axis=1, tiled=True)
    flat_rows = piece.reshape(2, -1, widths)
    gate_value = jnp.einsum(
        "krd,kdh->krh", flat_rows, stacked_gate, preferred_element_type=jnp.float32
    )
    up_value = jnp.einsum("krd,kdh->krh", flat_rows, stacked_up, preferred_element_type=jnp.float32)
    activated = (jax.nn.silu(gate_value) * up_value).astype(jnp.bfloat16)
    result = jnp.einsum("krh,khd->krd", activated, stacked_down, preferred_element_type=jnp.float32)
    partial_terms = result.reshape(piece.shape)
    summed = lax.psum_scatter(
        partial_terms.astype(jnp.bfloat16), "dp", scatter_dimension=1, tiled=True
    )
    returned = lax.all_to_all(summed, "expert", split_axis=2, concat_axis=2, tiled=True)
    gathered = returned.reshape(-1, widths)[places].reshape(tok_rows, TOP, widths)
    gate_weights = route_scale * router_scores / jnp.sum(router_scores, axis=1, keepdims=True)
    output = jnp.einsum("tk,tkd->td", gate_weights, gathered.astype(jnp.float32))
    return output.astype(jnp.bfloat16)


def solution(mesh):
    placed = (
        P(("dp", "expert"), None),
        P(("dp", "expert"), None),
        P(("dp", "expert"), None),
        P(),
        P("expert", None, "dp"),
        P("expert", None, "dp"),
        P("expert", "dp", None),
    )
    return jax.shard_map(
        per_device, mesh=mesh, in_specs=placed, out_specs=P(("dp", "expert"), None), check_vma=False
    )
```

profile of v0, /device:TPU:32, one launch (start us, length us, event | category | flops | bytes accessed | tf_op | source)
XLA Modules:
  0.0 893.3 jit_solution(4613830107713654108)
XLA Ops:
  12.6 5.5 gather_fusion
  18.1 9.3 %reshape.132 = bf16[2,32,12,3584]{3,2,1,0:T(8,128)(2,1)} reshape(bf16[768,3584]{1,0:T(8,128)(2,1)} %gather_fusion) | data formatting | bytes 11010048 | tf_op jit(solution)/shard_map/gather | solution.py:25
  27.4 3.6 broadcast_select_fusion
  31.1 21.7 %copy.48 = bf16[2,32,12,3584]{3,0,2,1:T(2,128)(2,1)S(1)} copy(bf16[2,32,12,3584]{3,2,1,0:T(8,128)(2,1)S(1)} %broadcast_select_fusion) | data formatting | bytes 11010048 | tf_op jit(solution)/shard_map/jit(_where)/select_n | solution.py:26
  52.8 71.7 %all_to_all.82 = bf16[2,32,12,3584]{3,0,2,1:T(2,128)(2,1)} all-to-all(bf16[2,32,12,3584]{3,0,2,1:T(2,128)(2,1)S(1)} %copy.48), channel_id=1, replica_groups=mesh['dp'=4,'expert'=32] {'expert'}, dimensions={1} | all-to-all | bytes 11010048 | tf_op jit(solution)/shard_map/all_to_all | solution.py:55
  124.5 7.8 copy.78
  132.7 25.4 %reduce.2 = bf16[3584,512]{1,0:T(8,128)(2,1)} reduce(bf16[3584,1,512]{2,1,0:T(2,128)(2,1)} %bitcast.50, bf16[]{:T(256)} %broadcast.126), dimensions={1}, to_apply=%bitcast.48.reduce_sub_computation | reduce | bytes 7340034
  158.1 9.2 %reshape.181 = bf16[32,2,28672]{2,1,0:T(2,128)(2,1)} reshape(bf16[3584,512]{1,0:T(8,128)(2,1)} %reduce.2) | data formatting | bytes 7340032
  167.3 6.9 all-to-all-start.1
  174.2 7.8 copy.77
  182.0 25.2 %reduce.3 = bf16[3584,512]{1,0:T(8,128)(2,1)} reduce(bf16[3584,1,512]{2,1,0:T(2,128)(2,1)} %bitcast.55, bf16[]{:T(256)} %broadcast.126), dimensions={1}, to_apply=%bitcast.47.reduce_sub_computation | reduce | bytes 7340034
  207.2 9.2 %reshape.179 = bf16[32,2,28672]{2,1,0:T(2,128)(2,1)} reshape(bf16[3584,512]{1,0:T(8,128)(2,1)} %reduce.3) | data formatting | bytes 7340032
  216.3 4.1 all-to-all-done.1
  220.4 6.5 all-to-all-start.3
  226.9 7.8 copy.76
  234.7 25.2 %reduce.4 = bf16[512,3584]{1,0:T(8,128)(2,1)} reduce(bf16[512,1,3584]{2,1,0:T(2,128)(2,1)} %bitcast.51, bf16[]{:T(256)} %broadcast.126), dimensions={1}, to_apply=%bitcast.46.reduce_sub_computation | reduce | bytes 7340034
  260.0 9.2 %reshape.183 = bf16[32,2,28672]{2,1,0:T(2,128)(2,1)} reshape(bf16[512,3584]{1,0:T(8,128)(2,1)} %reduce.4) | data formatting | bytes 7340032
  269.1 4.6 all-to-all-done.3
  273.8 6.3 all-to-all-start.5
  280.1 19.3 %reshape.182 = bf16[3584,1,512]{2,1,0:T(2,128)(2,1)} reshape(bf16[32,2,28672]{2,1,0:T(2,128)(2,1)} %all-to-all-done.1) | data formatting | bytes 7340032
  299.4 5.9 copy.60
  305.4 19.3 %reshape.180 = bf16[3584,1,512]{2,1,0:T(2,128)(2,1)} reshape(bf16[32,2,28672]{2,1,0:T(2,128)(2,1)} %all-to-all-done.3) | data formatting | bytes 7340032
  324.7 6.0 copy.61
  330.7 4.7 gather_fusion.3
  335.3 4.6 gather_fusion.4
  340.0 6.8 broadcast_select_fusion.2
  346.8 51.3 %all_to_all.83 = bf16[32,112,512]{2,1,0:T(8,128)(2,1)} all-to-all(bf16[32,112,512]{2,1,0:T(8,128)(2,1)} %get-tuple-element.7), channel_id=1, replica_groups=mesh['dp'=4,'expert'=32] {'expert'}, dimensions={0} | all-to-all | bytes 7340032 | tf_op jit(solution)/shard_map/all_to_all | solution.py:47
  398.1 5.7 all-to-all-start.2
  403.8 19.3 %reshape.184 = bf16[512,1,3584]{2,1,0:T(2,128)(2,1)} reshape(bf16[32,2,28672]{2,1,0:T(2,128)(2,1)} %all-to-all-done.5) | data formatting | bytes 7340032
  423.2 5.7 copy.62
  428.9 4.6 gather_fusion.1
  433.5 4.3 broadcast_select_fusion.3
  437.8 13.4 %all-to-all-done.2 = bf16[32,112,512]{2,1,0:T(8,128)(2,1)} async-done(((bf16[32,112,512]{2,1,0:T(8,128)(2,1)}), bf16[32,112,512]{2,1,0:T(8,128)(2,1)}, u32[]{:S(2)}, u32[]{:S(2)}) %all-to-all-start.2) | async-done | bytes 3670048 | tf_op jit(solution)/shard_map/all_to_all | solution.py:46
  451.2 5.5 all-to-all-start.6
  456.8 21.4 %fusion = f32[2,1536,512]{2,1,0:T(8,128)} fusion(bf16[2,1536,3584]{2,0,1:T(2,128)(2,1)} %bitcast.63, bf16[1,3584,512]{2,1,0:T(8,128)(2,1)} %bitcast.59, bf16[1,3584,512]{2,1,0:T(8,128)(2,1)} %param.14), kind=kOutput, calls=%fused_computation.7 | convolution fusion | flops 11277959168 | bytes 35651584 | tf_op jit(solution)/shard_map/krd,kdh->krh/dot_general | solution.py:61
  478.2 22.7 %multiply_convert_fusion = bf16[2,1536,512]{2,1,0:T(8,128)(2,1)} fusion(f32[2,1536,512]{2,1,0:T(8,128)} %fusion, bf16[1,3584,512]{2,1,0:T(8,128)(2,1)} %bitcast.5, bf16[1,3584,512]{2,1,0:T(8,128)(2,1)} %param.13, bf16[2,1536,3584]{2,0,1:T(2,128)(2,1)} %bitcast.64), kind=kOutput, calls=%fused_computation.21 | convolution fusion | flops 11287396352 | bytes 38797312 | tf_op jit(solution)/shard_map/krd,kdh->krh/dot_general | solution.py:58
  500.8 2.7 all-to-all-done.6
  503.6 19.0 %convolution_convert_fusion = bf16[2,1536,3584]{2,1,0:T(8,128)(2,1)} fusion(bf16[2,1536,512]{2,1,0:T(8,128)(2,1)} %multiply_convert_fusion, bf16[1,512,3584]{2,1,0:T(8,128)(2,1)} %bitcast.7, bf16[1,512,3584]{2,1,0:T(8,128)(2,1)} %param.15), kind=kOutput, calls=%fused_computation.6 | convolution fusion | flops 11288969216 | bytes 32505856 | tf_op jit(solution)/shard_map/krh,khd->krd/dot_general | solution.py:63
  522.5 39.6 %copy.54 = bf16[2,1536,3584]{2,0,1:T(2,128)(2,1)S(1)} copy(bf16[2,1536,3584]{2,1,0:T(8,128)(2,1)} %convolution_convert_fusion) | data formatting | bytes 44040192 | tf_op jit(solution)/shard_map/convert_element_type | solution.py:66
  562.1 8.1 copy.55
  570.3 190.0 %reduce-scatter.2.cloned.1.call-done = bf16[2,1,32,12,3584]{4,2,3,0,1:T(8,128)(2,1)} async-done(((bf16[2,4,32,12,3584]{4,2,3,0,1:T(8,128)(2,1)}), bf16[2,1,32,12,3584]{4,2,3,0,1:T(8,128)(2,1)}) %reduce-scatter.2.cloned.1.call-update) | async-done | bytes 5505040 | tf_op jit(solution)/shard_map/reduce_scatter | solution.py:65
  760.3 11.4 %copy.56 = bf16[2,1,32,12,3584]{4,0,3,1,2:T(2,128)(2,1)} copy(bf16[2,1,32,12,3584]{4,2,3,0,1:T(8,128)(2,1)} %reduce-scatter.2.cloned.1.call-done) | data formatting | bytes 11010048 | tf_op jit(solution)/shard_map/reduce_scatter | solution.py:65
  771.7 7.7 all-to-all-start.7
  779.5 75.0 %all-to-all-done.7 = bf16[2,1,32,12,3584]{4,0,3,1,2:T(2,128)(2,1)} async-done(((bf16[2,1,32,12,3584]{4,0,3,1,2:T(2,128)(2,1)}), bf16[2,1,32,12,3584]{4,0,3,1,2:T(2,128)(2,1)}, u32[]{:S(2)}, u32[]{:S(2)}) %all-to-all-start.7) | async-done | bytes 5505056 | tf_op jit(solution)/shard_map/all_to_all | solution.py:68
  854.5 6.9 copy.57
  861.5 9.4 %reshape.113 = bf16[768,3584]{1,0:T(8,128)(2,1)} reshape(bf16[2,1,32,12,3584]{4,3,2,0,1:T(8,128)(2,1)} %copy.57) | data formatting | bytes 11010048 | tf_op jit(solution)/shard_map/reshape | solution.py:69
  870.8 11.2 %gather_fusion.2 = bf16[512,3584]{1,0:T(8,128)(2,1)} fusion(bf16[768,3584]{1,0:T(8,128)(2,1)} %reshape.113, s32[1024]{0:T(1024)S(1)} %pad_clamp_fusion), kind=kCustom, calls=%fused_computation.4 | custom fusion | bytes 7342080 | tf_op jit(solution)/shard_map/gather | solution.py:69
  882.0 3.1 fusion.17
  (47 shorter events, 7.7 us)
Async XLA Ops:
  6.5 6.0 copy-start
  6.5 450.2 %all-gather.3.cloned.1.call-start = ((), (), s32[]{:S(2)}) async-start(), calls=%async_computation.10 | async-start | bytes 27525120 | tf_op jit(solution)/shard_map/all_gather | solution.py:56
  10.1 8.0 copy-start.3
  167.3 53.1 %all-to-all-start.1 = ((bf16[32,2,28672]{2,1,0:T(2,128)(2,1)}), bf16[32,2,28672]{2,1,0:T(2,128)(2,1)}, u32[]{:S(2)}, u32[]{:S(2)}) async-start(bf16[32,2,28672]{2,1,0:T(2,128)(2,1)} %reshape.181), calls=%async_computation.1 | async-start | bytes 7340032 | tf_op jit(solution)/shard_map/all_to_all | solution.py:36
  220.4 53.4 %all-to-all-start.3 = ((bf16[32,2,28672]{2,1,0:T(2,128)(2,1)}), bf16[32,2,28672]{2,1,0:T(2,128)(2,1)}, u32[]{:S(2)}, u32[]{:S(2)}) async-start(bf16[32,2,28672]{2,1,0:T(2,128)(2,1)} %reshape.179), calls=%async_computation.3 | async-start | bytes 7340032 | tf_op jit(solution)/shard_map/all_to_all | solution.py:37
  269.1 10.9 %copy-start.5 = (s32[32]{0:T(128)S(1)}, s32[32]{0:T(128)}, u32[]{:S(2)}) copy-start(s32[32]{0:T(128)} %param.12) | copy-start | bytes 388
  273.8 73.0 %all-to-all-start.5 = ((bf16[32,2,28672]{2,1,0:T(2,128)(2,1)}), bf16[32,2,28672]{2,1,0:T(2,128)(2,1)}, u32[]{:S(2)}, u32[]{:S(2)}) async-start(bf16[32,2,28672]{2,1,0:T(2,128)(2,1)} %reshape.183), calls=%async_computation.5 | async-start | bytes 7340032 | tf_op jit(solution)/shard_map/all_to_all | solution.py:38
  398.1 53.1 %all-to-all-start.2 = ((bf16[32,112,512]{2,1,0:T(8,128)(2,1)}), bf16[32,112,512]{2,1,0:T(8,128)(2,1)}, u32[]{:S(2)}, u32[]{:S(2)}) async-start(bf16[32,112,512]{2,1,0:T(8,128)(2,1)} %get-tuple-element.6), calls=%async_computation.2 | async-start | bytes 7340032 | tf_op jit(solution)/shard_map/all_to_all | solution.py:46
  451.2 52.4 %all-to-all-start.6 = ((bf16[32,16,3584]{2,1,0:T(8,128)(2,1)}), bf16[32,16,3584]{2,1,0:T(8,128)(2,1)}, u32[]{:S(2)}, u32[]{:S(2)}) async-start(bf16[32,16,3584]{2,1,0:T(8,128)(2,1)} %broadcast_select_fusion.3), calls=%async_computation.6 | async-start | bytes 7340032 | tf_op jit(solution)/shard_map/all_to_all | solution.py:48
  456.7 303.6 %reduce-scatter.2.cloned.1.call-start = ((), (), s32[]{:S(2)}) async-start(), calls=%async_computation.9 | async-start | bytes 27525120 | tf_op jit(solution)/shard_map/reduce_scatter | solution.py:65
  771.7 7.7 copy-start.2
  771.7 7.8 copy-start.4
  771.7 82.8 %all-to-all-start.7 = ((bf16[2,1,32,12,3584]{4,0,3,1,2:T(2,128)(2,1)}), bf16[2,1,32,12,3584]{4,0,3,1,2:T(2,128)(2,1)}, u32[]{:S(2)}, u32[]{:S(2)}) async-start(bf16[2,1,32,12,3584]{4,0,3,1,2:T(2,128)(2,1)} %copy.56), calls=%async_computation.8 | async-start | bytes 11010048 | tf_op jit(solution)/shard_map/all_to_all | solution.py:68
  870.8 15.2 %copy-start.1 = (bf16[64,3584]{1,0:T(8,128)(2,1)S(1)}, bf16[64,3584]{1,0:T(8,128)(2,1)}, u32[]{:S(2)}) copy-start(bf16[64,3584]{1,0:T(8,128)(2,1)} %param.9) | copy-start | bytes 1376260
Sparse Core Ops, SparseCore 0:
  124.6 197.1 all-gather.2
  570.4 189.8 reduce-scatter.1
where the time goes:
time: 904 us; the launch traced here: 893 us
  waiting for transfers between devices  290 us (32%)
  local copies, waits for them, and re-layouts  269 us (30%)
  blocking collectives  123 us (14%)
  other arithmetic  92.7 us (10%)
  matrix products  66.2 us (7%)
  starting transfers between devices  38.6 us (4%)
  between operations  14.1 us (2%)
    reduce_scatter x1, waiting for transfers between devices, per_device(): lax.psum_scatter(partial_terms.astype(jnp.bfloat16), 'dp', scatter_dimens...  190 us
    unnamed x26, local copies, waits for them, and re-layouts  128 us
    unnamed x3, other arithmetic  75.8 us
    all_to_all x1, waiting for transfers between devices, per_device(): lax.all_to_all(summed, 'expert', split_axis=2, concat_axis=2, tiled=True)  75 us
    all_to_all x1, blocking collectives, per_device(): lax.all_to_all(send_rows, 'expert', split_axis=1, concat_axis=1, tiled=True)  71.7 us
    all_to_all x1, blocking collectives, per_device(): lax.all_to_all(selected[1], 'expert', split_axis=0, concat_axis=1, tiled=...  51.3 us
    convert_element_type x2, local copies, waits for them, and re-layouts, per_device(): partial_terms.astype(jnp.bfloat16)  47.7 us
    dot_general x1, matrix products, per_device(): jnp.einsum('krd,kdh->krh', flat_rows, stacked_gate, preferred_element_typ...  22.7 us
  transfers between devices with their start and end apart: 8, of which 6 were waited for; matrix products, arithmetic and copies ran while one was open for 30% of the time, Pallas kernels for 0%

commit v1 on v0

v1 whole, which is shorter than its diff:
```python
import functools

import jax
import jax.numpy as jnp
from jax import lax
from jax.experimental import pallas as pl
from jax.experimental.pallas import tpu as pltpu
from jax.sharding import Mesh
from jax.sharding import PartitionSpec as P

ROUTE_SCALE = 2.5
AXES = ("x", "y", "z", "core")
PAD = 128
CHUNK = 16
GROUP = 2
COLS = 512


def token_gates(scores, route, source, experts):
    gates = ROUTE_SCALE * scores / jnp.sum(scores, axis=1, keepdims=True)
    native = jnp.arange(experts, dtype=jnp.int32)
    copies = jnp.arange(2 * experts, dtype=jnp.int32)
    held = jnp.concatenate((native, source))
    routed = route[:, :, None] == copies
    ids = jnp.sum(jnp.where(routed, held, 0), axis=2)
    return jnp.sum(jnp.where(ids[:, :, None] == native, gates[:, :, None], 0.0), axis=1)


def ffn_kernel(experts, ids, x_ref, ga, gb, ua, ub, da, db, o_ref, gate, up, down, act, sems):
    width, hid = ga.shape
    rows = x_ref.shape[0] * x_ref.shape[1] * x_ref.shape[2]
    copies = (
        pltpu.make_async_copy(ga, gate.at[0], sems.at[0]),
        pltpu.make_async_copy(ua, up.at[0], sems.at[1]),
        pltpu.make_async_copy(gb, gate.at[1], sems.at[2]),
        pltpu.make_async_copy(ub, up.at[1], sems.at[3]),
        pltpu.make_async_copy(da, down.at[pl.ds(0, hid)], sems.at[4]),
        pltpu.make_async_copy(db, down.at[pl.ds(hid, hid)], sems.at[5]),
    )
    first = pl.program_id(0) == 0

    @pl.when(first)
    def _():
        for copy in copies:
            copy.start()

    def ready(number):
        @pl.when(first)
        def _():
            copies[number].wait()

    block = x_ref[...].reshape(rows, width + PAD)
    tokens = block[:, :width]
    shares = block[:, width:].astype(jnp.float32)
    lane = lax.broadcasted_iota(jnp.int32, shares.shape, 1)
    for k in range(2):
        mine = (lane == ids[k]) | (lane == ids[k] + experts)
        share = jnp.sum(jnp.where(mine, shares, 0.0), axis=1, keepdims=True)
        ready(2 * k)
        g = jnp.dot(tokens, gate[k], preferred_element_type=jnp.float32)
        ready(2 * k + 1)
        u = jnp.dot(tokens, up[k], preferred_element_type=jnp.float32)
        act[:, k * hid : (k + 1) * hid] = (g / (1.0 + jnp.exp(-g)) * u * share).astype(act.dtype)
    ready(4)
    ready(5)
    for c in range(0, width, COLS):
        part = jnp.dot(act[...], down[:, c : c + COLS], preferred_element_type=jnp.float32)
        part = part.astype(o_ref.dtype).reshape(x_ref.shape[:3] + (COLS,))
        for j in range(x_ref.shape[0]):
            o_ref[:, j, :, c : c + COLS] = part[j]


def ffn(ids, rows, weights, planes, spots, chunk, experts):
    width, hid = weights[0].shape
    amount = planes * spots * chunk
    group = GROUP
    tile = group * spots * chunk
    return pl.pallas_call(
        functools.partial(ffn_kernel, experts),
        grid_spec=pltpu.PrefetchScalarGridSpec(
            num_scalar_prefetch=1,
            grid=(planes // group,),
            in_specs=[
                pl.BlockSpec((group, spots, chunk, width + PAD), lambda i, s: (i, 0, 0, 0))
            ]
            + [pl.BlockSpec(memory_space=pl.ANY)] * 6,
            out_specs=pl.BlockSpec((spots, group, chunk, width), lambda i, s: (0, i, 0, 0)),
            scratch_shapes=[
                pltpu.VMEM((2, width, hid), jnp.bfloat16),
                pltpu.VMEM((2, width, hid), jnp.bfloat16),
                pltpu.VMEM((2 * hid, width), jnp.bfloat16),
                pltpu.VMEM((tile, 2 * hid), jnp.bfloat16),
                pltpu.SemaphoreType.DMA((6,)),
            ],
        ),
        out_shape=jax.ShapeDtypeStruct((spots, planes, chunk, width), jnp.bfloat16),
        compiler_params=pltpu.CompilerParams(vmem_limit_bytes=56 * 1024 * 1024),
        cost_estimate=pl.CostEstimate(
            flops=amount * width * hid * 12,
            bytes_accessed=amount * width * 4 + 12 * width * hid,
            transcendentals=amount * hid * 2,
        ),
    )(ids, rows.reshape(planes, spots, chunk, width + PAD), *weights)


def per_device(hidden, scores, route, source, gate_proj, up_proj, down_proj):
    planes, spots = lax.axis_size("x"), lax.axis_size("y") * lax.axis_size("z")
    experts = 2 * spots
    tokens, width = hidden.shape
    swap = [(0, 1), (1, 0)]
    dense = token_gates(scores, route, source, experts)
    high = lax.reduce_precision(dense, 8, 7)
    low = dense - high
    filler = jnp.zeros((tokens, PAD - 2 * experts), jnp.bfloat16)
    packed = jnp.concatenate(
        (hidden, high.astype(jnp.bfloat16), low.astype(jnp.bfloat16), filler), axis=1
    )
    weights = []
    for own in (gate_proj[0], up_proj[0], down_proj[0]):
        weights += [own, lax.ppermute(own, "core", swap)]
    core = lax.axis_index("core")
    pair = (lax.axis_index("y") * lax.axis_size("z") + lax.axis_index("z")) * 2
    ids = jnp.stack((pair + core, pair + 1 - core)).astype(jnp.int32)
    results = []
    for start in range(0, tokens, CHUNK):
        rows = lax.all_gather(packed[start : start + CHUNK], ("x", "y", "z"), tiled=True)
        part = ffn(ids, rows, weights, planes, spots, CHUNK, experts)
        part = part.reshape(-1, width)
        part = lax.psum_scatter(part, ("y", "z"), scatter_dimension=0, tiled=True)
        results.append(lax.psum_scatter(part, "x", scatter_dimension=0, tiled=True))
    return jnp.concatenate(results, axis=0)


def solution(mesh):
    planes, experts = mesh.shape["dp"], mesh.shape["expert"]
    side = int(round((experts // 2) ** 0.5))
    grid = Mesh(mesh.devices.reshape(planes, side, side, 2), AXES)
    rows, spread = P(AXES, None), ("y", "z", "core")
    placed = (
        rows,
        rows,
        rows,
        P(),
        P(spread, None, "x"),
        P(spread, None, "x"),
        P(spread, "x", None),
    )
    return jax.shard_map(
        per_device, mesh=grid, in_specs=placed, out_specs=rows, check_vma=False
    )
```

time: 904 us -> 773 us (0.86); the launches traced: 893 us -> 773 us
  waiting for transfers between devices: 290 us -> 619 us
  local copies, waits for them, and re-layouts: 269 us -> 2.93 us
  Pallas kernels: 0 us -> 129 us
  blocking collectives: 123 us -> 0 us
  other arithmetic: 92.7 us -> 5.85 us
  matrix products: 66.2 us -> 0 us
  starting transfers between devices: 38.6 us -> 1.78 us
    reduce_scatter x1 -> x8, waiting for transfers between devices: 190 us -> 404 us  [the longest x4 312 us: per_device(): part = lax.psum_scatter(part, ('y', 'z'), scatter_dimension=0, tiled=True)]
    all_gather x1 -> x4, waiting for transfers between devices: 0.02 us -> 197 us  [per_device(): lax.all_gather(packed[start:start + CHUNK], ('x', 'y', 'z'), tiled=True)]
    pallas_call x0 -> x4, Pallas kernels: none -> 129 us  [ffn(): pl.pallas_call(functools.partial(ffn_kernel, experts), grid_spec=pltpu.Pr...]
    unnamed x26 -> x1, local copies, waits for them, and re-layouts: 128 us -> 0.77 us
    all_to_all x2 -> x0, blocking collectives: 123 us -> none  [the longest x1 71.7 us: per_device(): lax.all_to_all(send_rows, 'expert', split_axis=1, concat_axis=1, tiled=True)]
    all_to_all x6 -> x0, waiting for transfers between devices: 99.8 us -> none  [the longest x1 75 us: per_device(): lax.all_to_all(summed, 'expert', split_axis=2, concat_axis=2, tiled=True)]
    unnamed x3 -> x0, other arithmetic: 75.8 us -> none
    dot_general x4 -> x0, matrix products: 66.2 us -> none  [the longest x1 22.7 us: per_device(): jnp.einsum('krd,kdh->krh', flat_rows, stacked_gate, preferred_element_typ...]
  transfers between devices with their start and end apart: 8 -> 15, of which waited for: 6 -> 15; matrix products, arithmetic and copies ran while one was open for 30% -> 0% of each run, Pallas kernels for 0% -> 17%
where the time goes in v1:
time: 773 us
  waiting for transfers between devices  619 us (80%)
  Pallas kernels  129 us (17%)
  between operations  13.6 us (2%)
    reduce_scatter x4, waiting for transfers between devices, per_device(): part = lax.psum_scatter(part, ('y', 'z'), scatter_dimension=0, tiled=True)  312 us
    all_gather x4, waiting for transfers between devices, per_device(): lax.all_gather(packed[start:start + CHUNK], ('x', 'y', 'z'), tiled=True)  197 us
    pallas_call x4, Pallas kernels, ffn(): pl.pallas_call(functools.partial(ffn_kernel, experts), grid_spec=pltpu.Pr...  129 us
    reduce_scatter x4, waiting for transfers between devices, per_device(): results.append(lax.psum_scatter(part, 'x', scatter_dimension=0, tiled=True))  92.7 us
    ppermute x3, waiting for transfers between devices, per_device(): weights += [own, lax.ppermute(own, 'core', swap)]  16.1 us
  transfers between devices with their start and end apart: 15, of which 15 were waited for; matrix products, arithmetic and copies ran while one was open for 0% of the time, Pallas kernels for 17%

profile of v1, /device:TPU:32, one launch (start us, length us, event | category | flops | bytes accessed | tf_op | source)
XLA Modules:
  0.0 772.6 jit_solution(904821674730970107)
XLA Ops:
  6.5 0.8 copy.10
  7.3 0.7 pad_add_fusion.1
  8.0 1.2 select_reduce_fusion
  9.3 0.1 copy.11
  9.3 0.7 reduce_sum.28
  10.1 0.7 multiply_divide_fusion
  10.8 0.1 copy.12
  10.9 0.1 copy.13
  11.0 1.1 concatenate.10
  12.1 0.8 fusion.1
  12.9 0.0 all-gather.7.cloned.1.call-start
  13.0 0.7 all-gather.7.cloned.1.call-update
  13.7 0.0 all-gather.9.cloned.1.call-start
  13.7 0.7 all-gather.9.cloned.1.call-update
  14.4 0.0 all-gather.11.cloned.1.call-start
  14.5 0.5 all-gather.11.cloned.1.call-update
  15.0 0.0 reduce-scatter.9.cloned.1.call-start
  15.0 0.1 collective-permute-start
  15.1 0.5 collective-permute-start.1
  15.6 0.1 collective-permute-start.2
  15.7 0.6 pad_add_fusion.ids
  16.3 5.6 collective-permute-done.gb
  21.9 5.2 collective-permute-done.1.ub
  27.1 5.2 collective-permute-done.2.db
  32.4 58.7 %all-gather.5.cloned.1.call-done = bf16[1024,3712]{1,0:T(8,128)(2,1)} async-done(((bf16[16,3712]{1,0:T(8,128)(2,1)}), bf16[1024,3712]{1,0:T(8,128)(2,1)}) %all-gather.5.cloned.1.call-update) | async-done | bytes 7602192 | tf_op jit(solution)/shard_map/all_gather | solution.py:126
  91.0 32.3 %shard_map.73 = bf16[16,4,16,3584]{3,2,1,0:T(8,128)(2,1)} custom-call(s32[2]{0:T(128)} %pad_add_fusion.ids, bf16[4,16,16,3712]{3,2,1,0:T(8,128)(2,1)} %bitcast.20, bf16[3584,512]{1,0:T(8,128)(2,1)} %bitcast.22, bf16[3584,512]{1,0:T(8,128)(2,1)} %collective-permute-done.gb, bf16[3584,512]{1,0:T(8,128)(2,1)} %bitcast.27, ...), custom_call_target="tpu_custom_call" | custom-call | flops 22548578304 | bytes 36700160 | tf_op jit(solution)/shard_map/pallas_call | solution.py:78
  123.4 0.2 reduce-scatter.13.cloned.1.call-start
  123.6 46.1 %all-gather.7.cloned.1.call-done = bf16[1024,3712]{1,0:T(8,128)(2,1)} async-done(((bf16[16,3712]{1,0:T(8,128)(2,1)}), bf16[1024,3712]{1,0:T(8,128)(2,1)}) %all-gather.7.cloned.1.call-update) | async-done | bytes 7602192 | tf_op jit(solution)/shard_map/all_gather | solution.py:126
  169.7 32.2 %shard_map.74 = bf16[16,4,16,3584]{3,2,1,0:T(8,128)(2,1)} custom-call(s32[2]{0:T(128)} %pad_add_fusion.ids, bf16[4,16,16,3712]{3,2,1,0:T(8,128)(2,1)} %bitcast.19, bf16[3584,512]{1,0:T(8,128)(2,1)} %bitcast.23, bf16[3584,512]{1,0:T(8,128)(2,1)} %collective-permute-done.gb, bf16[3584,512]{1,0:T(8,128)(2,1)} %bitcast.28, ...), custom_call_target="tpu_custom_call" | custom-call | flops 22548578304 | bytes 36700160 | tf_op jit(solution)/shard_map/pallas_call | solution.py:78
  201.9 0.3 reduce-scatter.17.cloned.1.call-start
  202.2 46.2 %all-gather.9.cloned.1.call-done = bf16[1024,3712]{1,0:T(8,128)(2,1)} async-done(((bf16[16,3712]{1,0:T(8,128)(2,1)}), bf16[1024,3712]{1,0:T(8,128)(2,1)}) %all-gather.9.cloned.1.call-update) | async-done | bytes 7602192 | tf_op jit(solution)/shard_map/all_gather | solution.py:126
  248.4 32.2 %shard_map.75 = bf16[16,4,16,3584]{3,2,1,0:T(8,128)(2,1)} custom-call(s32[2]{0:T(128)} %pad_add_fusion.ids, bf16[4,16,16,3712]{3,2,1,0:T(8,128)(2,1)} %bitcast.18, bf16[3584,512]{1,0:T(8,128)(2,1)} %bitcast.24, bf16[3584,512]{1,0:T(8,128)(2,1)} %collective-permute-done.gb, bf16[3584,512]{1,0:T(8,128)(2,1)} %bitcast.29, ...), custom_call_target="tpu_custom_call" | custom-call | flops 22548578304 | bytes 36700160 | tf_op jit(solution)/shard_map/pallas_call | solution.py:78
  280.7 0.3 reduce-scatter.21.cloned.1.call-start
  281.0 46.0 %all-gather.11.cloned.1.call-done = bf16[1024,3712]{1,0:T(8,128)(2,1)} async-done(((bf16[16,3712]{1,0:T(8,128)(2,1)}), bf16[1024,3712]{1,0:T(8,128)(2,1)}) %all-gather.11.cloned.1.call-update) | async-done | bytes 7602192 | tf_op jit(solution)/shard_map/all_gather | solution.py:126
  327.0 32.2 %shard_map.76 = bf16[16,4,16,3584]{3,2,1,0:T(8,128)(2,1)} custom-call(s32[2]{0:T(128)} %pad_add_fusion.ids, bf16[4,16,16,3712]{3,2,1,0:T(8,128)(2,1)} %bitcast.17, bf16[3584,512]{1,0:T(8,128)(2,1)} %bitcast.25, bf16[3584,512]{1,0:T(8,128)(2,1)} %collective-permute-done.gb, bf16[3584,512]{1,0:T(8,128)(2,1)} %bitcast.30, ...), custom_call_target="tpu_custom_call" | custom-call | flops 22548578304 | bytes 36700160 | tf_op jit(solution)/shard_map/pallas_call | solution.py:78
  359.2 0.0 reduce-scatter.11.cloned.1.call-start
  359.3 53.6 %reduce-scatter.9.cloned.1.call-done = bf16[64,3584]{1,0:T(8,128)(2,1)} async-done(((bf16[1024,3584]{1,0:T(8,128)(2,1)}), bf16[64,3584]{1,0:T(8,128)(2,1)}) %reduce-scatter.9.cloned.1.call-update) | async-done | bytes 458768 | tf_op jit(solution)/shard_map/reduce_scatter | solution.py:129
  413.0 0.0 reduce-scatter.15.cloned.1.call-start
  413.0 86.1 %reduce-scatter.13.cloned.1.call-done = bf16[64,3584]{1,0:T(8,128)(2,1)} async-done(((bf16[1024,3584]{1,0:T(8,128)(2,1)}), bf16[64,3584]{1,0:T(8,128)(2,1)}) %reduce-scatter.13.cloned.1.call-update) | async-done | bytes 458768 | tf_op jit(solution)/shard_map/reduce_scatter | solution.py:129
  499.1 0.0 reduce-scatter.19.cloned.1.call-start
  499.2 85.7 %reduce-scatter.17.cloned.1.call-done = bf16[64,3584]{1,0:T(8,128)(2,1)} async-done(((bf16[1024,3584]{1,0:T(8,128)(2,1)}), bf16[64,3584]{1,0:T(8,128)(2,1)}) %reduce-scatter.17.cloned.1.call-update) | async-done | bytes 458768 | tf_op jit(solution)/shard_map/reduce_scatter | solution.py:129
  584.9 0.0 reduce-scatter.23.cloned.1.call-start
  585.0 86.2 %reduce-scatter.21.cloned.1.call-done = bf16[64,3584]{1,0:T(8,128)(2,1)} async-done(((bf16[1024,3584]{1,0:T(8,128)(2,1)}), bf16[64,3584]{1,0:T(8,128)(2,1)}) %reduce-scatter.21.cloned.1.call-update) | async-done | bytes 458768 | tf_op jit(solution)/shard_map/reduce_scatter | solution.py:129
  671.2 22.9 %reduce-scatter.11.cloned.1.call-done = bf16[16,3584]{1,0:T(8,128)(2,1)} async-done(((bf16[64,3584]{1,0:T(8,128)(2,1)}), bf16[16,3584]{1,0:T(8,128)(2,1)}) %reduce-scatter.11.cloned.1.call-update) | async-done | bytes 114704 | tf_op jit(solution)/shard_map/reduce_scatter | solution.py:130
  694.1 23.3 %reduce-scatter.15.cloned.1.call-done = bf16[16,3584]{1,0:T(8,128)(2,1)} async-done(((bf16[64,3584]{1,0:T(8,128)(2,1)}), bf16[16,3584]{1,0:T(8,128)(2,1)}) %reduce-scatter.15.cloned.1.call-update) | async-done | bytes 114704 | tf_op jit(solution)/shard_map/reduce_scatter | solution.py:130
  717.4 23.2 %reduce-scatter.19.cloned.1.call-done = bf16[16,3584]{1,0:T(8,128)(2,1)} async-done(((bf16[64,3584]{1,0:T(8,128)(2,1)}), bf16[16,3584]{1,0:T(8,128)(2,1)}) %reduce-scatter.19.cloned.1.call-update) | async-done | bytes 114704 | tf_op jit(solution)/shard_map/reduce_scatter | solution.py:130
  740.6 23.3 %reduce-scatter.23.cloned.1.call-done = bf16[16,3584]{1,0:T(8,128)(2,1)} async-done(((bf16[64,3584]{1,0:T(8,128)(2,1)}), bf16[16,3584]{1,0:T(8,128)(2,1)}) %reduce-scatter.23.cloned.1.call-update) | async-done | bytes 114704 | tf_op jit(solution)/shard_map/reduce_scatter | solution.py:130
  763.9 1.9 pad_maximum_fusion
  (14 shorter events, 0.2 us)
Async XLA Ops:
  6.5 84.5 %all-gather.5.cloned.1.call-start = ((), (), s32[]{:S(2)}) async-start(), calls=%async_computation.8 | async-start | bytes 7720960 | tf_op jit(solution)/shard_map/all_gather | solution.py:126
  12.9 156.8 %all-gather.7.cloned.1.call-start = ((), (), s32[]{:S(2)}) async-start(), calls=%async_computation.11 | async-start | bytes 7720960 | tf_op jit(solution)/shard_map/all_gather | solution.py:126
  13.7 234.7 %all-gather.9.cloned.1.call-start = ((), (), s32[]{:S(2)}) async-start(), calls=%async_computation.14 | async-start | bytes 7720960 | tf_op jit(solution)/shard_map/all_gather | solution.py:126
  14.4 312.5 %all-gather.11.cloned.1.call-start = ((), (), s32[]{:S(2)}) async-start(), calls=%async_computation.17 | async-start | bytes 7720960 | tf_op jit(solution)/shard_map/all_gather | solution.py:126
  15.0 397.9 %reduce-scatter.9.cloned.1.call-start = ((), (), s32[]{:S(2)}) async-start(), calls=%async_computation.9 | async-start | bytes 7798784 | tf_op jit(solution)/shard_map/reduce_scatter | solution.py:129
  15.0 6.8 collective-permute-start
  15.1 12.0 %collective-permute-start.1 = (bf16[3584,512]{1,0:T(8,128)(2,1)}, bf16[3584,512]{1,0:T(8,128)(2,1)}, u32[]{:S(2)}, u32[]{:S(2)}) collective-permute-start(bf16[3584,512]{1,0:T(8,128)(2,1)} %bitcast.26), channel_id=1, source_target_pairs={{0,1},{1,0},{2,3},{3,2},{4,5},{5,4},{6,7},{7,6},{8,9},{9,8},{10,11... | collective-permute-start | bytes 11010056 | tf_op jit(solution)/shard_map/ppermute | solution.py:120
  15.6 16.7 %collective-permute-start.2 = (bf16[512,3584]{1,0:T(8,128)(2,1)}, bf16[512,3584]{1,0:T(8,128)(2,1)}, u32[]{:S(2)}, u32[]{:S(2)}) collective-permute-start(bf16[512,3584]{1,0:T(8,128)(2,1)} %bitcast.31), channel_id=1, source_target_pairs={{0,1},{1,0},{2,3},{3,2},{4,5},{5,4},{6,7},{7,6},{8,9},{9,8},{10,11... | collective-permute-start | bytes 11010056 | tf_op jit(solution)/shard_map/ppermute | solution.py:120
  123.4 375.8 %reduce-scatter.13.cloned.1.call-start = ((), (), s32[]{:S(2)}) async-start(), calls=%async_computation.12 | async-start | bytes 7798784 | tf_op jit(solution)/shard_map/reduce_scatter | solution.py:129
  201.9 383.0 %reduce-scatter.17.cloned.1.call-start = ((), (), s32[]{:S(2)}) async-start(), calls=%async_computation.15 | async-start | bytes 7798784 | tf_op jit(solution)/shard_map/reduce_scatter | solution.py:129
  280.7 390.5 %reduce-scatter.21.cloned.1.call-start = ((), (), s32[]{:S(2)}) async-start(), calls=%async_computation.18 | async-start | bytes 7798784 | tf_op jit(solution)/shard_map/reduce_scatter | solution.py:129
  359.2 334.9 %reduce-scatter.11.cloned.1.call-start = ((), (), s32[]{:S(2)}) async-start(), calls=%async_computation.10 | async-start | bytes 573440 | tf_op jit(solution)/shard_map/reduce_scatter | solution.py:130
  413.0 304.4 %reduce-scatter.15.cloned.1.call-start = ((), (), s32[]{:S(2)}) async-start(), calls=%async_computation.13 | async-start | bytes 573440 | tf_op jit(solution)/shard_map/reduce_scatter | solution.py:130
  499.1 241.4 %reduce-scatter.19.cloned.1.call-start = ((), (), s32[]{:S(2)}) async-start(), calls=%async_computation.16 | async-start | bytes 573440 | tf_op jit(solution)/shard_map/reduce_scatter | solution.py:130
  584.9 178.9 %reduce-scatter.23.cloned.1.call-start = ((), (), s32[]{:S(2)}) async-start(), calls=%async_computation.19 | async-start | bytes 573440 | tf_op jit(solution)/shard_map/reduce_scatter | solution.py:130
Sparse Core Ops, SparseCore 0:
  13.1 77.9 all-gather.4
  93.9 75.7 all-gather.6
  172.6 75.7 all-gather.8
  251.1 75.7 all-gather.10
  330.3 82.5 reduce-scatter.8
  416.7 82.3 reduce-scatter.12
  502.6 82.2 reduce-scatter.16
  588.8 82.3 reduce-scatter.20
  673.6 20.4 reduce-scatter.10
  696.5 20.8 reduce-scatter.14
  719.8 20.7 reduce-scatter.18
  743.0 20.8 reduce-scatter.22

commit v2 on v1

v2 whole, which is shorter than its diff:
```python
import functools

import jax
import jax.numpy as jnp
from jax import lax
from jax.experimental import pallas as pl
from jax.experimental.pallas import tpu as pltpu
from jax.sharding import Mesh
from jax.sharding import PartitionSpec as P

ROUTE_SCALE = 2.5
AXES = ("x", "y", "z", "core")
ORDERS = (("x", "y", "z"), ("y", "z", "x"), ("z", "x", "y"))
PAD = 128
COUNTS = (24, 24, 16)
COLS = 512


def token_gates(scores, route, source, experts):
    gates = ROUTE_SCALE * scores / jnp.sum(scores, axis=1, keepdims=True)
    native = jnp.arange(experts, dtype=jnp.int32)
    copies = jnp.arange(2 * experts, dtype=jnp.int32)
    held = jnp.concatenate((native, source))
    routed = route[:, :, None] == copies
    ids = jnp.sum(jnp.where(routed, held, 0), axis=2)
    return jnp.sum(jnp.where(ids[:, :, None] == native, gates[:, :, None], 0.0), axis=1)


def ffn_kernel(experts, counts, ids, *refs):
    n = len(counts)
    pieces, weights, outs = refs[:n], refs[n : n + 6], refs[n + 6 : 2 * n + 6]
    x, gate, up, down, act, o, x_sems, w_sems, o_sems = refs[2 * n + 6 :]
    ga, gb, ua, ub, da, db = weights
    width, hid = ga.shape
    starts = [sum(counts[:j]) for j in range(n)]
    arrive = [
        pltpu.make_async_copy(pieces[j], x.at[pl.ds(starts[j], counts[j])], x_sems.at[j])
        for j in range(n)
    ]
    load = [
        pltpu.make_async_copy(ga, gate.at[0], w_sems.at[0]),
        pltpu.make_async_copy(ua, up.at[0], w_sems.at[1]),
        pltpu.make_async_copy(gb, gate.at[1], w_sems.at[2]),
        pltpu.make_async_copy(ub, up.at[1], w_sems.at[3]),
        pltpu.make_async_copy(da, down.at[pl.ds(0, hid)], w_sems.at[4]),
        pltpu.make_async_copy(db, down.at[pl.ds(hid, hid)], w_sems.at[5]),
    ]
    load[0].start()
    for copy in arrive[:2]:
        copy.start()
    load[0].wait()
    gates = []
    for j in range(n):
        arrive[j].wait()
        if j == 0:
            for copy in arrive[2:]:
                copy.start()
            load[1].start()
        rows = x[starts[j] : starts[j] + counts[j], :width]
        gates.append(jnp.dot(rows, gate[0], preferred_element_type=jnp.float32))
    for k in range(2):
        if k == 0:
            g = jnp.concatenate(gates)
        else:
            load[2].wait()
            load[4].start()
            load[5].start()
            g = jnp.dot(x[:, :width], gate[k], preferred_element_type=jnp.float32)
        load[2 * k + 1].wait()
        if k == 0:
            load[2].start()
            load[3].start()
        u = jnp.dot(x[:, :width], up[k], preferred_element_type=jnp.float32)
        shares = x[:, width:].astype(jnp.float32)
        lane = lax.broadcasted_iota(jnp.int32, shares.shape, 1)
        mine = (lane == ids[k]) | (lane == ids[k] + experts)
        share = jnp.sum(jnp.where(mine, shares, 0.0), axis=1, keepdims=True)
        act[:, k * hid : (k + 1) * hid] = (g / (1.0 + jnp.exp(-g)) * u * share).astype(act.dtype)
    load[4].wait()
    load[5].wait()
    leave = []
    for i, c in enumerate(range(0, width, COLS)):
        part = jnp.dot(act[...], down[:, c : c + COLS], preferred_element_type=jnp.float32)
        o[:, c : c + COLS] = part.astype(o.dtype)
        for j in range(n):
            copy = pltpu.make_async_copy(
                o.at[pl.ds(starts[j], counts[j]), pl.ds(c, COLS)],
                outs[j].at[:, pl.ds(c, COLS)],
                o_sems.at[i, j],
            )
            copy.start()
            leave.append(copy)
    for copy in leave:
        copy.wait()


def ffn(ids, pieces, weights, experts):
    width, hid = weights[0].shape
    counts = tuple(piece.shape[0] for piece in pieces)
    amount, n = sum(counts), len(counts)
    anywhere = pl.BlockSpec(memory_space=pl.ANY)
    return pl.pallas_call(
        functools.partial(ffn_kernel, experts, counts),
        in_specs=[pl.BlockSpec(memory_space=pltpu.SMEM)] + [anywhere] * (n + 6),
        out_specs=[anywhere] * n,
        scratch_shapes=[
            pltpu.VMEM((amount, width + PAD), jnp.bfloat16),
            pltpu.VMEM((2, width, hid), jnp.bfloat16),
            pltpu.VMEM((2, width, hid), jnp.bfloat16),
            pltpu.VMEM((2 * hid, width), jnp.bfloat16),
            pltpu.VMEM((amount, 2 * hid), jnp.bfloat16),
            pltpu.VMEM((amount, width), jnp.bfloat16),
            pltpu.SemaphoreType.DMA((n,)),
            pltpu.SemaphoreType.DMA((6,)),
            pltpu.SemaphoreType.DMA((width // COLS, n)),
        ],
        out_shape=[jax.ShapeDtypeStruct((count, width), jnp.bfloat16) for count in counts],
        compiler_params=pltpu.CompilerParams(vmem_limit_bytes=50 * 1024 * 1024),
        cost_estimate=pl.CostEstimate(
            flops=amount * width * hid * 12,
            bytes_accessed=amount * width * 4 + 12 * width * hid,
            transcendentals=amount * hid * 2,
        ),
    )(ids, *pieces, *weights)


def ring(axis, size, way):
    pairs = []
    for i in range(size):
        pairs += [(2 * i, (i + way) % size * 2), (2 * i + 1, (i - way) % size * 2 + 1)]
    return lambda block: lax.ppermute(block, (axis, "core"), pairs)


def meet(axis, size, first):
    pairs = []
    for i in range(size):
        for core in range(2):
            j = i ^ 1 if (core == 0) == first else size - 1 - i
            pairs.append((2 * i + core, 2 * j + core))
    return lambda block: lax.ppermute(block, (axis, "core"), pairs)


def double(block, axis):
    for first in (True, False):
        block = jnp.concatenate((block, meet(axis, lax.axis_size(axis), first)(block)), axis=0)
    return block


def add(one, other):
    return (one.astype(jnp.float32) + other.astype(jnp.float32)).astype(one.dtype)


def halve(totals, axes):
    for first in (False, True):
        halves = [jnp.split(total, 2) for total in totals]
        arrived = lax.optimization_barrier(
            [meet(a, lax.axis_size(a), first)(sent) for a, (_, sent) in zip(axes, halves)]
        )
        totals = [add(kept, other) for (kept, _), other in zip(halves, arrived)]
    return totals


def per_device(hidden, scores, route, source, gate_proj, up_proj, down_proj):
    spots = lax.axis_size("y") * lax.axis_size("z")
    experts = 2 * spots
    tokens, width = hidden.shape
    swap = [(0, 1), (1, 0)]
    dense = token_gates(scores, route, source, experts)
    high = lax.reduce_precision(dense, 8, 7)
    low = dense - high
    filler = jnp.zeros((tokens, PAD - 2 * experts), jnp.bfloat16)
    packed = jnp.concatenate(
        (hidden, high.astype(jnp.bfloat16), low.astype(jnp.bfloat16), filler), axis=1
    )
    weights = []
    for own in (gate_proj[0], up_proj[0], down_proj[0]):
        weights += [own, lax.ppermute(own, "core", swap)]
    core = lax.axis_index("core")
    pair = (lax.axis_index("y") * lax.axis_size("z") + lax.axis_index("z")) * 2
    ids = jnp.stack((pair + core, pair + 1 - core)).astype(jnp.int32)

    blocks, start = [], 0
    for count in COUNTS:
        blocks.append(packed[start : start + count])
        start += count
    for phase in range(2):
        blocks = [double(block, order[phase]) for block, order in zip(blocks, ORDERS)]
        if phase == 0:
            blocks = lax.optimization_barrier(blocks)
        else:
            blocks, weights = lax.optimization_barrier((blocks, weights))
    sends = [ring(order[2], lax.axis_size(order[2]), 1) for order in ORDERS]
    steps, done = [blocks], []
    for step in range(lax.axis_size("x") - 1):
        arriving = [send(block) for send, block in zip(sends, steps[-1])]
        done.append(ffn(ids, steps[-1], weights, experts))
        arriving, done[-1] = lax.optimization_barrier((arriving, done[-1]))
        steps.append(arriving)
    done.append(ffn(ids, steps[-1], weights, experts))
    totals = list(done[-1])
    backs = [ring(order[2], lax.axis_size(order[2]), -1) for order in ORDERS]
    for pieces in done[-2::-1]:
        arrived = lax.optimization_barrier([back(t) for back, t in zip(backs, totals)])
        totals = [add(*pair) for pair in zip(arrived, pieces)]
    for phase in (1, 0):
        totals = halve(totals, [order[phase] for order in ORDERS])
    return jnp.concatenate(totals, axis=0)


def solution(mesh):
    planes, experts = mesh.shape["dp"], mesh.shape["expert"]
    side = int(round((experts // 2) ** 0.5))
    grid = Mesh(mesh.devices.reshape(planes, side, side, 2), AXES)
    rows, held = P(AXES, None), ("y", "z", "core")
    placed = (
        rows,
        rows,
        rows,
        P(),
        P(held, None, "x"),
        P(held, None, "x"),
        P(held, "x", None),
    )
    return jax.shard_map(
        per_device, mesh=grid, in_specs=placed, out_specs=rows, check_vma=False
    )
```

time: 773 us -> 406 us (0.53)
  waiting for transfers between devices: 619 us -> 202 us
  starting transfers between devices: 1.78 us -> 48.9 us
  between operations: 13.6 us -> 0.69 us
  other arithmetic: 5.85 us -> 15.8 us
    reduce_scatter x8 -> x0, waiting for transfers between devices: 404 us -> none  [the longest x4 312 us: per_device(): part = lax.psum_scatter(part, ('y', 'z'), scatter_dimension=0, tiled=True)]
    ppermute x0 -> x42, waiting for transfers between devices: none -> 202 us  [the longest x18 114 us: ring(): return lambda block: lax.ppermute(block, (axis, 'core'), pairs)]
    all_gather x4 -> x0, waiting for transfers between devices: 197 us -> none  [per_device(): lax.all_gather(packed[start:start + CHUNK], ('x', 'y', 'z'), tiled=True)]
    ppermute x0 -> x42, starting transfers between devices: none -> 48.4 us  [the longest x24 30.5 us: meet(): return lambda block: lax.ppermute(block, (axis, 'core'), pairs)]
    ppermute x3, waiting for transfers between devices: 16.1 us -> 0.01 us  [per_device(): weights += [own, lax.ppermute(own, 'core', swap)]]
  transfers between devices with their start and end apart: 15 -> 45, of which waited for: 15 -> 34; matrix products, arithmetic and copies ran while one was open for 0% -> 2% of each run, Pallas kernels for 17% -> 23%
where the time goes in v2:
time: 406 us; the launch traced here: 400 us
  waiting for transfers between devices  202 us (50%)
  Pallas kernels  123 us (30%)
  starting transfers between devices  48.9 us (12%)
  other arithmetic  15.8 us (4%)
  local copies, waits for them, and re-layouts  9.35 us (2%)
    pallas_call x4, Pallas kernels, ffn(): pl.pallas_call(functools.partial(ffn_kernel, experts, counts), in_specs=[...  123 us
    ppermute x18, waiting for transfers between devices, ring(): return lambda block: lax.ppermute(block, (axis, 'core'), pairs)  114 us
    ppermute x24, waiting for transfers between devices, meet(): return lambda block: lax.ppermute(block, (axis, 'core'), pairs)  88.4 us
    ppermute x24, starting transfers between devices, meet(): return lambda block: lax.ppermute(block, (axis, 'core'), pairs)  30.5 us
    ppermute x18, starting transfers between devices, ring(): return lambda block: lax.ppermute(block, (axis, 'core'), pairs)  17.9 us
  transfers between devices with their start and end apart: 45, of which 34 were waited for; matrix products, arithmetic and copies ran while one was open for 2% of the time, Pallas kernels for 23%

profile of v2, /device:TPU:32, one launch (start us, length us, event | category | flops | bytes accessed | tf_op | source)
XLA Modules:
  0.0 399.6 jit_solution(9084647975039334520)
XLA Ops:
  10.5 2.0 collective-permute-start.5
  12.6 3.1 collective-permute-start.3
  15.7 2.8 collective-permute-start.1
  18.6 2.7 collective-permute-done.3
  21.3 3.1 collective-permute-done.1
  24.8 2.2 collective-permute-start.8
  27.5 5.6 %collective-permute-done.10 = bf16[64,3712]{1,0:T(8,128)(2,1)S(1)} collective-permute-done((bf16[64,3712]{1,0:T(8,128)(2,1)S(1)}, bf16[64,3712]{1,0:T(8,128)(2,1)S(1)}, u32[]{:S(2)}, u32[]{:S(2)}) %collective-permute-start.10) | collective-permute-done | bytes 475168 | tf_op jit(solution)/shard_map/ppermute | solution.py:140
  33.4 2.8 collective-permute-done.8
  36.2 2.6 collective-permute-start.11
  38.9 5.5 %collective-permute-done.6 = bf16[96,3712]{1,0:T(8,128)(2,1)S(1)} collective-permute-done((bf16[96,3712]{1,0:T(8,128)(2,1)S(1)}, bf16[96,3712]{1,0:T(8,128)(2,1)S(1)}, u32[]{:S(2)}, u32[]{:S(2)}) %collective-permute-start.6) | collective-permute-done | bytes 712736 | tf_op jit(solution)/shard_map/ppermute | solution.py:140
  44.4 2.4 collective-permute-start.9
  46.9 4.3 %collective-permute-done.11 = bf16[128,3712]{1,0:T(8,128)(2,1)S(1)} collective-permute-done((bf16[128,3712]{1,0:T(8,128)(2,1)S(1)}, bf16[128,3712]{1,0:T(8,128)(2,1)S(1)}, u32[]{:S(2)}, u32[]{:S(2)}) %collective-permute-start.11) | collective-permute-done | bytes 950304 | tf_op jit(solution)/shard_map/ppermute | solution.py:140
  52.4 11.1 %collective-permute-done.9 = bf16[192,3712]{1,0:T(8,128)(2,1)S(1)} collective-permute-done((bf16[192,3712]{1,0:T(8,128)(2,1)S(1)}, bf16[192,3712]{1,0:T(8,128)(2,1)S(1)}, u32[]{:S(2)}, u32[]{:S(2)}) %collective-permute-start.9) | collective-permute-done | bytes 1425440 | tf_op jit(solution)/shard_map/ppermute | solution.py:140
  63.6 1.8 pad_maximum_fusion.1.refs_1_
  65.4 5.8 %collective-permute-done.7 = bf16[192,3712]{1,0:T(8,128)(2,1)S(1)} collective-permute-done((bf16[192,3712]{1,0:T(8,128)(2,1)S(1)}, bf16[192,3712]{1,0:T(8,128)(2,1)S(1)}, u32[]{:S(2)}, u32[]{:S(2)}) %collective-permute-start.7) | collective-permute-done | bytes 1425440 | tf_op jit(solution)/shard_map/ppermute | solution.py:140
  71.2 1.8 pad_maximum_fusion.refs_0_
  73.0 1.8 copy-done.7
  74.8 1.8 copy-done.8
  76.6 1.9 copy-done.9
  78.5 2.9 collective-permute-start.15
  81.6 30.7 %shard_map.73 = (bf16[384,3584]{1,0:T(8,128)(2,1)}, bf16[384,3584]{1,0:T(8,128)(2,1)}, bf16[256,3584]{1,0:T(8,128)(2,1)S(1)}) custom-call(s32[2]{0:T(128)S(1)} %pad_add_fusion.ids, bf16[384,3712]{1,0:T(8,128)(2,1)} %pad_maximum_fusion.refs_0_, bf16[384,3712]{1,0:T(8,128)(2,1)} %pad_maximum_fusion.1.refs_1_, bf16[256,3712]{1,0:T(8,128)(2,1)S(1)} %pad_maximum_fusion.2.refs_2_, ...), custom_call_target="tpu_custom_call" | custom-call | flops 22548578304 | bytes 36700160 | tf_op jit(solution)/shard_map/pallas_call | solution.py:102
  113.3 3.7 collective-permute-done.16.refs_1_
  117.0 30.5 %shard_map.74 = (bf16[384,3584]{1,0:T(8,128)(2,1)}, bf16[384,3584]{1,0:T(8,128)(2,1)}, bf16[256,3584]{1,0:T(8,128)(2,1)S(1)}) custom-call(s32[2]{0:T(128)S(1)} %pad_add_fusion.ids, bf16[384,3712]{1,0:T(8,128)(2,1)} %collective-permute-done.15.refs_0_, bf16[384,3712]{1,0:T(8,128)(2,1)} %collective-permute-done.16.refs_1_, ...), custom_call_target="tpu_custom_call" | custom-call | flops 22548578304 | bytes 36700160 | tf_op jit(solution)/shard_map/pallas_call | solution.py:102
  147.5 3.8 collective-permute-done.18.refs_0_
  152.6 1.8 collective-permute-start.21
  154.4 30.8 %shard_map.75 = (bf16[384,3584]{1,0:T(8,128)(2,1)}, bf16[384,3584]{1,0:T(8,128)(2,1)}, bf16[256,3584]{1,0:T(8,128)(2,1)S(1)}) custom-call(s32[2]{0:T(128)S(1)} %pad_add_fusion.ids, bf16[384,3712]{1,0:T(8,128)(2,1)} %copy-done.10, bf16[384,3712]{1,0:T(8,128)(2,1)} %collective-permute-done.19.refs_1_, bf16[256,3712]{1,0:T(8,128)(2,1)S(1)} %collective-permute-done.20.refs_2_, ...), custom_call_target="tpu_custom_call" | custom-call | flops 22548578304 | bytes 36700160 | tf_op jit(solution)/shard_map/pallas_call | solution.py:102
  186.8 3.2 collective-permute-done.22.refs_1_
  190.0 30.8 %shard_map.76 = (bf16[384,3584]{1,0:T(8,128)(2,1)}, bf16[384,3584]{1,0:T(8,128)(2,1)}, bf16[256,3584]{1,0:T(8,128)(2,1)S(1)}) custom-call(s32[2]{0:T(128)S(1)} %pad_add_fusion.ids, bf16[384,3712]{1,0:T(8,128)(2,1)} %collective-permute-done.21.refs_0_, bf16[384,3712]{1,0:T(8,128)(2,1)} %collective-permute-done.22.refs_1_, ...), custom_call_target="tpu_custom_call" | custom-call | flops 22548578304 | bytes 36700160 | tf_op jit(solution)/shard_map/pallas_call | solution.py:102
  222.8 21.6 %collective-permute-done.26 = bf16[256,3584]{1,0:T(8,128)(2,1)S(1)} collective-permute-done((bf16[256,3584]{1,0:T(8,128)(2,1)S(1)}, bf16[256,3584]{1,0:T(8,128)(2,1)S(1)}, u32[]{:S(2)}, u32[]{:S(2)}) %collective-permute-start.26) | collective-permute-done | bytes 1835040 | tf_op jit(solution)/shard_map/ppermute | solution.py:131
  244.3 9.8 %collective-permute-done.24 = bf16[384,3584]{1,0:T(8,128)(2,1)S(1)} collective-permute-done((bf16[384,3584]{1,0:T(8,128)(2,1)}, bf16[384,3584]{1,0:T(8,128)(2,1)S(1)}, u32[]{:S(2)}, u32[]{:S(2)}) %collective-permute-start.24) | collective-permute-done | bytes 2752544 | tf_op jit(solution)/shard_map/ppermute | solution.py:131
  257.1 3.3 collective-permute-start.27
  262.6 21.6 %collective-permute-done.29 = bf16[256,3584]{1,0:T(8,128)(2,1)S(1)} collective-permute-done((bf16[256,3584]{1,0:T(8,128)(2,1)S(1)}, bf16[256,3584]{1,0:T(8,128)(2,1)S(1)}, u32[]{:S(2)}, u32[]{:S(2)}) %collective-permute-start.29) | collective-permute-done | bytes 1835040 | tf_op jit(solution)/shard_map/ppermute | solution.py:131
  284.2 4.0 %collective-permute-done.28 = bf16[384,3584]{1,0:T(8,128)(2,1)S(1)} collective-permute-done((bf16[384,3584]{1,0:T(8,128)(2,1)S(1)}, bf16[384,3584]{1,0:T(8,128)(2,1)S(1)}, u32[]{:S(2)}, u32[]{:S(2)}) %collective-permute-start.28) | collective-permute-done | bytes 2752544 | tf_op jit(solution)/shard_map/ppermute | solution.py:131
  288.2 2.7 collective-permute-done.27
  292.4 3.0 collective-permute-start.30
  297.6 22.5 %collective-permute-done.32 = bf16[256,3584]{1,0:T(8,128)(2,1)S(1)} collective-permute-done((bf16[256,3584]{1,0:T(8,128)(2,1)S(1)}, bf16[256,3584]{1,0:T(8,128)(2,1)S(1)}, u32[]{:S(2)}, u32[]{:S(2)}) %collective-permute-start.32) | collective-permute-done | bytes 1835040 | tf_op jit(solution)/shard_map/ppermute | solution.py:131
  320.1 9.7 %collective-permute-done.31 = bf16[384,3584]{1,0:T(8,128)(2,1)S(1)} collective-permute-done((bf16[384,3584]{1,0:T(8,128)(2,1)S(1)}, bf16[384,3584]{1,0:T(8,128)(2,1)S(1)}, u32[]{:S(2)}, u32[]{:S(2)}) %collective-permute-start.31) | collective-permute-done | bytes 2752544 | tf_op jit(solution)/shard_map/ppermute | solution.py:131
  329.8 7.0 %collective-permute-done.30 = bf16[384,3584]{1,0:T(8,128)(2,1)S(1)} collective-permute-done((bf16[384,3584]{1,0:T(8,128)(2,1)S(1)}, bf16[384,3584]{1,0:T(8,128)(2,1)S(1)}, u32[]{:S(2)}, u32[]{:S(2)}) %collective-permute-start.30) | collective-permute-done | bytes 2752544 | tf_op jit(solution)/shard_map/ppermute | solution.py:131
  340.0 2.4 collective-permute-start.33
  343.0 19.5 %collective-permute-done.35 = bf16[128,3584]{1,0:T(8,128)(2,1)S(1)} collective-permute-done((bf16[128,3584]{1,0:T(8,128)(2,1)S(1)}, bf16[128,3584]{1,0:T(8,128)(2,1)S(1)}, u32[]{:S(2)}, u32[]{:S(2)}) %collective-permute-start.35) | collective-permute-done | bytes 917536 | tf_op jit(solution)/shard_map/ppermute | solution.py:140
  363.6 3.4 collective-permute-done.33
  367.4 2.6 collective-permute-start.37
  371.5 7.8 %collective-permute-done.38 = bf16[64,3584]{1,0:T(8,128)(2,1)S(1)} collective-permute-done((bf16[64,3584]{1,0:T(8,128)(2,1)S(1)}, bf16[64,3584]{1,0:T(8,128)(2,1)S(1)}, u32[]{:S(2)}, u32[]{:S(2)}) %collective-permute-start.38) | collective-permute-done | bytes 458784 | tf_op jit(solution)/shard_map/ppermute | solution.py:140
  379.4 2.1 collective-permute-done.36
  381.7 2.2 collective-permute-start.40
  385.8 4.6 %collective-permute-done.41 = bf16[32,3584]{1,0:T(8,128)(2,1)S(1)} collective-permute-done((bf16[32,3584]{1,0:T(8,128)(2,1)S(1)}, bf16[32,3584]{1,0:T(8,128)(2,1)S(1)}, u32[]{:S(2)}, u32[]{:S(2)}) %collective-permute-start.41) | collective-permute-done | bytes 229408 | tf_op jit(solution)/shard_map/ppermute | solution.py:140
  390.4 2.2 collective-permute-done.39
  393.2 4.8 %collective-permute-done.44 = bf16[16,3584]{1,0:T(8,128)(2,1)S(1)} collective-permute-done((bf16[16,3584]{1,0:T(8,128)(2,1)S(1)}, bf16[16,3584]{1,0:T(8,128)(2,1)S(1)}, u32[]{:S(2)}, u32[]{:S(2)}) %collective-permute-start.44) | collective-permute-done | bytes 114720 | tf_op jit(solution)/shard_map/ppermute | solution.py:140
  (130 shorter events, 38.8 us)
Async XLA Ops:
  5.6 4.9 %collective-permute-start.4 = (bf16[16,3712]{1,0:T(8,128)(2,1)S(1)}, bf16[16,3712]{1,0:T(8,128)(2,1)S(1)}, u32[]{:S(2)}, u32[]{:S(2)}) collective-permute-start(bf16[16,3712]{1,0:T(8,128)(2,1)S(1)} %slice.14), channel_id=1, source_target_pairs={{0,2},{1,7},{2,0},{3,5},{4,6},{5,3},{6,4},{7,1},{8,10},{9,15},{10,... | collective-permute-start | bytes 356360 | tf_op jit(solution)/shard_map/ppermute | solution.py:140
  5.7 6.8 %collective-permute-start.2 = (bf16[24,3712]{1,0:T(8,128)(2,1)S(1)}, bf16[24,3712]{1,0:T(8,128)(2,1)S(1)}, u32[]{:S(2)}, u32[]{:S(2)}) collective-permute-start(bf16[24,3712]{1,0:T(8,128)(2,1)S(1)} %get-tuple-element.131), channel_id=1, source_target_pairs={{0,8},{1,25},{8,0},{9,17},{16,24},{17,9},{24,16},{25,1},{2,10},{3,... | collective-permute-start | bytes 534536 | tf_op jit(solution)/shard_map/ppermute | solution.py:140
  7.5 8.2 %collective-permute-start = (bf16[24,3712]{1,0:T(8,128)(2,1)S(1)}, bf16[24,3712]{1,0:T(8,128)(2,1)S(1)}, u32[]{:S(2)}, u32[]{:S(2)}) collective-permute-start(bf16[24,3712]{1,0:T(8,128)(2,1)S(1)} %get-tuple-element.132), channel_id=1, source_target_pairs={{0,32},{1,97},{32,0},{33,65},{64,96},{65,33},{96,64},{97,1},{2,34}... | collective-permute-start | bytes 534536 | tf_op jit(solution)/shard_map/ppermute | solution.py:140
  10.5 8.0 %collective-permute-start.5 = (bf16[32,3712]{1,0:T(8,128)(2,1)S(1)}, bf16[32,3712]{1,0:T(8,128)(2,1)S(1)}, u32[]{:S(2)}, u32[]{:S(2)}) collective-permute-start(bf16[32,3712]{1,0:T(8,128)(2,1)S(1)} %pad_maximum_fusion.12), channel_id=1, source_target_pairs={{0,6},{1,3},{2,4},{3,1},{4,2},{5,7},{6,0},{7,5},{8,14},{9,11},{10,... | collective-permute-start | bytes 712712 | tf_op jit(solution)/shard_map/ppermute | solution.py:140
  12.6 8.7 %collective-permute-start.3 = (bf16[48,3712]{1,0:T(8,128)(2,1)S(1)}, bf16[48,3712]{1,0:T(8,128)(2,1)S(1)}, u32[]{:S(2)}, u32[]{:S(2)}) collective-permute-start(bf16[48,3712]{1,0:T(8,128)(2,1)S(1)} %pad_maximum_fusion.11), channel_id=1, source_target_pairs={{0,24},{1,9},{8,16},{9,1},{16,8},{17,25},{24,0},{25,17},{2,26},{3,... | collective-permute-start | bytes 1069064 | tf_op jit(solution)/shard_map/ppermute | solution.py:140
  15.7 8.7 %collective-permute-start.1 = (bf16[48,3712]{1,0:T(8,128)(2,1)S(1)}, bf16[48,3712]{1,0:T(8,128)(2,1)S(1)}, u32[]{:S(2)}, u32[]{:S(2)}) collective-permute-start(bf16[48,3712]{1,0:T(8,128)(2,1)S(1)} %pad_maximum_fusion.10), channel_id=1, source_target_pairs={{0,96},{1,33},{32,64},{33,1},{64,32},{65,97},{96,0},{97,65},{2,98}... | collective-permute-start | bytes 1069064 | tf_op jit(solution)/shard_map/ppermute | solution.py:140
  24.4 8.7 %collective-permute-start.10 = (bf16[64,3712]{1,0:T(8,128)(2,1)S(1)}, bf16[64,3712]{1,0:T(8,128)(2,1)S(1)}, u32[]{:S(2)}, u32[]{:S(2)}) collective-permute-start(bf16[64,3712]{1,0:T(8,128)(2,1)S(1)} %pad_maximum_fusion.8), channel_id=1, source_target_pairs={{0,32},{1,97},{32,0},{33,65},{64,96},{65,33},{96,64},{97,1},{2,34}... | collective-permute-start | bytes 1425416 | tf_op jit(solution)/shard_map/ppermute | solution.py:140
  24.8 11.4 %collective-permute-start.8 = (bf16[96,3712]{1,0:T(8,128)(2,1)S(1)}, bf16[96,3712]{1,0:T(8,128)(2,1)S(1)}, u32[]{:S(2)}, u32[]{:S(2)}) collective-permute-start(bf16[96,3712]{1,0:T(8,128)(2,1)S(1)} %pad_maximum_fusion.7), channel_id=1, source_target_pairs={{0,2},{1,7},{2,0},{3,5},{4,6},{5,3},{6,4},{7,1},{8,10},{9,15},{10,... | collective-permute-start | bytes 2138120 | tf_op jit(solution)/shard_map/ppermute | solution.py:140
  27.0 45.9 %collective-permute-start.12 = (bf16[3584,512]{1,0:T(8,128)(2,1)S(1)}, bf16[3584,512]{1,0:T(8,128)(2,1)S(1)}, u32[]{:S(2)}, u32[]{:S(2)}) collective-permute-start(bf16[3584,512]{1,0:T(8,128)(2,1)S(1)} %bitcast.9), channel_id=1, source_target_pairs={{0,1},{1,0},{2,3},{3,2},{4,5},{5,4},{6,7},{7,6},{8,9},{9,8},{10,11... | collective-permute-start | bytes 11010056 | tf_op jit(solution)/shard_map/ppermute | solution.py:177
  27.0 47.7 %collective-permute-start.13 = (bf16[3584,512]{1,0:T(8,128)(2,1)}, bf16[3584,512]{1,0:T(8,128)(2,1)S(1)}, u32[]{:S(2)}, u32[]{:S(2)}) collective-permute-start(bf16[3584,512]{1,0:T(8,128)(2,1)} %bitcast.10), channel_id=1, source_target_pairs={{0,1},{1,0},{2,3},{3,2},{4,5},{5,4},{6,7},{7,6},{8,9},{9,8},{10,11... | collective-permute-start | bytes 11010056 | tf_op jit(solution)/shard_map/ppermute | solution.py:177
  27.5 49.0 %collective-permute-start.14 = (bf16[512,3584]{1,0:T(8,128)(2,1)}, bf16[512,3584]{1,0:T(8,128)(2,1)S(1)}, u32[]{:S(2)}, u32[]{:S(2)}) collective-permute-start(bf16[512,3584]{1,0:T(8,128)(2,1)} %bitcast.15), channel_id=1, source_target_pairs={{0,1},{1,0},{2,3},{3,2},{4,5},{5,4},{6,7},{7,6},{8,9},{9,8},{10,11... | collective-permute-start | bytes 11010056 | tf_op jit(solution)/shard_map/ppermute | solution.py:177
  33.2 11.2 %collective-permute-start.6 = (bf16[96,3712]{1,0:T(8,128)(2,1)S(1)}, bf16[96,3712]{1,0:T(8,128)(2,1)S(1)}, u32[]{:S(2)}, u32[]{:S(2)}) collective-permute-start(bf16[96,3712]{1,0:T(8,128)(2,1)S(1)} %pad_maximum_fusion.6), channel_id=1, source_target_pairs={{0,8},{1,25},{8,0},{9,17},{16,24},{17,9},{24,16},{25,1},{2,10},{3,... | collective-permute-start | bytes 2138120 | tf_op jit(solution)/shard_map/ppermute | solution.py:140
  36.2 15.0 %collective-permute-start.11 = (bf16[128,3712]{1,0:T(8,128)(2,1)S(1)}, bf16[128,3712]{1,0:T(8,128)(2,1)S(1)}, u32[]{:S(2)}, u32[]{:S(2)}) collective-permute-start(bf16[128,3712]{1,0:T(8,128)(2,1)S(1)} %pad_maximum_fusion.5), channel_id=1, source_target_pairs={{0,96},{1,33},{32,64},{33,1},{64,32},{65,97},{96,0},{97,65},{2,98}... | collective-permute-start | bytes 2850824 | tf_op jit(solution)/shard_map/ppermute | solution.py:140
  44.4 19.2 %collective-permute-start.9 = (bf16[192,3712]{1,0:T(8,128)(2,1)S(1)}, bf16[192,3712]{1,0:T(8,128)(2,1)S(1)}, u32[]{:S(2)}, u32[]{:S(2)}) collective-permute-start(bf16[192,3712]{1,0:T(8,128)(2,1)S(1)} %pad_maximum_fusion.4), channel_id=1, source_target_pairs={{0,6},{1,3},{2,4},{3,1},{4,2},{5,7},{6,0},{7,5},{8,14},{9,11},{10,... | collective-permute-start | bytes 4276232 | tf_op jit(solution)/shard_map/ppermute | solution.py:140
  51.2 20.0 %collective-permute-start.7 = (bf16[192,3712]{1,0:T(8,128)(2,1)S(1)}, bf16[192,3712]{1,0:T(8,128)(2,1)S(1)}, u32[]{:S(2)}, u32[]{:S(2)}) collective-permute-start(bf16[192,3712]{1,0:T(8,128)(2,1)S(1)} %pad_maximum_fusion.3), channel_id=1, source_target_pairs={{0,24},{1,9},{8,16},{9,1},{16,8},{17,25},{24,0},{25,17},{2,26},{3,... | collective-permute-start | bytes 4276232 | tf_op jit(solution)/shard_map/ppermute | solution.py:140
  78.5 34.8 %collective-permute-start.15 = (bf16[384,3712]{1,0:T(8,128)(2,1)}, bf16[384,3712]{1,0:T(8,128)(2,1)}, u32[]{:S(2)}, u32[]{:S(2)}) collective-permute-start(bf16[384,3712]{1,0:T(8,128)(2,1)} %pad_maximum_fusion.refs_0_), channel_id=1, source_target_pairs={{0,2},{1,7},{2,4},{3,1},{4,6},{5,3},{6,0},{7,5},{8,10},{9,15},{10,... | collective-permute-start | bytes 8552456 | tf_op jit(solution)/shard_map/ppermute | solution.py:131
  81.3 35.6 %collective-permute-start.16 = (bf16[384,3712]{1,0:T(8,128)(2,1)}, bf16[384,3712]{1,0:T(8,128)(2,1)}, u32[]{:S(2)}, u32[]{:S(2)}) collective-permute-start(bf16[384,3712]{1,0:T(8,128)(2,1)} %pad_maximum_fusion.1.refs_1_), channel_id=1, source_target_pairs={{0,32},{1,97},{32,64},{33,1},{64,96},{65,33},{96,0},{97,65},{2,34}... | collective-permute-start | bytes 8552456 | tf_op jit(solution)/shard_map/ppermute | solution.py:131
  81.4 30.9 %collective-permute-start.17 = (bf16[256,3712]{1,0:T(8,128)(2,1)S(1)}, bf16[256,3712]{1,0:T(8,128)(2,1)S(1)}, u32[]{:S(2)}, u32[]{:S(2)}) collective-permute-start(bf16[256,3712]{1,0:T(8,128)(2,1)S(1)} %pad_maximum_fusion.2.refs_2_), channel_id=1, source_target_pairs={{0,8},{1,25},{8,16},{9,1},{16,24},{17,9},{24,0},{25,17},{2,10},{3,... | collective-permute-start | bytes 5701640 | tf_op jit(solution)/shard_map/ppermute | solution.py:131
  116.9 34.3 %collective-permute-start.18 = (bf16[384,3712]{1,0:T(8,128)(2,1)}, bf16[384,3712]{1,0:T(8,128)(2,1)S(1)}, u32[]{:S(2)}, u32[]{:S(2)}) collective-permute-start(bf16[384,3712]{1,0:T(8,128)(2,1)} %collective-permute-done.15.refs_0_), channel_id=1, source_target_pairs={{0,2},{1,7},{2,4},{3,1},{4,6},{5,3},{6,0},{7,5},{8,10},{9,15},{10,... | collective-permute-start | bytes 8552456 | tf_op jit(solution)/shard_map/ppermute | solution.py:131
  117.0 35.6 %collective-permute-start.19 = (bf16[384,3712]{1,0:T(8,128)(2,1)}, bf16[384,3712]{1,0:T(8,128)(2,1)}, u32[]{:S(2)}, u32[]{:S(2)}) collective-permute-start(bf16[384,3712]{1,0:T(8,128)(2,1)} %collective-permute-done.16.refs_1_), channel_id=1, source_target_pairs={{0,32},{1,97},{32,64},{33,1},{64,96},{65,33},{96,0},{97,65},{2,34}... | collective-permute-start | bytes 8552456 | tf_op jit(solution)/shard_map/ppermute | solution.py:131
  117.0 30.5 %collective-permute-start.20 = (bf16[256,3712]{1,0:T(8,128)(2,1)S(1)}, bf16[256,3712]{1,0:T(8,128)(2,1)S(1)}, u32[]{:S(2)}, u32[]{:S(2)}) collective-permute-start(bf16[256,3712]{1,0:T(8,128)(2,1)S(1)} %collective-permute-done.17.refs_2_), channel_id=1, source_target_pairs={{0,8},{1,25},{8,16},{9,1},{16,24},{17,9},{24,0},{25,17},{2,10},{3,... | collective-permute-start | bytes 5701640 | tf_op jit(solution)/shard_map/ppermute | solution.py:131
  152.6 34.2 %collective-permute-start.21 = (bf16[384,3712]{1,0:T(8,128)(2,1)S(1)}, bf16[384,3712]{1,0:T(8,128)(2,1)}, u32[]{:S(2)}, u32[]{:S(2)}) collective-permute-start(bf16[384,3712]{1,0:T(8,128)(2,1)S(1)} %collective-permute-done.18.refs_0_), channel_id=1, source_target_pairs={{0,2},{1,7},{2,4},{3,1},{4,6},{5,3},{6,0},{7,5},{8,10},{9,15},{10,... | collective-permute-start | bytes 8552456 | tf_op jit(solution)/shard_map/ppermute | solution.py:131
  154.4 35.6 %collective-permute-start.22 = (bf16[384,3712]{1,0:T(8,128)(2,1)}, bf16[384,3712]{1,0:T(8,128)(2,1)}, u32[]{:S(2)}, u32[]{:S(2)}) collective-permute-start(bf16[384,3712]{1,0:T(8,128)(2,1)} %collective-permute-done.19.refs_1_), channel_id=1, source_target_pairs={{0,32},{1,97},{32,64},{33,1},{64,96},{65,33},{96,0},{97,65},{2,34}... | collective-permute-start | bytes 8552456 | tf_op jit(solution)/shard_map/ppermute | solution.py:131
  154.4 30.8 %collective-permute-start.23 = (bf16[256,3712]{1,0:T(8,128)(2,1)S(1)}, bf16[256,3712]{1,0:T(8,128)(2,1)S(1)}, u32[]{:S(2)}, u32[]{:S(2)}) collective-permute-start(bf16[256,3712]{1,0:T(8,128)(2,1)S(1)} %collective-permute-done.20.refs_2_), channel_id=1, source_target_pairs={{0,8},{1,25},{8,16},{9,1},{16,24},{17,9},{24,0},{25,17},{2,10},{3,... | collective-permute-start | bytes 5701640 | tf_op jit(solution)/shard_map/ppermute | solution.py:131
  190.0 64.4 %copy-start.5 = (bf16[384,3584]{1,0:T(8,128)(2,1)S(1)}, bf16[384,3584]{1,0:T(8,128)(2,1)}, u32[]{:S(2)}) copy-start(bf16[384,3584]{1,0:T(8,128)(2,1)} %get-tuple-element.104) | copy-start | bytes 8257540
  220.8 33.3 %collective-permute-start.24 = (bf16[384,3584]{1,0:T(8,128)(2,1)}, bf16[384,3584]{1,0:T(8,128)(2,1)S(1)}, u32[]{:S(2)}, u32[]{:S(2)}) collective-permute-start(bf16[384,3584]{1,0:T(8,128)(2,1)} %get-tuple-element.98), channel_id=1, source_target_pairs={{0,6},{1,3},{2,0},{3,5},{4,2},{5,7},{6,4},{7,1},{8,14},{9,11},{10,... | collective-permute-start | bytes 8257544 | tf_op jit(solution)/shard_map/ppermute | solution.py:131
  221.1 33.3 %collective-permute-start.25 = (bf16[384,3584]{1,0:T(8,128)(2,1)}, bf16[384,3584]{1,0:T(8,128)(2,1)S(1)}, u32[]{:S(2)}, u32[]{:S(2)}) collective-permute-start(bf16[384,3584]{1,0:T(8,128)(2,1)} %get-tuple-element.99), channel_id=1, source_target_pairs={{0,96},{1,33},{32,0},{33,65},{64,32},{65,97},{96,64},{97,1},{2,98}... | collective-permute-start | bytes 8257544 | tf_op jit(solution)/shard_map/ppermute | solution.py:131
  221.1 35.3 %copy-start.4 = (bf16[384,3584]{1,0:T(8,128)(2,1)S(1)}, bf16[384,3584]{1,0:T(8,128)(2,1)}, u32[]{:S(2)}) copy-start(bf16[384,3584]{1,0:T(8,128)(2,1)} %get-tuple-element.102) | copy-start | bytes 8257540
  221.1 23.2 %collective-permute-start.26 = (bf16[256,3584]{1,0:T(8,128)(2,1)S(1)}, bf16[256,3584]{1,0:T(8,128)(2,1)S(1)}, u32[]{:S(2)}, u32[]{:S(2)}) collective-permute-start(bf16[256,3584]{1,0:T(8,128)(2,1)S(1)} %get-tuple-element.100), channel_id=1, source_target_pairs={{0,24},{1,9},{8,0},{9,17},{16,8},{17,25},{24,16},{25,1},{2,26},{3,... | collective-permute-start | bytes 5505032 | tf_op jit(solution)/shard_map/ppermute | solution.py:131
  255.1 33.1 %collective-permute-start.28 = (bf16[384,3584]{1,0:T(8,128)(2,1)S(1)}, bf16[384,3584]{1,0:T(8,128)(2,1)S(1)}, u32[]{:S(2)}, u32[]{:S(2)}) collective-permute-start(bf16[384,3584]{1,0:T(8,128)(2,1)S(1)} %add_convert_fusion.4), channel_id=1, source_target_pairs={{0,96},{1,33},{32,0},{33,65},{64,32},{65,97},{96,64},{97,1},{2,98}... | collective-permute-start | bytes 8257544 | tf_op jit(solution)/shard_map/ppermute | solution.py:131
  257.1 33.9 %collective-permute-start.27 = (bf16[384,3584]{1,0:T(8,128)(2,1)S(1)}, bf16[384,3584]{1,0:T(8,128)(2,1)S(1)}, u32[]{:S(2)}, u32[]{:S(2)}) collective-permute-start(bf16[384,3584]{1,0:T(8,128)(2,1)S(1)} %add_convert_fusion.5), channel_id=1, source_target_pairs={{0,6},{1,3},{2,0},{3,5},{4,2},{5,7},{6,4},{7,1},{8,14},{9,11},{10,... | collective-permute-start | bytes 8257544 | tf_op jit(solution)/shard_map/ppermute | solution.py:131
  260.9 23.3 %collective-permute-start.29 = (bf16[256,3584]{1,0:T(8,128)(2,1)S(1)}, bf16[256,3584]{1,0:T(8,128)(2,1)S(1)}, u32[]{:S(2)}, u32[]{:S(2)}) collective-permute-start(bf16[256,3584]{1,0:T(8,128)(2,1)S(1)} %add_convert_fusion.8), channel_id=1, source_target_pairs={{0,24},{1,9},{8,0},{9,17},{16,8},{17,25},{24,16},{25,1},{2,26},{3,... | collective-permute-start | bytes 5505032 | tf_op jit(solution)/shard_map/ppermute | solution.py:131
  291.6 38.2 %collective-permute-start.31 = (bf16[384,3584]{1,0:T(8,128)(2,1)S(1)}, bf16[384,3584]{1,0:T(8,128)(2,1)S(1)}, u32[]{:S(2)}, u32[]{:S(2)}) collective-permute-start(bf16[384,3584]{1,0:T(8,128)(2,1)S(1)} %add_convert_fusion.2), channel_id=1, source_target_pairs={{0,96},{1,33},{32,0},{33,65},{64,32},{65,97},{96,64},{97,1},{2,98}... | collective-permute-start | bytes 8257544 | tf_op jit(solution)/shard_map/ppermute | solution.py:131
  292.4 44.4 %copy-start.1 = (bf16[384,3584]{1,0:T(8,128)(2,1)S(1)}, bf16[384,3584]{1,0:T(8,128)(2,1)}, u32[]{:S(2)}) copy-start(bf16[384,3584]{1,0:T(8,128)(2,1)} %get-tuple-element.116) | copy-start | bytes 8257540
  292.4 44.4 %collective-permute-start.30 = (bf16[384,3584]{1,0:T(8,128)(2,1)S(1)}, bf16[384,3584]{1,0:T(8,128)(2,1)S(1)}, u32[]{:S(2)}, u32[]{:S(2)}) collective-permute-start(bf16[384,3584]{1,0:T(8,128)(2,1)S(1)} %add_convert_fusion.3), channel_id=1, source_target_pairs={{0,6},{1,3},{2,0},{3,5},{4,2},{5,7},{6,4},{7,1},{8,14},{9,11},{10,... | collective-permute-start | bytes 8257544 | tf_op jit(solution)/shard_map/ppermute | solution.py:131
  295.8 24.3 %collective-permute-start.32 = (bf16[256,3584]{1,0:T(8,128)(2,1)S(1)}, bf16[256,3584]{1,0:T(8,128)(2,1)S(1)}, u32[]{:S(2)}, u32[]{:S(2)}) collective-permute-start(bf16[256,3584]{1,0:T(8,128)(2,1)S(1)} %add_convert_fusion.7), channel_id=1, source_target_pairs={{0,24},{1,9},{8,0},{9,17},{16,8},{17,25},{24,16},{25,1},{2,26},{3,... | collective-permute-start | bytes 5505032 | tf_op jit(solution)/shard_map/ppermute | solution.py:131
  337.6 26.0 %collective-permute-start.34 = (bf16[192,3584]{1,0:T(8,128)(2,1)S(1)}, bf16[192,3584]{1,0:T(8,128)(2,1)S(1)}, u32[]{:S(2)}, u32[]{:S(2)}) collective-permute-start(bf16[192,3584]{1,0:T(8,128)(2,1)S(1)} %split.98), channel_id=1, source_target_pairs={{0,6},{1,3},{2,4},{3,1},{4,2},{5,7},{6,0},{7,5},{8,14},{9,11},{10,... | collective-permute-start | bytes 4128776 | tf_op jit(solution)/shard_map/ppermute | solution.py:140
  340.0 27.0 %collective-permute-start.33 = (bf16[192,3584]{1,0:T(8,128)(2,1)S(1)}, bf16[192,3584]{1,0:T(8,128)(2,1)S(1)}, u32[]{:S(2)}, u32[]{:S(2)}) collective-permute-start(bf16[192,3584]{1,0:T(8,128)(2,1)S(1)} %split.97), channel_id=1, source_target_pairs={{0,24},{1,9},{8,16},{9,1},{16,8},{17,25},{24,0},{25,17},{2,26},{3,... | collective-permute-start | bytes 4128776 | tf_op jit(solution)/shard_map/ppermute | solution.py:140
  342.9 19.6 %collective-permute-start.35 = (bf16[128,3584]{1,0:T(8,128)(2,1)S(1)}, bf16[128,3584]{1,0:T(8,128)(2,1)S(1)}, u32[]{:S(2)}, u32[]{:S(2)}) collective-permute-start(bf16[128,3584]{1,0:T(8,128)(2,1)S(1)} %split.99), channel_id=1, source_target_pairs={{0,96},{1,33},{32,64},{33,1},{64,32},{65,97},{96,0},{97,65},{2,98}... | collective-permute-start | bytes 2752520 | tf_op jit(solution)/shard_map/ppermute | solution.py:140
  367.4 12.0 %collective-permute-start.37 = (bf16[96,3584]{1,0:T(8,128)(2,1)S(1)}, bf16[96,3584]{1,0:T(8,128)(2,1)S(1)}, u32[]{:S(2)}, u32[]{:S(2)}) collective-permute-start(bf16[96,3584]{1,0:T(8,128)(2,1)S(1)} %split.103), channel_id=1, source_target_pairs={{0,2},{1,7},{2,0},{3,5},{4,6},{5,3},{6,4},{7,1},{8,10},{9,15},{10,... | collective-permute-start | bytes 2064392 | tf_op jit(solution)/shard_map/ppermute | solution.py:140
  370.5 11.0 %collective-permute-start.36 = (bf16[96,3584]{1,0:T(8,128)(2,1)S(1)}, bf16[96,3584]{1,0:T(8,128)(2,1)S(1)}, u32[]{:S(2)}, u32[]{:S(2)}) collective-permute-start(bf16[96,3584]{1,0:T(8,128)(2,1)S(1)} %split.101), channel_id=1, source_target_pairs={{0,8},{1,25},{8,0},{9,17},{16,24},{17,9},{24,16},{25,1},{2,10},{3,... | collective-permute-start | bytes 2064392 | tf_op jit(solution)/shard_map/ppermute | solution.py:140
  370.8 8.6 %collective-permute-start.38 = (bf16[64,3584]{1,0:T(8,128)(2,1)S(1)}, bf16[64,3584]{1,0:T(8,128)(2,1)S(1)}, u32[]{:S(2)}, u32[]{:S(2)}) collective-permute-start(bf16[64,3584]{1,0:T(8,128)(2,1)S(1)} %split.105), channel_id=1, source_target_pairs={{0,32},{1,97},{32,0},{33,65},{64,96},{65,33},{96,64},{97,1},{2,34}... | collective-permute-start | bytes 1376264 | tf_op jit(solution)/shard_map/ppermute | solution.py:140
  381.7 8.8 %collective-permute-start.40 = (bf16[48,3584]{1,0:T(8,128)(2,1)S(1)}, bf16[48,3584]{1,0:T(8,128)(2,1)S(1)}, u32[]{:S(2)}, u32[]{:S(2)}) collective-permute-start(bf16[48,3584]{1,0:T(8,128)(2,1)S(1)} %split.109), channel_id=1, source_target_pairs={{0,24},{1,9},{8,16},{9,1},{16,8},{17,25},{24,0},{25,17},{2,26},{3,... | collective-permute-start | bytes 1032200 | tf_op jit(solution)/shard_map/ppermute | solution.py:140
  384.1 8.5 %collective-permute-start.39 = (bf16[48,3584]{1,0:T(8,128)(2,1)S(1)}, bf16[48,3584]{1,0:T(8,128)(2,1)S(1)}, u32[]{:S(2)}, u32[]{:S(2)}) collective-permute-start(bf16[48,3584]{1,0:T(8,128)(2,1)S(1)} %split.107), channel_id=1, source_target_pairs={{0,96},{1,33},{32,64},{33,1},{64,32},{65,97},{96,0},{97,65},{2,98}... | collective-permute-start | bytes 1032200 | tf_op jit(solution)/shard_map/ppermute | solution.py:140
  384.3 6.1 %collective-permute-start.41 = (bf16[32,3584]{1,0:T(8,128)(2,1)S(1)}, bf16[32,3584]{1,0:T(8,128)(2,1)S(1)}, u32[]{:S(2)}, u32[]{:S(2)}) collective-permute-start(bf16[32,3584]{1,0:T(8,128)(2,1)S(1)} %split.111), channel_id=1, source_target_pairs={{0,6},{1,3},{2,4},{3,1},{4,2},{5,7},{6,0},{7,5},{8,14},{9,11},{10,... | collective-permute-start | bytes 688136 | tf_op jit(solution)/shard_map/ppermute | solution.py:140
  392.7 5.5 %collective-permute-start.43 = (bf16[24,3584]{1,0:T(8,128)(2,1)S(1)}, bf16[24,3584]{1,0:T(8,128)(2,1)S(1)}, u32[]{:S(2)}, u32[]{:S(2)}) collective-permute-start(bf16[24,3584]{1,0:T(8,128)(2,1)S(1)} %split.115), channel_id=1, source_target_pairs={{0,8},{1,25},{8,0},{9,17},{16,24},{17,9},{24,16},{25,1},{2,10},{3,... | collective-permute-start | bytes 516104 | tf_op jit(solution)/shard_map/ppermute | solution.py:140
  392.9 5.5 %collective-permute-start.42 = (bf16[24,3584]{1,0:T(8,128)(2,1)S(1)}, bf16[24,3584]{1,0:T(8,128)(2,1)S(1)}, u32[]{:S(2)}, u32[]{:S(2)}) collective-permute-start(bf16[24,3584]{1,0:T(8,128)(2,1)S(1)} %split.113), channel_id=1, source_target_pairs={{0,32},{1,97},{32,0},{33,65},{64,96},{65,33},{96,64},{97,1},{2,34}... | collective-permute-start | bytes 516104 | tf_op jit(solution)/shard_map/ppermute | solution.py:140
  393.1 4.9 %collective-permute-start.44 = (bf16[16,3584]{1,0:T(8,128)(2,1)S(1)}, bf16[16,3584]{1,0:T(8,128)(2,1)S(1)}, u32[]{:S(2)}, u32[]{:S(2)}) collective-permute-start(bf16[16,3584]{1,0:T(8,128)(2,1)S(1)} %split.117), channel_id=1, source_target_pairs={{0,2},{1,7},{2,0},{3,5},{4,6},{5,3},{6,4},{7,1},{8,10},{9,15},{10,... | collective-permute-start | bytes 344072 | tf_op jit(solution)/shard_map/ppermute | solution.py:140
  (8 other events, 94.6 us)

commit v3 on v2

--- a/solution.py
+++ b/solution.py
@@ -12,7 +12,7 @@
 AXES = ("x", "y", "z", "core")
 ORDERS = (("x", "y", "z"), ("y", "z", "x"), ("z", "x", "y"))
 PAD = 128
-COUNTS = (24, 24, 16)
+COUNTS = (22, 21, 21)
 COLS = 512
 
 
@@ -186,9 +186,9 @@
     for phase in range(2):
         blocks = [double(block, order[phase]) for block, order in zip(blocks, ORDERS)]
         if phase == 0:
+            blocks, weights = lax.optimization_barrier((blocks, weights))
+        else:
             blocks = lax.optimization_barrier(blocks)
-        else:
-            blocks, weights = lax.optimization_barrier((blocks, weights))
     sends = [ring(order[2], lax.axis_size(order[2]), 1) for order in ORDERS]
     steps, done = [blocks], []
     for step in range(lax.axis_size("x") - 1):

time: 406 us -> 383 us (0.943)
  waiting for transfers between devices: 202 us -> 168 us
  starting transfers between devices: 48.9 us -> 66.7 us
  local copies, waits for them, and re-layouts: 9.35 us -> 3.21 us
    ppermute x18, waiting for transfers between devices: 114 us -> 93.9 us  [ring(): return lambda block: lax.ppermute(block, (axis, 'core'), pairs)]
    ppermute x24, waiting for transfers between devices: 88.4 us -> 73.9 us  [meet(): return lambda block: lax.ppermute(block, (axis, 'core'), pairs)]
    ppermute x24, starting transfers between devices: 30.5 us -> 40.3 us  [meet(): return lambda block: lax.ppermute(block, (axis, 'core'), pairs)]
    ppermute x18, starting transfers between devices: 17.9 us -> 25.9 us  [ring(): return lambda block: lax.ppermute(block, (axis, 'core'), pairs)]
    unnamed x23 -> x17, local copies, waits for them, and re-layouts: 7.49 us -> 0.8 us
  transfers between devices with their start and end apart: 45 -> 45, of which waited for: 34 -> 25; matrix products, arithmetic and copies ran while one was open for 2% -> 4% of each run, Pallas kernels for 23% -> 24%
where the time goes in v3:
time: 383 us; the launch traced here: 376 us
  waiting for transfers between devices  168 us (44%)
  Pallas kernels  121 us (32%)
  starting transfers between devices  66.7 us (17%)
  other arithmetic  16.3 us (4%)
    pallas_call x4, Pallas kernels, ffn(): pl.pallas_call(functools.partial(ffn_kernel, experts, counts), in_specs=[...  121 us
    ppermute x18, waiting for transfers between devices, ring(): return lambda block: lax.ppermute(block, (axis, 'core'), pairs)  93.9 us
    ppermute x24, waiting for transfers between devices, meet(): return lambda block: lax.ppermute(block, (axis, 'core'), pairs)  73.9 us
    ppermute x24, starting transfers between devices, meet(): return lambda block: lax.ppermute(block, (axis, 'core'), pairs)  40.3 us
    ppermute x18, starting transfers between devices, ring(): return lambda block: lax.ppermute(block, (axis, 'core'), pairs)  25.9 us
  transfers between devices with their start and end apart: 45, of which 25 were waited for; matrix products, arithmetic and copies ran while one was open for 4% of the time, Pallas kernels for 24%

profile of v3, /device:TPU:32, one launch (start us, length us, event | category | flops | bytes accessed | tf_op | source)
XLA Modules:
  0.0 376.2 jit_solution(2821169509496223984)
XLA Ops:
  6.3 1.7 collective-permute-start.2
  8.0 3.8 %collective-permute-done.4 = bf16[21,3712]{1,0:T(8,128)(2,1)S(1)} collective-permute-done((bf16[21,3712]{1,0:T(8,128)(2,1)S(1)}, bf16[21,3712]{1,0:T(8,128)(2,1)S(1)}, u32[]{:S(2)}, u32[]{:S(2)}) %collective-permute-start.4) | collective-permute-done | bytes 155936 | tf_op jit(solution)/shard_map/ppermute | solution.py:140
  13.3 2.0 collective-permute-start.5
  15.4 1.8 collective-permute-done
  17.2 3.0 collective-permute-start.3
  20.8 2.6 collective-permute-start.1
  23.6 2.2 collective-permute-done.3
  26.0 3.4 collective-permute-done.1
  29.8 2.1 collective-permute-start.11
  31.9 1.6 collective-permute-start.9
  33.4 6.8 %collective-permute-done.13 = bf16[84,3712]{1,0:T(8,128)(2,1)S(1)} collective-permute-done((bf16[84,3712]{1,0:T(8,128)(2,1)S(1)}, bf16[84,3712]{1,0:T(8,128)(2,1)S(1)}, u32[]{:S(2)}, u32[]{:S(2)}) %collective-permute-start.13) | collective-permute-done | bytes 623648 | tf_op jit(solution)/shard_map/ppermute | solution.py:140
  40.4 2.7 collective-permute-start.14
  43.3 2.9 collective-permute-start.12
  46.2 3.1 collective-permute-start.10
  49.3 9.3 %collective-permute-done.14 = bf16[168,3712]{1,0:T(8,128)(2,1)S(1)} collective-permute-done((bf16[168,3712]{1,0:T(8,128)(2,1)S(1)}, bf16[168,3712]{1,0:T(8,128)(2,1)S(1)}, u32[]{:S(2)}, u32[]{:S(2)}) %collective-permute-start.14) | collective-permute-done | bytes 1247264 | tf_op jit(solution)/shard_map/ppermute | solution.py:140
  58.6 1.7 pad_maximum_fusion.2.refs_2_
  61.0 1.7 pad_maximum_fusion.1.refs_1_
  62.8 2.3 collective-permute-done.10
  67.1 30.3 %shard_map.73 = (bf16[352,3584]{1,0:T(8,128)(2,1)}, bf16[336,3584]{1,0:T(8,128)(2,1)S(1)}, bf16[336,3584]{1,0:T(8,128)(2,1)}) custom-call(s32[2]{0:T(128)S(1)} %pad_add_fusion.ids, bf16[352,3712]{1,0:T(8,128)(2,1)} %copy-done, bf16[336,3712]{1,0:T(8,128)(2,1)} %pad_maximum_fusion.1.refs_1_, bf16[336,3712]{1,0:T(8,128)(2,1)} %pad_maximum_fusion.2.refs_2_, ...), custom_call_target="tpu_custom_call" | custom-call | flops 22548578304 | bytes 36700160 | tf_op jit(solution)/shard_map/pallas_call | solution.py:102
  98.2 4.3 %collective-permute-start.18 = (bf16[352,3712]{1,0:T(8,128)(2,1)}, bf16[352,3712]{1,0:T(8,128)(2,1)S(1)}, u32[]{:S(2)}, u32[]{:S(2)}) collective-permute-start(bf16[352,3712]{1,0:T(8,128)(2,1)} %collective-permute-done.15.refs_0_), channel_id=1, source_target_pairs={{0,2},{1,7},{2,4},{3,1},{4,6},{5,3},{6,0},{7,5},{8,10},{9,15},{10,... | collective-permute-start | bytes 7839752 | tf_op jit(solution)/shard_map/ppermute | solution.py:131
  103.0 2.0 collective-permute-start.20
  105.1 30.2 %shard_map.74 = (bf16[352,3584]{1,0:T(8,128)(2,1)}, bf16[336,3584]{1,0:T(8,128)(2,1)S(1)}, bf16[336,3584]{1,0:T(8,128)(2,1)}) custom-call(s32[2]{0:T(128)S(1)} %pad_add_fusion.ids, bf16[352,3712]{1,0:T(8,128)(2,1)} %collective-permute-done.15.refs_0_, bf16[336,3712]{1,0:T(8,128)(2,1)} %collective-permute-done.16.refs_1_, ...), custom_call_target="tpu_custom_call" | custom-call | flops 22548578304 | bytes 36700160 | tf_op jit(solution)/shard_map/pallas_call | solution.py:102
  136.9 1.9 collective-permute-start.23
  138.8 30.5 %shard_map.75 = (bf16[352,3584]{1,0:T(8,128)(2,1)}, bf16[336,3584]{1,0:T(8,128)(2,1)S(1)}, bf16[336,3584]{1,0:T(8,128)(2,1)}) custom-call(s32[2]{0:T(128)S(1)} %pad_add_fusion.ids, bf16[352,3712]{1,0:T(8,128)(2,1)} %copy-done.7, bf16[336,3712]{1,0:T(8,128)(2,1)} %collective-permute-done.19.refs_1_, bf16[336,3712]{1,0:T(8,128)(2,1)} %collective-permute-done.20.refs_2_, ...), custom_call_target="tpu_custom_call" | custom-call | flops 22548578304 | bytes 36700160 | tf_op jit(solution)/shard_map/pallas_call | solution.py:102
  169.3 30.4 %shard_map.76 = (bf16[352,3584]{1,0:T(8,128)(2,1)}, bf16[336,3584]{1,0:T(8,128)(2,1)S(1)}, bf16[336,3584]{1,0:T(8,128)(2,1)}) custom-call(s32[2]{0:T(128)S(1)} %pad_add_fusion.ids, bf16[352,3712]{1,0:T(8,128)(2,1)} %collective-permute-done.21.refs_0_, bf16[336,3712]{1,0:T(8,128)(2,1)} %collective-permute-done.22.refs_1_, ...), custom_call_target="tpu_custom_call" | custom-call | flops 22548578304 | bytes 36700160 | tf_op jit(solution)/shard_map/pallas_call | solution.py:102
  201.2 1.9 collective-permute-start.25
  203.2 2.0 collective-permute-start.26
  205.1 26.2 %collective-permute-done.25 = bf16[336,3584]{1,0:T(8,128)(2,1)S(1)} collective-permute-done((bf16[336,3584]{1,0:T(8,128)(2,1)S(1)}, bf16[336,3584]{1,0:T(8,128)(2,1)S(1)}, u32[]{:S(2)}, u32[]{:S(2)}) %collective-permute-start.25) | collective-permute-done | bytes 2408480 | tf_op jit(solution)/shard_map/ppermute | solution.py:131
  233.3 3.2 collective-permute-start.29
  237.2 2.0 collective-permute-start.27
  239.9 23.5 %collective-permute-done.29 = bf16[336,3584]{1,0:T(8,128)(2,1)S(1)} collective-permute-done((bf16[336,3584]{1,0:T(8,128)(2,1)S(1)}, bf16[336,3584]{1,0:T(8,128)(2,1)S(1)}, u32[]{:S(2)}, u32[]{:S(2)}) %collective-permute-start.29) | collective-permute-done | bytes 2408480 | tf_op jit(solution)/shard_map/ppermute | solution.py:131
  263.4 5.8 %collective-permute-done.28 = bf16[336,3584]{1,0:T(8,128)(2,1)S(1)} collective-permute-done((bf16[336,3584]{1,0:T(8,128)(2,1)S(1)}, bf16[336,3584]{1,0:T(8,128)(2,1)S(1)}, u32[]{:S(2)}, u32[]{:S(2)}) %collective-permute-start.28) | collective-permute-done | bytes 2408480 | tf_op jit(solution)/shard_map/ppermute | solution.py:131
  271.8 2.5 collective-permute-start.31
  274.3 30.5 %collective-permute-done.32 = bf16[336,3584]{1,0:T(8,128)(2,1)S(1)} collective-permute-done((bf16[336,3584]{1,0:T(8,128)(2,1)S(1)}, bf16[336,3584]{1,0:T(8,128)(2,1)S(1)}, u32[]{:S(2)}, u32[]{:S(2)}) %collective-permute-start.32) | collective-permute-done | bytes 2408480 | tf_op jit(solution)/shard_map/ppermute | solution.py:131
  304.8 5.6 %collective-permute-done.31 = bf16[336,3584]{1,0:T(8,128)(2,1)S(1)} collective-permute-done((bf16[336,3584]{1,0:T(8,128)(2,1)S(1)}, bf16[336,3584]{1,0:T(8,128)(2,1)S(1)}, u32[]{:S(2)}, u32[]{:S(2)}) %collective-permute-start.31) | collective-permute-done | bytes 2408480 | tf_op jit(solution)/shard_map/ppermute | solution.py:131
  311.1 1.6 collective-permute-start.35
  315.3 20.3 %collective-permute-done.35 = bf16[168,3584]{1,0:T(8,128)(2,1)S(1)} collective-permute-done((bf16[168,3584]{1,0:T(8,128)(2,1)S(1)}, bf16[168,3584]{1,0:T(8,128)(2,1)S(1)}, u32[]{:S(2)}, u32[]{:S(2)}) %collective-permute-start.35) | collective-permute-done | bytes 1204256 | tf_op jit(solution)/shard_map/ppermute | solution.py:140
  335.6 2.2 collective-permute-done.34
  338.9 2.0 collective-permute-start.38
  342.6 3.2 collective-permute-start.37
  345.8 4.3 %collective-permute-done.38 = bf16[84,3584]{1,0:T(8,128)(2,1)S(1)} collective-permute-done((bf16[84,3584]{1,0:T(8,128)(2,1)S(1)}, bf16[84,3584]{1,0:T(8,128)(2,1)S(1)}, u32[]{:S(2)}, u32[]{:S(2)}) %collective-permute-start.38) | collective-permute-done | bytes 602144 | tf_op jit(solution)/shard_map/ppermute | solution.py:140
  350.1 4.0 %collective-permute-done.37 = bf16[84,3584]{1,0:T(8,128)(2,1)S(1)} collective-permute-done((bf16[84,3584]{1,0:T(8,128)(2,1)S(1)}, bf16[84,3584]{1,0:T(8,128)(2,1)S(1)}, u32[]{:S(2)}, u32[]{:S(2)}) %collective-permute-start.37) | collective-permute-done | bytes 602144 | tf_op jit(solution)/shard_map/ppermute | solution.py:140
  357.0 2.4 collective-permute-start.40
  359.4 2.2 collective-permute-done.41
  361.6 3.9 %collective-permute-done.40 = bf16[42,3584]{1,0:T(8,128)(2,1)S(1)} collective-permute-done((bf16[42,3584]{1,0:T(8,128)(2,1)S(1)}, bf16[42,3584]{1,0:T(8,128)(2,1)S(1)}, u32[]{:S(2)}, u32[]{:S(2)}) %collective-permute-start.40) | collective-permute-done | bytes 301088 | tf_op jit(solution)/shard_map/ppermute | solution.py:140
  365.7 2.5 collective-permute-start.44
  369.5 2.0 collective-permute-done.44
  371.6 3.3 collective-permute-done.43
  (124 shorter events, 34.0 us)
Async XLA Ops:
  0.0 29.5 %collective-permute-start.6 = (bf16[3584,512]{1,0:T(8,128)(2,1)}, bf16[3584,512]{1,0:T(8,128)(2,1)}, u32[]{:S(2)}, u32[]{:S(2)}) collective-permute-start(bf16[3584,512]{1,0:T(8,128)(2,1)} %bitcast.5), channel_id=1, source_target_pairs={{0,1},{1,0},{2,3},{3,2},{4,5},{5,4},{6,7},{7,6},{8,9},{9,8},{10,11... | collective-permute-start | bytes 11010056 | tf_op jit(solution)/shard_map/ppermute | solution.py:177
  0.0 29.5 %collective-permute-start.7 = (bf16[3584,512]{1,0:T(8,128)(2,1)}, bf16[3584,512]{1,0:T(8,128)(2,1)}, u32[]{:S(2)}, u32[]{:S(2)}) collective-permute-start(bf16[3584,512]{1,0:T(8,128)(2,1)} %bitcast.10), channel_id=1, source_target_pairs={{0,1},{1,0},{2,3},{3,2},{4,5},{5,4},{6,7},{7,6},{8,9},{9,8},{10,11... | collective-permute-start | bytes 11010056 | tf_op jit(solution)/shard_map/ppermute | solution.py:177
  0.5 29.0 %collective-permute-start.8 = (bf16[512,3584]{1,0:T(8,128)(2,1)}, bf16[512,3584]{1,0:T(8,128)(2,1)}, u32[]{:S(2)}, u32[]{:S(2)}) collective-permute-start(bf16[512,3584]{1,0:T(8,128)(2,1)} %bitcast.15), channel_id=1, source_target_pairs={{0,1},{1,0},{2,3},{3,2},{4,5},{5,4},{6,7},{7,6},{8,9},{9,8},{10,11... | collective-permute-start | bytes 11010056 | tf_op jit(solution)/shard_map/ppermute | solution.py:177
  6.2 5.6 %collective-permute-start.4 = (bf16[21,3712]{1,0:T(8,128)(2,1)S(1)}, bf16[21,3712]{1,0:T(8,128)(2,1)S(1)}, u32[]{:S(2)}, u32[]{:S(2)}) collective-permute-start(bf16[21,3712]{1,0:T(8,128)(2,1)S(1)} %get-tuple-element.131), channel_id=1, source_target_pairs={{0,2},{1,7},{2,0},{3,5},{4,6},{5,3},{6,4},{7,1},{8,10},{9,15},{10,... | collective-permute-start | bytes 467720 | tf_op jit(solution)/shard_map/ppermute | solution.py:140
  6.3 7.0 %collective-permute-start.2 = (bf16[21,3712]{1,0:T(8,128)(2,1)S(1)}, bf16[21,3712]{1,0:T(8,128)(2,1)S(1)}, u32[]{:S(2)}, u32[]{:S(2)}) collective-permute-start(bf16[21,3712]{1,0:T(8,128)(2,1)S(1)} %get-tuple-element.132), channel_id=1, source_target_pairs={{0,8},{1,25},{8,0},{9,17},{16,24},{17,9},{24,16},{25,1},{2,10},{3,... | collective-permute-start | bytes 467720 | tf_op jit(solution)/shard_map/ppermute | solution.py:140
  11.7 5.5 %collective-permute-start = (bf16[22,3712]{1,0:T(8,128)(2,1)S(1)}, bf16[22,3712]{1,0:T(8,128)(2,1)S(1)}, u32[]{:S(2)}, u32[]{:S(2)}) collective-permute-start(bf16[22,3712]{1,0:T(8,128)(2,1)S(1)} %slice.12), channel_id=1, source_target_pairs={{0,32},{1,97},{32,0},{33,65},{64,96},{65,33},{96,64},{97,1},{2,34}... | collective-permute-start | bytes 489992 | tf_op jit(solution)/shard_map/ppermute | solution.py:140
  13.3 7.5 %collective-permute-start.5 = (bf16[42,3712]{1,0:T(8,128)(2,1)S(1)}, bf16[42,3712]{1,0:T(8,128)(2,1)S(1)}, u32[]{:S(2)}, u32[]{:S(2)}) collective-permute-start(bf16[42,3712]{1,0:T(8,128)(2,1)S(1)} %pad_maximum_fusion.12), channel_id=1, source_target_pairs={{0,6},{1,3},{2,4},{3,1},{4,2},{5,7},{6,0},{7,5},{8,14},{9,11},{10,... | collective-permute-start | bytes 935432 | tf_op jit(solution)/shard_map/ppermute | solution.py:140
  17.2 8.6 %collective-permute-start.3 = (bf16[42,3712]{1,0:T(8,128)(2,1)S(1)}, bf16[42,3712]{1,0:T(8,128)(2,1)S(1)}, u32[]{:S(2)}, u32[]{:S(2)}) collective-permute-start(bf16[42,3712]{1,0:T(8,128)(2,1)S(1)} %pad_maximum_fusion.11), channel_id=1, source_target_pairs={{0,24},{1,9},{8,16},{9,1},{16,8},{17,25},{24,0},{25,17},{2,26},{3,... | collective-permute-start | bytes 935432 | tf_op jit(solution)/shard_map/ppermute | solution.py:140
  20.8 8.6 %collective-permute-start.1 = (bf16[44,3712]{1,0:T(8,128)(2,1)S(1)}, bf16[44,3712]{1,0:T(8,128)(2,1)S(1)}, u32[]{:S(2)}, u32[]{:S(2)}) collective-permute-start(bf16[44,3712]{1,0:T(8,128)(2,1)S(1)} %pad_maximum_fusion.10), channel_id=1, source_target_pairs={{0,96},{1,33},{32,64},{33,1},{64,32},{65,97},{96,0},{97,65},{2,98}... | collective-permute-start | bytes 979976 | tf_op jit(solution)/shard_map/ppermute | solution.py:140
  29.6 10.6 %collective-permute-start.13 = (bf16[84,3712]{1,0:T(8,128)(2,1)S(1)}, bf16[84,3712]{1,0:T(8,128)(2,1)S(1)}, u32[]{:S(2)}, u32[]{:S(2)}) collective-permute-start(bf16[84,3712]{1,0:T(8,128)(2,1)S(1)} %pad_maximum_fusion.8), channel_id=1, source_target_pairs={{0,32},{1,97},{32,0},{33,65},{64,96},{65,33},{96,64},{97,1},{2,34}... | collective-permute-start | bytes 1870856 | tf_op jit(solution)/shard_map/ppermute | solution.py:140
  29.8 13.3 %collective-permute-start.11 = (bf16[84,3712]{1,0:T(8,128)(2,1)S(1)}, bf16[84,3712]{1,0:T(8,128)(2,1)S(1)}, u32[]{:S(2)}, u32[]{:S(2)}) collective-permute-start(bf16[84,3712]{1,0:T(8,128)(2,1)S(1)} %pad_maximum_fusion.7), channel_id=1, source_target_pairs={{0,2},{1,7},{2,0},{3,5},{4,6},{5,3},{6,4},{7,1},{8,10},{9,15},{10,... | collective-permute-start | bytes 1870856 | tf_op jit(solution)/shard_map/ppermute | solution.py:140
  31.9 14.3 %collective-permute-start.9 = (bf16[88,3712]{1,0:T(8,128)(2,1)S(1)}, bf16[88,3712]{1,0:T(8,128)(2,1)S(1)}, u32[]{:S(2)}, u32[]{:S(2)}) collective-permute-start(bf16[88,3712]{1,0:T(8,128)(2,1)S(1)} %pad_maximum_fusion.6), channel_id=1, source_target_pairs={{0,8},{1,25},{8,0},{9,17},{16,24},{17,9},{24,16},{25,1},{2,10},{3,... | collective-permute-start | bytes 1959944 | tf_op jit(solution)/shard_map/ppermute | solution.py:140
  40.4 18.2 %collective-permute-start.14 = (bf16[168,3712]{1,0:T(8,128)(2,1)S(1)}, bf16[168,3712]{1,0:T(8,128)(2,1)S(1)}, u32[]{:S(2)}, u32[]{:S(2)}) collective-permute-start(bf16[168,3712]{1,0:T(8,128)(2,1)S(1)} %pad_maximum_fusion.5), channel_id=1, source_target_pairs={{0,96},{1,33},{32,64},{33,1},{64,32},{65,97},{96,0},{97,65},{2,98}... | collective-permute-start | bytes 3741704 | tf_op jit(solution)/shard_map/ppermute | solution.py:140
  43.3 17.8 %collective-permute-start.12 = (bf16[168,3712]{1,0:T(8,128)(2,1)S(1)}, bf16[168,3712]{1,0:T(8,128)(2,1)S(1)}, u32[]{:S(2)}, u32[]{:S(2)}) collective-permute-start(bf16[168,3712]{1,0:T(8,128)(2,1)S(1)} %pad_maximum_fusion.4), channel_id=1, source_target_pairs={{0,6},{1,3},{2,4},{3,1},{4,2},{5,7},{6,0},{7,5},{8,14},{9,11},{10,... | collective-permute-start | bytes 3741704 | tf_op jit(solution)/shard_map/ppermute | solution.py:140
  46.2 18.9 %collective-permute-start.10 = (bf16[176,3712]{1,0:T(8,128)(2,1)S(1)}, bf16[176,3712]{1,0:T(8,128)(2,1)S(1)}, u32[]{:S(2)}, u32[]{:S(2)}) collective-permute-start(bf16[176,3712]{1,0:T(8,128)(2,1)S(1)} %pad_maximum_fusion.3), channel_id=1, source_target_pairs={{0,24},{1,9},{8,16},{9,1},{16,8},{17,25},{24,0},{25,17},{2,26},{3,... | collective-permute-start | bytes 3919880 | tf_op jit(solution)/shard_map/ppermute | solution.py:140
  65.3 32.9 %collective-permute-start.15 = (bf16[352,3712]{1,0:T(8,128)(2,1)S(1)}, bf16[352,3712]{1,0:T(8,128)(2,1)}, u32[]{:S(2)}, u32[]{:S(2)}) collective-permute-start(bf16[352,3712]{1,0:T(8,128)(2,1)S(1)} %pad_maximum_fusion.refs_0_), channel_id=1, source_target_pairs={{0,2},{1,7},{2,4},{3,1},{4,6},{5,3},{6,0},{7,5},{8,10},{9,15},{10,... | collective-permute-start | bytes 7839752 | tf_op jit(solution)/shard_map/ppermute | solution.py:131
  65.4 32.0 %collective-permute-start.16 = (bf16[336,3712]{1,0:T(8,128)(2,1)}, bf16[336,3712]{1,0:T(8,128)(2,1)}, u32[]{:S(2)}, u32[]{:S(2)}) collective-permute-start(bf16[336,3712]{1,0:T(8,128)(2,1)} %pad_maximum_fusion.1.refs_1_), channel_id=1, source_target_pairs={{0,32},{1,97},{32,64},{33,1},{64,96},{65,33},{96,0},{97,65},{2,34}... | collective-permute-start | bytes 7483400 | tf_op jit(solution)/shard_map/ppermute | solution.py:131
  66.2 32.0 %collective-permute-start.17 = (bf16[336,3712]{1,0:T(8,128)(2,1)}, bf16[336,3712]{1,0:T(8,128)(2,1)}, u32[]{:S(2)}, u32[]{:S(2)}) collective-permute-start(bf16[336,3712]{1,0:T(8,128)(2,1)} %pad_maximum_fusion.2.refs_2_), channel_id=1, source_target_pairs={{0,8},{1,25},{8,16},{9,1},{16,24},{17,9},{24,0},{25,17},{2,10},{3,... | collective-permute-start | bytes 7483400 | tf_op jit(solution)/shard_map/ppermute | solution.py:131
  98.2 37.1 %collective-permute-start.18 = (bf16[352,3712]{1,0:T(8,128)(2,1)}, bf16[352,3712]{1,0:T(8,128)(2,1)S(1)}, u32[]{:S(2)}, u32[]{:S(2)}) collective-permute-start(bf16[352,3712]{1,0:T(8,128)(2,1)} %collective-permute-done.15.refs_0_), channel_id=1, source_target_pairs={{0,2},{1,7},{2,4},{3,1},{4,6},{5,3},{6,0},{7,5},{8,10},{9,15},{10,... | collective-permute-start | bytes 7839752 | tf_op jit(solution)/shard_map/ppermute | solution.py:131
  102.5 32.8 %collective-permute-start.19 = (bf16[336,3712]{1,0:T(8,128)(2,1)}, bf16[336,3712]{1,0:T(8,128)(2,1)}, u32[]{:S(2)}, u32[]{:S(2)}) collective-permute-start(bf16[336,3712]{1,0:T(8,128)(2,1)} %collective-permute-done.16.refs_1_), channel_id=1, source_target_pairs={{0,32},{1,97},{32,64},{33,1},{64,96},{65,33},{96,0},{97,65},{2,34}... | collective-permute-start | bytes 7483400 | tf_op jit(solution)/shard_map/ppermute | solution.py:131
  103.0 32.3 %collective-permute-start.20 = (bf16[336,3712]{1,0:T(8,128)(2,1)}, bf16[336,3712]{1,0:T(8,128)(2,1)}, u32[]{:S(2)}, u32[]{:S(2)}) collective-permute-start(bf16[336,3712]{1,0:T(8,128)(2,1)} %collective-permute-done.17.refs_2_), channel_id=1, source_target_pairs={{0,8},{1,25},{8,16},{9,1},{16,24},{17,9},{24,0},{25,17},{2,10},{3,... | collective-permute-start | bytes 7483400 | tf_op jit(solution)/shard_map/ppermute | solution.py:131
  135.3 34.0 %collective-permute-start.21 = (bf16[352,3712]{1,0:T(8,128)(2,1)S(1)}, bf16[352,3712]{1,0:T(8,128)(2,1)}, u32[]{:S(2)}, u32[]{:S(2)}) collective-permute-start(bf16[352,3712]{1,0:T(8,128)(2,1)S(1)} %collective-permute-done.18.refs_0_), channel_id=1, source_target_pairs={{0,2},{1,7},{2,4},{3,1},{4,6},{5,3},{6,0},{7,5},{8,10},{9,15},{10,... | collective-permute-start | bytes 7839752 | tf_op jit(solution)/shard_map/ppermute | solution.py:131
  136.8 32.5 %collective-permute-start.22 = (bf16[336,3712]{1,0:T(8,128)(2,1)}, bf16[336,3712]{1,0:T(8,128)(2,1)}, u32[]{:S(2)}, u32[]{:S(2)}) collective-permute-start(bf16[336,3712]{1,0:T(8,128)(2,1)} %collective-permute-done.19.refs_1_), channel_id=1, source_target_pairs={{0,32},{1,97},{32,64},{33,1},{64,96},{65,33},{96,0},{97,65},{2,34}... | collective-permute-start | bytes 7483400 | tf_op jit(solution)/shard_map/ppermute | solution.py:131
  136.9 32.4 %collective-permute-start.23 = (bf16[336,3712]{1,0:T(8,128)(2,1)}, bf16[336,3712]{1,0:T(8,128)(2,1)}, u32[]{:S(2)}, u32[]{:S(2)}) collective-permute-start(bf16[336,3712]{1,0:T(8,128)(2,1)} %collective-permute-done.20.refs_2_), channel_id=1, source_target_pairs={{0,8},{1,25},{8,16},{9,1},{16,24},{17,9},{24,0},{25,17},{2,10},{3,... | collective-permute-start | bytes 7483400 | tf_op jit(solution)/shard_map/ppermute | solution.py:131
  169.3 63.4 %copy-start.6 = (bf16[336,3584]{1,0:T(8,128)(2,1)S(1)}, bf16[336,3584]{1,0:T(8,128)(2,1)}, u32[]{:S(2)}) copy-start(bf16[336,3584]{1,0:T(8,128)(2,1)} %get-tuple-element.106) | copy-start | bytes 7225348
  199.7 33.0 %collective-permute-start.24 = (bf16[352,3584]{1,0:T(8,128)(2,1)}, bf16[352,3584]{1,0:T(8,128)(2,1)S(1)}, u32[]{:S(2)}, u32[]{:S(2)}) collective-permute-start(bf16[352,3584]{1,0:T(8,128)(2,1)} %get-tuple-element.98), channel_id=1, source_target_pairs={{0,6},{1,3},{2,0},{3,5},{4,2},{5,7},{6,4},{7,1},{8,14},{9,11},{10,... | collective-permute-start | bytes 7569416 | tf_op jit(solution)/shard_map/ppermute | solution.py:131
  201.2 30.1 %collective-permute-start.25 = (bf16[336,3584]{1,0:T(8,128)(2,1)S(1)}, bf16[336,3584]{1,0:T(8,128)(2,1)S(1)}, u32[]{:S(2)}, u32[]{:S(2)}) collective-permute-start(bf16[336,3584]{1,0:T(8,128)(2,1)S(1)} %get-tuple-element.99), channel_id=1, source_target_pairs={{0,96},{1,33},{32,0},{33,65},{64,32},{65,97},{96,64},{97,1},{2,98}... | collective-permute-start | bytes 7225352 | tf_op jit(solution)/shard_map/ppermute | solution.py:131
  203.1 33.4 %copy-start.3 = (bf16[352,3584]{1,0:T(8,128)(2,1)S(1)}, bf16[352,3584]{1,0:T(8,128)(2,1)}, u32[]{:S(2)}) copy-start(bf16[352,3584]{1,0:T(8,128)(2,1)} %get-tuple-element.102) | copy-start | bytes 7569412
  203.2 29.6 %collective-permute-start.26 = (bf16[336,3584]{1,0:T(8,128)(2,1)}, bf16[336,3584]{1,0:T(8,128)(2,1)S(1)}, u32[]{:S(2)}, u32[]{:S(2)}) collective-permute-start(bf16[336,3584]{1,0:T(8,128)(2,1)} %get-tuple-element.100), channel_id=1, source_target_pairs={{0,24},{1,9},{8,0},{9,17},{16,8},{17,25},{24,16},{25,1},{2,26},{3,... | collective-permute-start | bytes 7225352 | tf_op jit(solution)/shard_map/ppermute | solution.py:131
  233.3 30.1 %collective-permute-start.29 = (bf16[336,3584]{1,0:T(8,128)(2,1)S(1)}, bf16[336,3584]{1,0:T(8,128)(2,1)S(1)}, u32[]{:S(2)}, u32[]{:S(2)}) collective-permute-start(bf16[336,3584]{1,0:T(8,128)(2,1)S(1)} %add_convert_fusion.7), channel_id=1, source_target_pairs={{0,24},{1,9},{8,0},{9,17},{16,8},{17,25},{24,16},{25,1},{2,26},{3,... | collective-permute-start | bytes 7225352 | tf_op jit(solution)/shard_map/ppermute | solution.py:131
  237.2 32.1 %collective-permute-start.27 = (bf16[352,3584]{1,0:T(8,128)(2,1)S(1)}, bf16[352,3584]{1,0:T(8,128)(2,1)S(1)}, u32[]{:S(2)}, u32[]{:S(2)}) collective-permute-start(bf16[352,3584]{1,0:T(8,128)(2,1)S(1)} %add_convert_fusion.2), channel_id=1, source_target_pairs={{0,6},{1,3},{2,0},{3,5},{4,2},{5,7},{6,4},{7,1},{8,14},{9,11},{10,... | collective-permute-start | bytes 7569416 | tf_op jit(solution)/shard_map/ppermute | solution.py:131
  239.8 29.4 %collective-permute-start.28 = (bf16[336,3584]{1,0:T(8,128)(2,1)S(1)}, bf16[336,3584]{1,0:T(8,128)(2,1)S(1)}, u32[]{:S(2)}, u32[]{:S(2)}) collective-permute-start(bf16[336,3584]{1,0:T(8,128)(2,1)S(1)} %add_convert_fusion.8), channel_id=1, source_target_pairs={{0,96},{1,33},{32,0},{33,65},{64,32},{65,97},{96,64},{97,1},{2,98}... | collective-permute-start | bytes 7225352 | tf_op jit(solution)/shard_map/ppermute | solution.py:131
  269.8 35.0 %collective-permute-start.32 = (bf16[336,3584]{1,0:T(8,128)(2,1)S(1)}, bf16[336,3584]{1,0:T(8,128)(2,1)S(1)}, u32[]{:S(2)}, u32[]{:S(2)}) collective-permute-start(bf16[336,3584]{1,0:T(8,128)(2,1)S(1)} %add_convert_fusion.5), channel_id=1, source_target_pairs={{0,24},{1,9},{8,0},{9,17},{16,8},{17,25},{24,16},{25,1},{2,26},{3,... | collective-permute-start | bytes 7225352 | tf_op jit(solution)/shard_map/ppermute | solution.py:131
  270.5 39.9 %copy-start.4 = (bf16[336,3584]{1,0:T(8,128)(2,1)S(1)}, bf16[336,3584]{1,0:T(8,128)(2,1)}, u32[]{:S(2)}) copy-start(bf16[336,3584]{1,0:T(8,128)(2,1)} %get-tuple-element.118) | copy-start | bytes 7225348
  270.6 39.8 %collective-permute-start.30 = (bf16[352,3584]{1,0:T(8,128)(2,1)S(1)}, bf16[352,3584]{1,0:T(8,128)(2,1)S(1)}, u32[]{:S(2)}, u32[]{:S(2)}) collective-permute-start(bf16[352,3584]{1,0:T(8,128)(2,1)S(1)} %add_convert_fusion.1), channel_id=1, source_target_pairs={{0,6},{1,3},{2,0},{3,5},{4,2},{5,7},{6,4},{7,1},{8,14},{9,11},{10,... | collective-permute-start | bytes 7569416 | tf_op jit(solution)/shard_map/ppermute | solution.py:131
  271.8 38.6 %collective-permute-start.31 = (bf16[336,3584]{1,0:T(8,128)(2,1)S(1)}, bf16[336,3584]{1,0:T(8,128)(2,1)S(1)}, u32[]{:S(2)}, u32[]{:S(2)}) collective-permute-start(bf16[336,3584]{1,0:T(8,128)(2,1)S(1)} %add_convert_fusion.6), channel_id=1, source_target_pairs={{0,96},{1,33},{32,0},{33,65},{64,32},{65,97},{96,64},{97,1},{2,98}... | collective-permute-start | bytes 7225352 | tf_op jit(solution)/shard_map/ppermute | solution.py:131
  311.1 24.5 %collective-permute-start.35 = (bf16[168,3584]{1,0:T(8,128)(2,1)S(1)}, bf16[168,3584]{1,0:T(8,128)(2,1)S(1)}, u32[]{:S(2)}, u32[]{:S(2)}) collective-permute-start(bf16[168,3584]{1,0:T(8,128)(2,1)S(1)} %split.99), channel_id=1, source_target_pairs={{0,96},{1,33},{32,64},{33,1},{64,32},{65,97},{96,0},{97,65},{2,98}... | collective-permute-start | bytes 3612680 | tf_op jit(solution)/shard_map/ppermute | solution.py:140
  313.4 25.1 %collective-permute-start.33 = (bf16[176,3584]{1,0:T(8,128)(2,1)S(1)}, bf16[176,3584]{1,0:T(8,128)(2,1)S(1)}, u32[]{:S(2)}, u32[]{:S(2)}) collective-permute-start(bf16[176,3584]{1,0:T(8,128)(2,1)S(1)} %split.97), channel_id=1, source_target_pairs={{0,24},{1,9},{8,16},{9,1},{16,8},{17,25},{24,0},{25,17},{2,26},{3,... | collective-permute-start | bytes 3784712 | tf_op jit(solution)/shard_map/ppermute | solution.py:140
  314.2 23.5 %collective-permute-start.34 = (bf16[168,3584]{1,0:T(8,128)(2,1)S(1)}, bf16[168,3584]{1,0:T(8,128)(2,1)S(1)}, u32[]{:S(2)}, u32[]{:S(2)}) collective-permute-start(bf16[168,3584]{1,0:T(8,128)(2,1)S(1)} %split.98), channel_id=1, source_target_pairs={{0,6},{1,3},{2,4},{3,1},{4,2},{5,7},{6,0},{7,5},{8,14},{9,11},{10,... | collective-permute-start | bytes 3612680 | tf_op jit(solution)/shard_map/ppermute | solution.py:140
  338.9 11.1 %collective-permute-start.38 = (bf16[84,3584]{1,0:T(8,128)(2,1)S(1)}, bf16[84,3584]{1,0:T(8,128)(2,1)S(1)}, u32[]{:S(2)}, u32[]{:S(2)}) collective-permute-start(bf16[84,3584]{1,0:T(8,128)(2,1)S(1)} %split.105), channel_id=1, source_target_pairs={{0,32},{1,97},{32,0},{33,65},{64,96},{65,33},{96,64},{97,1},{2,34}... | collective-permute-start | bytes 1806344 | tf_op jit(solution)/shard_map/ppermute | solution.py:140
  341.3 12.8 %collective-permute-start.36 = (bf16[88,3584]{1,0:T(8,128)(2,1)S(1)}, bf16[88,3584]{1,0:T(8,128)(2,1)S(1)}, u32[]{:S(2)}, u32[]{:S(2)}) collective-permute-start(bf16[88,3584]{1,0:T(8,128)(2,1)S(1)} %split.101), channel_id=1, source_target_pairs={{0,8},{1,25},{8,0},{9,17},{16,24},{17,9},{24,16},{25,1},{2,10},{3,... | collective-permute-start | bytes 1892360 | tf_op jit(solution)/shard_map/ppermute | solution.py:140
  342.6 11.5 %collective-permute-start.37 = (bf16[84,3584]{1,0:T(8,128)(2,1)S(1)}, bf16[84,3584]{1,0:T(8,128)(2,1)S(1)}, u32[]{:S(2)}, u32[]{:S(2)}) collective-permute-start(bf16[84,3584]{1,0:T(8,128)(2,1)S(1)} %split.103), channel_id=1, source_target_pairs={{0,2},{1,7},{2,0},{3,5},{4,6},{5,3},{6,4},{7,1},{8,10},{9,15},{10,... | collective-permute-start | bytes 1806344 | tf_op jit(solution)/shard_map/ppermute | solution.py:140
  354.3 7.3 %collective-permute-start.41 = (bf16[42,3584]{1,0:T(8,128)(2,1)S(1)}, bf16[42,3584]{1,0:T(8,128)(2,1)S(1)}, u32[]{:S(2)}, u32[]{:S(2)}) collective-permute-start(bf16[42,3584]{1,0:T(8,128)(2,1)S(1)} %split.111), channel_id=1, source_target_pairs={{0,6},{1,3},{2,4},{3,1},{4,2},{5,7},{6,0},{7,5},{8,14},{9,11},{10,... | collective-permute-start | bytes 903176 | tf_op jit(solution)/shard_map/ppermute | solution.py:140
  355.6 10.0 %collective-permute-start.39 = (bf16[44,3584]{1,0:T(8,128)(2,1)S(1)}, bf16[44,3584]{1,0:T(8,128)(2,1)S(1)}, u32[]{:S(2)}, u32[]{:S(2)}) collective-permute-start(bf16[44,3584]{1,0:T(8,128)(2,1)S(1)} %split.107), channel_id=1, source_target_pairs={{0,96},{1,33},{32,64},{33,1},{64,32},{65,97},{96,0},{97,65},{2,98}... | collective-permute-start | bytes 946184 | tf_op jit(solution)/shard_map/ppermute | solution.py:140
  357.0 8.5 %collective-permute-start.40 = (bf16[42,3584]{1,0:T(8,128)(2,1)S(1)}, bf16[42,3584]{1,0:T(8,128)(2,1)S(1)}, u32[]{:S(2)}, u32[]{:S(2)}) collective-permute-start(bf16[42,3584]{1,0:T(8,128)(2,1)S(1)} %split.109), channel_id=1, source_target_pairs={{0,24},{1,9},{8,16},{9,1},{16,8},{17,25},{24,0},{25,17},{2,26},{3,... | collective-permute-start | bytes 903176 | tf_op jit(solution)/shard_map/ppermute | solution.py:140
  365.7 5.9 %collective-permute-start.44 = (bf16[21,3584]{1,0:T(8,128)(2,1)S(1)}, bf16[21,3584]{1,0:T(8,128)(2,1)S(1)}, u32[]{:S(2)}, u32[]{:S(2)}) collective-permute-start(bf16[21,3584]{1,0:T(8,128)(2,1)S(1)} %split.117), channel_id=1, source_target_pairs={{0,2},{1,7},{2,0},{3,5},{4,6},{5,3},{6,4},{7,1},{8,10},{9,15},{10,... | collective-permute-start | bytes 451592 | tf_op jit(solution)/shard_map/ppermute | solution.py:140
  368.4 6.6 %collective-permute-start.42 = (bf16[22,3584]{1,0:T(8,128)(2,1)S(1)}, bf16[22,3584]{1,0:T(8,128)(2,1)S(1)}, u32[]{:S(2)}, u32[]{:S(2)}) collective-permute-start(bf16[22,3584]{1,0:T(8,128)(2,1)S(1)} %split.113), channel_id=1, source_target_pairs={{0,32},{1,97},{32,0},{33,65},{64,96},{65,33},{96,64},{97,1},{2,34}... | collective-permute-start | bytes 473096 | tf_op jit(solution)/shard_map/ppermute | solution.py:140
  369.5 5.5 %collective-permute-start.43 = (bf16[21,3584]{1,0:T(8,128)(2,1)S(1)}, bf16[21,3584]{1,0:T(8,128)(2,1)S(1)}, u32[]{:S(2)}, u32[]{:S(2)}) collective-permute-start(bf16[21,3584]{1,0:T(8,128)(2,1)S(1)} %split.115), channel_id=1, source_target_pairs={{0,8},{1,25},{8,0},{9,17},{16,24},{17,9},{24,16},{25,1},{2,10},{3,... | collective-permute-start | bytes 451592 | tf_op jit(solution)/shard_map/ppermute | solution.py:140
  (5 other events, 69.8 us)

commit v4 on v3

--- a/solution.py
+++ b/solution.py
@@ -16,17 +16,35 @@
 COLS = 512
 
 
-def token_gates(scores, route, source, experts):
-    gates = ROUTE_SCALE * scores / jnp.sum(scores, axis=1, keepdims=True)
-    native = jnp.arange(experts, dtype=jnp.int32)
-    copies = jnp.arange(2 * experts, dtype=jnp.int32)
-    held = jnp.concatenate((native, source))
-    routed = route[:, :, None] == copies
-    ids = jnp.sum(jnp.where(routed, held, 0), axis=2)
-    return jnp.sum(jnp.where(ids[:, :, None] == native, gates[:, :, None], 0.0), axis=1)
-
-
-def ffn_kernel(experts, counts, ids, *refs):
+def pack_kernel(experts, source, hidden, scores, route, o_ref):
+    width = hidden.shape[1]
+    gates = ROUTE_SCALE * scores[...] / jnp.sum(scores[...], axis=1, keepdims=True)
+    ids = route[...]
+    for s in range(experts):
+        ids = jnp.where(route[...] == experts + s, source[s], ids)
+    lane = lax.broadcasted_iota(jnp.int32, (hidden.shape[0], PAD), 1)
+    dense = jnp.zeros(lane.shape, jnp.float32)
+    for k in range(ids.shape[1]):
+        mine = (lane == ids[:, k : k + 1]) | (lane == ids[:, k : k + 1] + experts)
+        dense += jnp.where(mine, gates[:, k : k + 1], 0.0)
+    high = dense.astype(jnp.bfloat16).astype(jnp.float32)
+    o_ref[:, width:] = jnp.where(lane < experts, high, dense - high).astype(o_ref.dtype)
+    o_ref[:, :width] = hidden[...]
+
+
+def pack(hidden, scores, route, source):
+    tokens, width = hidden.shape
+    whole = pl.BlockSpec(memory_space=pltpu.VMEM)
+    return pl.pallas_call(
+        functools.partial(pack_kernel, source.shape[0]),
+        in_specs=[pl.BlockSpec(memory_space=pltpu.SMEM), whole, whole, whole],
+        out_specs=whole,
+        out_shape=jax.ShapeDtypeStruct((tokens, width + PAD), hidden.dtype),
+        compiler_params=pltpu.CompilerParams(vmem_limit_bytes=8 * 1024 * 1024),
+    )(source, hidden, scores, route)
+
+
+def ffn_kernel(experts, offsets, counts, ids, *refs):
     n = len(counts)
     pieces, weights, outs = refs[:n], refs[n : n + 6], refs[n + 6 : 2 * n + 6]
     x, gate, up, down, act, o, x_sems, w_sems, o_sems = refs[2 * n + 6 :]
@@ -34,7 +52,11 @@
     width, hid = ga.shape
     starts = [sum(counts[:j]) for j in range(n)]
     arrive = [
-        pltpu.make_async_copy(pieces[j], x.at[pl.ds(starts[j], counts[j])], x_sems.at[j])
+        pltpu.make_async_copy(
+            pieces[j].at[pl.ds(offsets[j], counts[j])],
+            x.at[pl.ds(starts[j], counts[j])],
+            x_sems.at[j],
+        )
         for j in range(n)
     ]
     load = [
@@ -94,13 +116,17 @@
         copy.wait()
 
 
-def ffn(ids, pieces, weights, experts):
+def ffn(ids, pieces, weights, experts, half=None):
     width, hid = weights[0].shape
-    counts = tuple(piece.shape[0] for piece in pieces)
+    offsets, counts = (0,) * len(pieces), tuple(piece.shape[0] for piece in pieces)
+    if half is not None:
+        cuts = tuple(-(-count // 32) * 16 for count in counts)
+        rests = tuple(count - cut for count, cut in zip(counts, cuts))
+        offsets, counts = (offsets, cuts) if half == 0 else (cuts, rests)
     amount, n = sum(counts), len(counts)
     anywhere = pl.BlockSpec(memory_space=pl.ANY)
     return pl.pallas_call(
-        functools.partial(ffn_kernel, experts, counts),
+        functools.partial(ffn_kernel, experts, offsets, counts),
         in_specs=[pl.BlockSpec(memory_space=pltpu.SMEM)] + [anywhere] * (n + 6),
         out_specs=[anywhere] * n,
         scratch_shapes=[
@@ -165,13 +191,7 @@
     experts = 2 * spots
     tokens, width = hidden.shape
     swap = [(0, 1), (1, 0)]
-    dense = token_gates(scores, route, source, experts)
-    high = lax.reduce_precision(dense, 8, 7)
-    low = dense - high
-    filler = jnp.zeros((tokens, PAD - 2 * experts), jnp.bfloat16)
-    packed = jnp.concatenate(
-        (hidden, high.astype(jnp.bfloat16), low.astype(jnp.bfloat16), filler), axis=1
-    )
+    packed = pack(hidden, scores, route, source)
     weights = []
     for own in (gate_proj[0], up_proj[0], down_proj[0]):
         weights += [own, lax.ppermute(own, "core", swap)]
@@ -196,12 +216,18 @@
         done.append(ffn(ids, steps[-1], weights, experts))
         arriving, done[-1] = lax.optimization_barrier((arriving, done[-1]))
         steps.append(arriving)
-    done.append(ffn(ids, steps[-1], weights, experts))
-    totals = list(done[-1])
     backs = [ring(order[2], lax.axis_size(order[2]), -1) for order in ORDERS]
-    for pieces in done[-2::-1]:
-        arrived = lax.optimization_barrier([back(t) for back, t in zip(backs, totals)])
-        totals = [add(*pair) for pair in zip(arrived, pieces)]
+    head = ffn(ids, steps[-1], weights, experts, 0)
+    early = [back(t) for back, t in zip(backs, head)]
+    tail = ffn(ids, steps[-1], weights, experts, 1)
+    early, tail = lax.optimization_barrier((early, tail))
+    late = lax.optimization_barrier([back(t) for back, t in zip(backs, tail)])
+    arrived = (early, late)
+    arrived = [jnp.concatenate(pair, axis=0) for pair in zip(*arrived)]
+    for pieces in done[::-1]:
+        if arrived is None:
+            arrived = lax.optimization_barrier([back(t) for back, t in zip(backs, totals)])
+        totals, arrived = [add(*pair) for pair in zip(arrived, pieces)], None
     for phase in (1, 0):
         totals = halve(totals, [order[phase] for order in ORDERS])
     return jnp.concatenate(totals, axis=0)

time: 383 us -> 382 us (level)
  waiting for transfers between devices: 168 us -> 153 us
  Pallas kernels: 121 us -> 128 us
  starting transfers between devices: 66.7 us -> 70.9 us
  local copies, waits for them, and re-layouts: 3.21 us -> 7.15 us
    ppermute x18 -> x21, waiting for transfers between devices: 93.9 us -> 78.7 us  [ring(): return lambda block: lax.ppermute(block, (axis, 'core'), pairs)]
    pallas_call x4 -> x6, Pallas kernels: 121 us -> 128 us  [the longest x5 127 us: ffn(): pl.pallas_call(functools.partial(ffn_kernel, experts, offsets, counts), i...]
    unnamed x17 -> x24, local copies, waits for them, and re-layouts: 0.8 us -> 6.08 us
    ppermute x18 -> x21, starting transfers between devices: 25.9 us -> 31.1 us  [ring(): return lambda block: lax.ppermute(block, (axis, 'core'), pairs)]
  transfers between devices with their start and end apart: 45 -> 48, of which waited for: 25 -> 25; matrix products, arithmetic and copies ran while one was open for 4% -> 3% of each run, Pallas kernels for 24% -> 29%
where the time goes in v4:
time: 382 us; the launch traced here: 376 us
  waiting for transfers between devices  153 us (40%)
  Pallas kernels  128 us (34%)
  starting transfers between devices  70.9 us (19%)
  other arithmetic  16.1 us (4%)
  local copies, waits for them, and re-layouts  7.15 us (2%)
    pallas_call x5, Pallas kernels, ffn(): pl.pallas_call(functools.partial(ffn_kernel, experts, offsets, counts), i...  127 us
    ppermute x21, waiting for transfers between devices, ring(): return lambda block: lax.ppermute(block, (axis, 'core'), pairs)  78.7 us
    ppermute x24, waiting for transfers between devices, meet(): return lambda block: lax.ppermute(block, (axis, 'core'), pairs)  74.5 us
    ppermute x24, starting transfers between devices, meet(): return lambda block: lax.ppermute(block, (axis, 'core'), pairs)  39.2 us
    ppermute x21, starting transfers between devices, ring(): return lambda block: lax.ppermute(block, (axis, 'core'), pairs)  31.1 us
    convert_element_type x20, other arithmetic, add(): (one.astype(jnp.float32) + other.astype(jnp.float32)).astype(one.dtype)  10.4 us
  transfers between devices with their start and end apart: 48, of which 25 were waited for; matrix products, arithmetic and copies ran while one was open for 3% of the time, Pallas kernels for 29%

profile of v4, /device:TPU:32, one launch (start us, length us, event | category | flops | bytes accessed | tf_op | source)
XLA Modules:
  0.0 375.7 jit_solution(7238055158546900305)
XLA Ops:
  4.9 1.7 collective-permute-start.2
  6.5 3.8 %collective-permute-done.4 = bf16[21,3712]{1,0:T(8,128)(2,1)S(1)} collective-permute-done((bf16[21,3712]{1,0:T(8,128)(2,1)S(1)}, bf16[21,3712]{1,0:T(8,128)(2,1)S(1)}, u32[]{:S(2)}, u32[]{:S(2)}) %collective-permute-start.4) | collective-permute-done | bytes 155936 | tf_op jit(solution)/shard_map/ppermute | solution.py:166
  11.9 2.0 collective-permute-start.5
  13.9 1.8 collective-permute-done
  15.8 3.0 collective-permute-start.3
  19.3 2.6 collective-permute-start.1
  22.1 2.2 collective-permute-done.3
  24.5 3.4 collective-permute-done.1
  28.3 2.1 collective-permute-start.11
  32.0 6.8 %collective-permute-done.13 = bf16[84,3712]{1,0:T(8,128)(2,1)S(1)} collective-permute-done((bf16[84,3712]{1,0:T(8,128)(2,1)S(1)}, bf16[84,3712]{1,0:T(8,128)(2,1)S(1)}, u32[]{:S(2)}, u32[]{:S(2)}) %collective-permute-start.13) | collective-permute-done | bytes 623648 | tf_op jit(solution)/shard_map/ppermute | solution.py:166
  38.9 2.7 collective-permute-start.14
  41.8 2.9 collective-permute-start.12
  44.8 3.1 collective-permute-start.10
  47.9 9.3 %collective-permute-done.14 = bf16[168,3712]{1,0:T(8,128)(2,1)S(1)} collective-permute-done((bf16[168,3712]{1,0:T(8,128)(2,1)S(1)}, bf16[168,3712]{1,0:T(8,128)(2,1)S(1)}, u32[]{:S(2)}, u32[]{:S(2)}) %collective-permute-start.14) | collective-permute-done | bytes 1247264 | tf_op jit(solution)/shard_map/ppermute | solution.py:166
  57.2 1.7 pad_maximum_fusion.2.refs_2_
  59.6 1.7 pad_maximum_fusion.1.refs_1_
  61.3 2.3 collective-permute-done.10
  65.7 30.6 %shard_map.74 = (bf16[352,3584]{1,0:T(8,128)(2,1)}, bf16[336,3584]{1,0:T(8,128)(2,1)S(1)}, bf16[336,3584]{1,0:T(8,128)(2,1)}) custom-call(s32[2]{0:T(128)S(1)} %pad_add_fusion.ids, bf16[352,3712]{1,0:T(8,128)(2,1)} %copy-done.2, bf16[336,3712]{1,0:T(8,128)(2,1)} %pad_maximum_fusion.1.refs_1_, bf16[336,3712]{1,0:T(8,128)(2,1)} %pad_maximum_fusion.2.refs_2_, ...), custom_call_target="tpu_custom_call" | custom-call | flops 22548578304 | bytes 36700160 | tf_op jit(solution)/shard_map/pallas_call | solution.py:128
  96.9 4.5 %collective-permute-start.18 = (bf16[352,3712]{1,0:T(8,128)(2,1)}, bf16[352,3712]{1,0:T(8,128)(2,1)S(1)}, u32[]{:S(2)}, u32[]{:S(2)}) collective-permute-start(bf16[352,3712]{1,0:T(8,128)(2,1)} %collective-permute-done.15.refs_0_), channel_id=1, source_target_pairs={{0,2},{1,7},{2,4},{3,1},{4,6},{5,3},{6,0},{7,5},{8,10},{9,15},{10,... | collective-permute-start | bytes 7839752 | tf_op jit(solution)/shard_map/ppermute | solution.py:157
  102.0 1.7 collective-permute-start.20
  103.7 30.2 %shard_map.75 = (bf16[352,3584]{1,0:T(8,128)(2,1)}, bf16[336,3584]{1,0:T(8,128)(2,1)S(1)}, bf16[336,3584]{1,0:T(8,128)(2,1)}) custom-call(s32[2]{0:T(128)S(1)} %pad_add_fusion.ids, bf16[352,3712]{1,0:T(8,128)(2,1)} %collective-permute-done.15.refs_0_, bf16[336,3712]{1,0:T(8,128)(2,1)} %collective-permute-done.16.refs_1_, ...), custom_call_target="tpu_custom_call" | custom-call | flops 22548578304 | bytes 36700160 | tf_op jit(solution)/shard_map/pallas_call | solution.py:128
  136.8 1.9 collective-permute-start.23
  138.8 30.5 %shard_map.76 = (bf16[352,3584]{1,0:T(8,128)(2,1)}, bf16[336,3584]{1,0:T(8,128)(2,1)S(1)}, bf16[336,3584]{1,0:T(8,128)(2,1)}) custom-call(s32[2]{0:T(128)S(1)} %pad_add_fusion.ids, bf16[352,3712]{1,0:T(8,128)(2,1)} %copy-done.9, bf16[336,3712]{1,0:T(8,128)(2,1)} %copy-done.10, bf16[336,3712]{1,0:T(8,128)(2,1)} %collective-permute-done.20.refs_2_, ...), custom_call_target="tpu_custom_call" | custom-call | flops 22548578304 | bytes 36700160 | tf_op jit(solution)/shard_map/pallas_call | solution.py:128
  170.8 18.4 %shard_map.77 = (bf16[176,3584]{1,0:T(8,128)(2,1)}, bf16[176,3584]{1,0:T(8,128)(2,1)S(1)}, bf16[176,3584]{1,0:T(8,128)(2,1)S(1)}) custom-call(s32[2]{0:T(128)S(1)} %pad_add_fusion.ids, bf16[352,3712]{1,0:T(8,128)(2,1)} %copy-done.8, bf16[336,3712]{1,0:T(8,128)(2,1)} %collective-permute-done.22.refs_1_, bf16[336,3712]{1,0:T(8,128)(2,1)} %collective-permute-done.23.refs_2_, ...), custom_call_target="tpu_custom_call" | custom-call | flops 11626610688 | bytes 29589504 | tf_op jit(solution)/shard_map/pallas_call | solution.py:128
  190.7 1.9 collective-permute-start.25
  192.6 2.0 collective-permute-start.26
  194.6 17.0 %shard_map.78 = (bf16[176,3584]{1,0:T(8,128)(2,1)S(1)}, bf16[160,3584]{1,0:T(8,128)(2,1)S(1)}, bf16[160,3584]{1,0:T(8,128)(2,1)S(1)}) custom-call(s32[2]{0:T(128)S(1)} %pad_add_fusion.ids, bf16[352,3712]{1,0:T(8,128)(2,1)} %copy-done.8, bf16[336,3712]{1,0:T(8,128)(2,1)} %collective-permute-done.22.refs_1_, ...), custom_call_target="tpu_custom_call" | custom-call | flops 10921967616 | bytes 29130752 | tf_op jit(solution)/shard_map/pallas_call | solution.py:128
  214.5 13.7 %collective-permute-done.28 = bf16[160,3584]{1,0:T(8,128)(2,1)S(1)} collective-permute-done((bf16[160,3584]{1,0:T(8,128)(2,1)S(1)}, bf16[160,3584]{1,0:T(8,128)(2,1)S(1)}, u32[]{:S(2)}, u32[]{:S(2)}) %collective-permute-start.28) | collective-permute-done | bytes 1146912 | tf_op jit(solution)/shard_map/ppermute | solution.py:157
  229.1 2.6 add_convert_fusion.7
  231.7 2.7 collective-permute-start.32
  234.4 1.9 add_convert_fusion.2
  238.0 1.9 collective-permute-start.31
  239.9 21.4 %collective-permute-done.32 = bf16[336,3584]{1,0:T(8,128)(2,1)S(1)} collective-permute-done((bf16[336,3584]{1,0:T(8,128)(2,1)S(1)}, bf16[336,3584]{1,0:T(8,128)(2,1)S(1)}, u32[]{:S(2)}, u32[]{:S(2)}) %collective-permute-start.32) | collective-permute-done | bytes 2408480 | tf_op jit(solution)/shard_map/ppermute | solution.py:157
  261.3 6.1 %collective-permute-done.31 = bf16[336,3584]{1,0:T(8,128)(2,1)S(1)} collective-permute-done((bf16[336,3584]{1,0:T(8,128)(2,1)S(1)}, bf16[336,3584]{1,0:T(8,128)(2,1)S(1)}, u32[]{:S(2)}, u32[]{:S(2)}) %collective-permute-start.31) | collective-permute-done | bytes 2408480 | tf_op jit(solution)/shard_map/ppermute | solution.py:157
  271.2 3.3 collective-permute-start.34
  274.5 27.9 %collective-permute-done.35 = bf16[336,3584]{1,0:T(8,128)(2,1)S(1)} collective-permute-done((bf16[336,3584]{1,0:T(8,128)(2,1)S(1)}, bf16[336,3584]{1,0:T(8,128)(2,1)S(1)}, u32[]{:S(2)}, u32[]{:S(2)}) %collective-permute-start.35) | collective-permute-done | bytes 2408480 | tf_op jit(solution)/shard_map/ppermute | solution.py:157
  302.4 8.0 %collective-permute-done.34 = bf16[336,3584]{1,0:T(8,128)(2,1)S(1)} collective-permute-done((bf16[336,3584]{1,0:T(8,128)(2,1)S(1)}, bf16[336,3584]{1,0:T(8,128)(2,1)S(1)}, u32[]{:S(2)}, u32[]{:S(2)}) %collective-permute-start.34) | collective-permute-done | bytes 2408480 | tf_op jit(solution)/shard_map/ppermute | solution.py:157
  311.1 3.3 collective-permute-start.38
  316.0 19.6 %collective-permute-done.38 = bf16[168,3584]{1,0:T(8,128)(2,1)S(1)} collective-permute-done((bf16[168,3584]{1,0:T(8,128)(2,1)S(1)}, bf16[168,3584]{1,0:T(8,128)(2,1)S(1)}, u32[]{:S(2)}, u32[]{:S(2)}) %collective-permute-start.38) | collective-permute-done | bytes 1204256 | tf_op jit(solution)/shard_map/ppermute | solution.py:166
  335.6 3.6 collective-permute-done.37
  343.3 2.7 collective-permute-start.40
  346.0 4.6 %collective-permute-done.41 = bf16[84,3584]{1,0:T(8,128)(2,1)S(1)} collective-permute-done((bf16[84,3584]{1,0:T(8,128)(2,1)S(1)}, bf16[84,3584]{1,0:T(8,128)(2,1)S(1)}, u32[]{:S(2)}, u32[]{:S(2)}) %collective-permute-start.41) | collective-permute-done | bytes 602144 | tf_op jit(solution)/shard_map/ppermute | solution.py:166
  350.7 3.7 collective-permute-done.40
  356.2 2.4 collective-permute-start.43
  358.6 3.3 collective-permute-done.44
  361.9 2.8 collective-permute-done.43
  364.9 2.4 collective-permute-start.47
  370.6 3.9 %collective-permute-done.46 = bf16[21,3584]{1,0:T(8,128)(2,1)S(1)} collective-permute-done((bf16[21,3584]{1,0:T(8,128)(2,1)S(1)}, bf16[21,3584]{1,0:T(8,128)(2,1)S(1)}, u32[]{:S(2)}, u32[]{:S(2)}) %collective-permute-start.46) | collective-permute-done | bytes 150560 | tf_op jit(solution)/shard_map/ppermute | solution.py:166
  (126 shorter events, 41.2 us)
Async XLA Ops:
  0.0 28.1 %collective-permute-start.6 = (bf16[3584,512]{1,0:T(8,128)(2,1)}, bf16[3584,512]{1,0:T(8,128)(2,1)}, u32[]{:S(2)}, u32[]{:S(2)}) collective-permute-start(bf16[3584,512]{1,0:T(8,128)(2,1)} %bitcast.5), channel_id=1, source_target_pairs={{0,1},{1,0},{2,3},{3,2},{4,5},{5,4},{6,7},{7,6},{8,9},{9,8},{10,11... | collective-permute-start | bytes 11010056 | tf_op jit(solution)/shard_map/ppermute | solution.py:197
  0.0 28.1 %collective-permute-start.7 = (bf16[3584,512]{1,0:T(8,128)(2,1)}, bf16[3584,512]{1,0:T(8,128)(2,1)}, u32[]{:S(2)}, u32[]{:S(2)}) collective-permute-start(bf16[3584,512]{1,0:T(8,128)(2,1)} %bitcast.11), channel_id=1, source_target_pairs={{0,1},{1,0},{2,3},{3,2},{4,5},{5,4},{6,7},{7,6},{8,9},{9,8},{10,11... | collective-permute-start | bytes 11010056 | tf_op jit(solution)/shard_map/ppermute | solution.py:197
  0.5 27.6 %collective-permute-start.8 = (bf16[512,3584]{1,0:T(8,128)(2,1)}, bf16[512,3584]{1,0:T(8,128)(2,1)}, u32[]{:S(2)}, u32[]{:S(2)}) collective-permute-start(bf16[512,3584]{1,0:T(8,128)(2,1)} %bitcast.17), channel_id=1, source_target_pairs={{0,1},{1,0},{2,3},{3,2},{4,5},{5,4},{6,7},{7,6},{8,9},{9,8},{10,11... | collective-permute-start | bytes 11010056 | tf_op jit(solution)/shard_map/ppermute | solution.py:197
  4.7 5.6 %collective-permute-start.4 = (bf16[21,3712]{1,0:T(8,128)(2,1)S(1)}, bf16[21,3712]{1,0:T(8,128)(2,1)S(1)}, u32[]{:S(2)}, u32[]{:S(2)}) collective-permute-start(bf16[21,3712]{1,0:T(8,128)(2,1)S(1)} %get-tuple-element.149), channel_id=1, source_target_pairs={{0,2},{1,7},{2,0},{3,5},{4,6},{5,3},{6,4},{7,1},{8,10},{9,15},{10,... | collective-permute-start | bytes 467720 | tf_op jit(solution)/shard_map/ppermute | solution.py:166
  4.9 7.0 %collective-permute-start.2 = (bf16[21,3712]{1,0:T(8,128)(2,1)S(1)}, bf16[21,3712]{1,0:T(8,128)(2,1)S(1)}, u32[]{:S(2)}, u32[]{:S(2)}) collective-permute-start(bf16[21,3712]{1,0:T(8,128)(2,1)S(1)} %get-tuple-element.150), channel_id=1, source_target_pairs={{0,8},{1,25},{8,0},{9,17},{16,24},{17,9},{24,16},{25,1},{2,10},{3,... | collective-permute-start | bytes 467720 | tf_op jit(solution)/shard_map/ppermute | solution.py:166
  10.3 5.5 %collective-permute-start = (bf16[22,3712]{1,0:T(8,128)(2,1)S(1)}, bf16[22,3712]{1,0:T(8,128)(2,1)S(1)}, u32[]{:S(2)}, u32[]{:S(2)}) collective-permute-start(bf16[22,3712]{1,0:T(8,128)(2,1)S(1)} %slice.12), channel_id=1, source_target_pairs={{0,32},{1,97},{32,0},{33,65},{64,96},{65,33},{96,64},{97,1},{2,34}... | collective-permute-start | bytes 489992 | tf_op jit(solution)/shard_map/ppermute | solution.py:166
  11.9 7.5 %collective-permute-start.5 = (bf16[42,3712]{1,0:T(8,128)(2,1)S(1)}, bf16[42,3712]{1,0:T(8,128)(2,1)S(1)}, u32[]{:S(2)}, u32[]{:S(2)}) collective-permute-start(bf16[42,3712]{1,0:T(8,128)(2,1)S(1)} %pad_maximum_fusion.12), channel_id=1, source_target_pairs={{0,6},{1,3},{2,4},{3,1},{4,2},{5,7},{6,0},{7,5},{8,14},{9,11},{10,... | collective-permute-start | bytes 935432 | tf_op jit(solution)/shard_map/ppermute | solution.py:166
  15.8 8.6 %collective-permute-start.3 = (bf16[42,3712]{1,0:T(8,128)(2,1)S(1)}, bf16[42,3712]{1,0:T(8,128)(2,1)S(1)}, u32[]{:S(2)}, u32[]{:S(2)}) collective-permute-start(bf16[42,3712]{1,0:T(8,128)(2,1)S(1)} %pad_maximum_fusion.11), channel_id=1, source_target_pairs={{0,24},{1,9},{8,16},{9,1},{16,8},{17,25},{24,0},{25,17},{2,26},{3,... | collective-permute-start | bytes 935432 | tf_op jit(solution)/shard_map/ppermute | solution.py:166
  19.3 8.6 %collective-permute-start.1 = (bf16[44,3712]{1,0:T(8,128)(2,1)S(1)}, bf16[44,3712]{1,0:T(8,128)(2,1)S(1)}, u32[]{:S(2)}, u32[]{:S(2)}) collective-permute-start(bf16[44,3712]{1,0:T(8,128)(2,1)S(1)} %pad_maximum_fusion.10), channel_id=1, source_target_pairs={{0,96},{1,33},{32,64},{33,1},{64,32},{65,97},{96,0},{97,65},{2,98}... | collective-permute-start | bytes 979976 | tf_op jit(solution)/shard_map/ppermute | solution.py:166
  28.1 10.6 %collective-permute-start.13 = (bf16[84,3712]{1,0:T(8,128)(2,1)S(1)}, bf16[84,3712]{1,0:T(8,128)(2,1)S(1)}, u32[]{:S(2)}, u32[]{:S(2)}) collective-permute-start(bf16[84,3712]{1,0:T(8,128)(2,1)S(1)} %pad_maximum_fusion.8), channel_id=1, source_target_pairs={{0,32},{1,97},{32,0},{33,65},{64,96},{65,33},{96,64},{97,1},{2,34}... | collective-permute-start | bytes 1870856 | tf_op jit(solution)/shard_map/ppermute | solution.py:166
  28.3 13.3 %collective-permute-start.11 = (bf16[84,3712]{1,0:T(8,128)(2,1)S(1)}, bf16[84,3712]{1,0:T(8,128)(2,1)S(1)}, u32[]{:S(2)}, u32[]{:S(2)}) collective-permute-start(bf16[84,3712]{1,0:T(8,128)(2,1)S(1)} %pad_maximum_fusion.7), channel_id=1, source_target_pairs={{0,2},{1,7},{2,0},{3,5},{4,6},{5,3},{6,4},{7,1},{8,10},{9,15},{10,... | collective-permute-start | bytes 1870856 | tf_op jit(solution)/shard_map/ppermute | solution.py:166
  30.4 14.3 %collective-permute-start.9 = (bf16[88,3712]{1,0:T(8,128)(2,1)S(1)}, bf16[88,3712]{1,0:T(8,128)(2,1)S(1)}, u32[]{:S(2)}, u32[]{:S(2)}) collective-permute-start(bf16[88,3712]{1,0:T(8,128)(2,1)S(1)} %pad_maximum_fusion.6), channel_id=1, source_target_pairs={{0,8},{1,25},{8,0},{9,17},{16,24},{17,9},{24,16},{25,1},{2,10},{3,... | collective-permute-start | bytes 1959944 | tf_op jit(solution)/shard_map/ppermute | solution.py:166
  38.9 18.2 %collective-permute-start.14 = (bf16[168,3712]{1,0:T(8,128)(2,1)S(1)}, bf16[168,3712]{1,0:T(8,128)(2,1)S(1)}, u32[]{:S(2)}, u32[]{:S(2)}) collective-permute-start(bf16[168,3712]{1,0:T(8,128)(2,1)S(1)} %pad_maximum_fusion.5), channel_id=1, source_target_pairs={{0,96},{1,33},{32,64},{33,1},{64,32},{65,97},{96,0},{97,65},{2,98}... | collective-permute-start | bytes 3741704 | tf_op jit(solution)/shard_map/ppermute | solution.py:166
  41.8 17.8 %collective-permute-start.12 = (bf16[168,3712]{1,0:T(8,128)(2,1)S(1)}, bf16[168,3712]{1,0:T(8,128)(2,1)S(1)}, u32[]{:S(2)}, u32[]{:S(2)}) collective-permute-start(bf16[168,3712]{1,0:T(8,128)(2,1)S(1)} %pad_maximum_fusion.4), channel_id=1, source_target_pairs={{0,6},{1,3},{2,4},{3,1},{4,2},{5,7},{6,0},{7,5},{8,14},{9,11},{10,... | collective-permute-start | bytes 3741704 | tf_op jit(solution)/shard_map/ppermute | solution.py:166
  44.8 18.9 %collective-permute-start.10 = (bf16[176,3712]{1,0:T(8,128)(2,1)S(1)}, bf16[176,3712]{1,0:T(8,128)(2,1)S(1)}, u32[]{:S(2)}, u32[]{:S(2)}) collective-permute-start(bf16[176,3712]{1,0:T(8,128)(2,1)S(1)} %pad_maximum_fusion.3), channel_id=1, source_target_pairs={{0,24},{1,9},{8,16},{9,1},{16,8},{17,25},{24,0},{25,17},{2,26},{3,... | collective-permute-start | bytes 3919880 | tf_op jit(solution)/shard_map/ppermute | solution.py:166
  63.8 33.0 %collective-permute-start.15 = (bf16[352,3712]{1,0:T(8,128)(2,1)S(1)}, bf16[352,3712]{1,0:T(8,128)(2,1)}, u32[]{:S(2)}, u32[]{:S(2)}) collective-permute-start(bf16[352,3712]{1,0:T(8,128)(2,1)S(1)} %pad_maximum_fusion.refs_0_), channel_id=1, source_target_pairs={{0,2},{1,7},{2,4},{3,1},{4,6},{5,3},{6,0},{7,5},{8,10},{9,15},{10,... | collective-permute-start | bytes 7839752 | tf_op jit(solution)/shard_map/ppermute | solution.py:157
  63.9 32.4 %collective-permute-start.16 = (bf16[336,3712]{1,0:T(8,128)(2,1)}, bf16[336,3712]{1,0:T(8,128)(2,1)}, u32[]{:S(2)}, u32[]{:S(2)}) collective-permute-start(bf16[336,3712]{1,0:T(8,128)(2,1)} %pad_maximum_fusion.1.refs_1_), channel_id=1, source_target_pairs={{0,32},{1,97},{32,64},{33,1},{64,96},{65,33},{96,0},{97,65},{2,34}... | collective-permute-start | bytes 7483400 | tf_op jit(solution)/shard_map/ppermute | solution.py:157
  64.8 32.1 %collective-permute-start.17 = (bf16[336,3712]{1,0:T(8,128)(2,1)}, bf16[336,3712]{1,0:T(8,128)(2,1)}, u32[]{:S(2)}, u32[]{:S(2)}) collective-permute-start(bf16[336,3712]{1,0:T(8,128)(2,1)} %pad_maximum_fusion.2.refs_2_), channel_id=1, source_target_pairs={{0,8},{1,25},{8,16},{9,1},{16,24},{17,9},{24,0},{25,17},{2,10},{3,... | collective-permute-start | bytes 7483400 | tf_op jit(solution)/shard_map/ppermute | solution.py:157
  96.9 37.1 %collective-permute-start.18 = (bf16[352,3712]{1,0:T(8,128)(2,1)}, bf16[352,3712]{1,0:T(8,128)(2,1)S(1)}, u32[]{:S(2)}, u32[]{:S(2)}) collective-permute-start(bf16[352,3712]{1,0:T(8,128)(2,1)} %collective-permute-done.15.refs_0_), channel_id=1, source_target_pairs={{0,2},{1,7},{2,4},{3,1},{4,6},{5,3},{6,0},{7,5},{8,10},{9,15},{10,... | collective-permute-start | bytes 7839752 | tf_op jit(solution)/shard_map/ppermute | solution.py:157
  101.3 32.6 %collective-permute-start.19 = (bf16[336,3712]{1,0:T(8,128)(2,1)}, bf16[336,3712]{1,0:T(8,128)(2,1)S(1)}, u32[]{:S(2)}, u32[]{:S(2)}) collective-permute-start(bf16[336,3712]{1,0:T(8,128)(2,1)} %collective-permute-done.16.refs_1_), channel_id=1, source_target_pairs={{0,32},{1,97},{32,64},{33,1},{64,96},{65,33},{96,0},{97,65},{2,34}... | collective-permute-start | bytes 7483400 | tf_op jit(solution)/shard_map/ppermute | solution.py:157
  102.0 32.0 %collective-permute-start.20 = (bf16[336,3712]{1,0:T(8,128)(2,1)}, bf16[336,3712]{1,0:T(8,128)(2,1)}, u32[]{:S(2)}, u32[]{:S(2)}) collective-permute-start(bf16[336,3712]{1,0:T(8,128)(2,1)} %collective-permute-done.17.refs_2_), channel_id=1, source_target_pairs={{0,8},{1,25},{8,16},{9,1},{16,24},{17,9},{24,0},{25,17},{2,10},{3,... | collective-permute-start | bytes 7483400 | tf_op jit(solution)/shard_map/ppermute | solution.py:157
  135.4 33.9 %collective-permute-start.21 = (bf16[352,3712]{1,0:T(8,128)(2,1)S(1)}, bf16[352,3712]{1,0:T(8,128)(2,1)S(1)}, u32[]{:S(2)}, u32[]{:S(2)}) collective-permute-start(bf16[352,3712]{1,0:T(8,128)(2,1)S(1)} %collective-permute-done.18.refs_0_), channel_id=1, source_target_pairs={{0,2},{1,7},{2,4},{3,1},{4,6},{5,3},{6,0},{7,5},{8,10},{9,15},{10,... | collective-permute-start | bytes 7839752 | tf_op jit(solution)/shard_map/ppermute | solution.py:157
  136.1 33.2 %collective-permute-start.22 = (bf16[336,3712]{1,0:T(8,128)(2,1)}, bf16[336,3712]{1,0:T(8,128)(2,1)}, u32[]{:S(2)}, u32[]{:S(2)}) collective-permute-start(bf16[336,3712]{1,0:T(8,128)(2,1)} %copy-done.10), channel_id=1, source_target_pairs={{0,32},{1,97},{32,64},{33,1},{64,96},{65,33},{96,0},{97,65},{2,34}... | collective-permute-start | bytes 7483400 | tf_op jit(solution)/shard_map/ppermute | solution.py:157
  136.8 32.5 %collective-permute-start.23 = (bf16[336,3712]{1,0:T(8,128)(2,1)}, bf16[336,3712]{1,0:T(8,128)(2,1)}, u32[]{:S(2)}, u32[]{:S(2)}) collective-permute-start(bf16[336,3712]{1,0:T(8,128)(2,1)} %collective-permute-done.20.refs_2_), channel_id=1, source_target_pairs={{0,8},{1,25},{8,16},{9,1},{16,24},{17,9},{24,0},{25,17},{2,10},{3,... | collective-permute-start | bytes 7483400 | tf_op jit(solution)/shard_map/ppermute | solution.py:157
  189.2 22.5 %collective-permute-start.24 = (bf16[176,3584]{1,0:T(8,128)(2,1)}, bf16[176,3584]{1,0:T(8,128)(2,1)}, u32[]{:S(2)}, u32[]{:S(2)}) collective-permute-start(bf16[176,3584]{1,0:T(8,128)(2,1)} %get-tuple-element.107), channel_id=1, source_target_pairs={{0,6},{1,3},{2,0},{3,5},{4,2},{5,7},{6,4},{7,1},{8,14},{9,11},{10,... | collective-permute-start | bytes 3784712 | tf_op jit(solution)/shard_map/ppermute | solution.py:157
  190.7 20.9 %collective-permute-start.25 = (bf16[176,3584]{1,0:T(8,128)(2,1)S(1)}, bf16[176,3584]{1,0:T(8,128)(2,1)S(1)}, u32[]{:S(2)}, u32[]{:S(2)}) collective-permute-start(bf16[176,3584]{1,0:T(8,128)(2,1)S(1)} %get-tuple-element.108), channel_id=1, source_target_pairs={{0,96},{1,33},{32,0},{33,65},{64,32},{65,97},{96,64},{97,1},{2,98}... | collective-permute-start | bytes 3784712 | tf_op jit(solution)/shard_map/ppermute | solution.py:157
  192.6 19.0 %collective-permute-start.26 = (bf16[176,3584]{1,0:T(8,128)(2,1)S(1)}, bf16[176,3584]{1,0:T(8,128)(2,1)}, u32[]{:S(2)}, u32[]{:S(2)}) collective-permute-start(bf16[176,3584]{1,0:T(8,128)(2,1)S(1)} %get-tuple-element.109), channel_id=1, source_target_pairs={{0,24},{1,9},{8,0},{9,17},{16,8},{17,25},{24,16},{25,1},{2,26},{3,... | collective-permute-start | bytes 3784712 | tf_op jit(solution)/shard_map/ppermute | solution.py:157
  211.7 17.4 %collective-permute-start.27 = (bf16[176,3584]{1,0:T(8,128)(2,1)S(1)}, bf16[176,3584]{1,0:T(8,128)(2,1)S(1)}, u32[]{:S(2)}, u32[]{:S(2)}) collective-permute-start(bf16[176,3584]{1,0:T(8,128)(2,1)S(1)} %get-tuple-element.114), channel_id=1, source_target_pairs={{0,6},{1,3},{2,0},{3,5},{4,2},{5,7},{6,4},{7,1},{8,14},{9,11},{10,... | collective-permute-start | bytes 3784712 | tf_op jit(solution)/shard_map/ppermute | solution.py:157
  212.3 15.9 %collective-permute-start.28 = (bf16[160,3584]{1,0:T(8,128)(2,1)S(1)}, bf16[160,3584]{1,0:T(8,128)(2,1)S(1)}, u32[]{:S(2)}, u32[]{:S(2)}) collective-permute-start(bf16[160,3584]{1,0:T(8,128)(2,1)S(1)} %get-tuple-element.115), channel_id=1, source_target_pairs={{0,96},{1,33},{32,0},{33,65},{64,32},{65,97},{96,64},{97,1},{2,98}... | collective-permute-start | bytes 3440648 | tf_op jit(solution)/shard_map/ppermute | solution.py:157
  213.2 15.9 %collective-permute-start.29 = (bf16[160,3584]{1,0:T(8,128)(2,1)S(1)}, bf16[160,3584]{1,0:T(8,128)(2,1)S(1)}, u32[]{:S(2)}, u32[]{:S(2)}) collective-permute-start(bf16[160,3584]{1,0:T(8,128)(2,1)S(1)} %get-tuple-element.116), channel_id=1, source_target_pairs={{0,24},{1,9},{8,0},{9,17},{16,8},{17,25},{24,16},{25,1},{2,26},{3,... | collective-permute-start | bytes 3440648 | tf_op jit(solution)/shard_map/ppermute | solution.py:157
  231.7 29.7 %collective-permute-start.32 = (bf16[336,3584]{1,0:T(8,128)(2,1)S(1)}, bf16[336,3584]{1,0:T(8,128)(2,1)S(1)}, u32[]{:S(2)}, u32[]{:S(2)}) collective-permute-start(bf16[336,3584]{1,0:T(8,128)(2,1)S(1)} %add_convert_fusion.7), channel_id=1, source_target_pairs={{0,24},{1,9},{8,0},{9,17},{16,8},{17,25},{24,16},{25,1},{2,26},{3,... | collective-permute-start | bytes 7225352 | tf_op jit(solution)/shard_map/ppermute | solution.py:157
  236.4 31.1 %collective-permute-start.30 = (bf16[352,3584]{1,0:T(8,128)(2,1)S(1)}, bf16[352,3584]{1,0:T(8,128)(2,1)S(1)}, u32[]{:S(2)}, u32[]{:S(2)}) collective-permute-start(bf16[352,3584]{1,0:T(8,128)(2,1)S(1)} %add_convert_fusion.2), channel_id=1, source_target_pairs={{0,6},{1,3},{2,0},{3,5},{4,2},{5,7},{6,4},{7,1},{8,14},{9,11},{10,... | collective-permute-start | bytes 7569416 | tf_op jit(solution)/shard_map/ppermute | solution.py:157
  238.0 29.4 %collective-permute-start.31 = (bf16[336,3584]{1,0:T(8,128)(2,1)S(1)}, bf16[336,3584]{1,0:T(8,128)(2,1)S(1)}, u32[]{:S(2)}, u32[]{:S(2)}) collective-permute-start(bf16[336,3584]{1,0:T(8,128)(2,1)S(1)} %add_convert_fusion.8), channel_id=1, source_target_pairs={{0,96},{1,33},{32,0},{33,65},{64,32},{65,97},{96,64},{97,1},{2,98}... | collective-permute-start | bytes 7225352 | tf_op jit(solution)/shard_map/ppermute | solution.py:157
  268.1 34.3 %collective-permute-start.35 = (bf16[336,3584]{1,0:T(8,128)(2,1)S(1)}, bf16[336,3584]{1,0:T(8,128)(2,1)S(1)}, u32[]{:S(2)}, u32[]{:S(2)}) collective-permute-start(bf16[336,3584]{1,0:T(8,128)(2,1)S(1)} %add_convert_fusion.5), channel_id=1, source_target_pairs={{0,24},{1,9},{8,0},{9,17},{16,8},{17,25},{24,16},{25,1},{2,26},{3,... | collective-permute-start | bytes 7225352 | tf_op jit(solution)/shard_map/ppermute | solution.py:157
  269.5 41.0 %collective-permute-start.33 = (bf16[352,3584]{1,0:T(8,128)(2,1)S(1)}, bf16[352,3584]{1,0:T(8,128)(2,1)S(1)}, u32[]{:S(2)}, u32[]{:S(2)}) collective-permute-start(bf16[352,3584]{1,0:T(8,128)(2,1)S(1)} %add_convert_fusion.1), channel_id=1, source_target_pairs={{0,6},{1,3},{2,0},{3,5},{4,2},{5,7},{6,4},{7,1},{8,14},{9,11},{10,... | collective-permute-start | bytes 7569416 | tf_op jit(solution)/shard_map/ppermute | solution.py:157
  271.2 39.2 %collective-permute-start.34 = (bf16[336,3584]{1,0:T(8,128)(2,1)S(1)}, bf16[336,3584]{1,0:T(8,128)(2,1)S(1)}, u32[]{:S(2)}, u32[]{:S(2)}) collective-permute-start(bf16[336,3584]{1,0:T(8,128)(2,1)S(1)} %add_convert_fusion.6), channel_id=1, source_target_pairs={{0,96},{1,33},{32,0},{33,65},{64,32},{65,97},{96,64},{97,1},{2,98}... | collective-permute-start | bytes 7225352 | tf_op jit(solution)/shard_map/ppermute | solution.py:157
  311.1 24.5 %collective-permute-start.38 = (bf16[168,3584]{1,0:T(8,128)(2,1)S(1)}, bf16[168,3584]{1,0:T(8,128)(2,1)S(1)}, u32[]{:S(2)}, u32[]{:S(2)}) collective-permute-start(bf16[168,3584]{1,0:T(8,128)(2,1)S(1)} %split.99), channel_id=1, source_target_pairs={{0,96},{1,33},{32,64},{33,1},{64,32},{65,97},{96,0},{97,65},{2,98}... | collective-permute-start | bytes 3612680 | tf_op jit(solution)/shard_map/ppermute | solution.py:166
  315.1 24.7 %collective-permute-start.36 = (bf16[176,3584]{1,0:T(8,128)(2,1)S(1)}, bf16[176,3584]{1,0:T(8,128)(2,1)S(1)}, u32[]{:S(2)}, u32[]{:S(2)}) collective-permute-start(bf16[176,3584]{1,0:T(8,128)(2,1)S(1)} %split.97), channel_id=1, source_target_pairs={{0,24},{1,9},{8,16},{9,1},{16,8},{17,25},{24,0},{25,17},{2,26},{3,... | collective-permute-start | bytes 3784712 | tf_op jit(solution)/shard_map/ppermute | solution.py:166
  315.9 23.3 %collective-permute-start.37 = (bf16[168,3584]{1,0:T(8,128)(2,1)S(1)}, bf16[168,3584]{1,0:T(8,128)(2,1)S(1)}, u32[]{:S(2)}, u32[]{:S(2)}) collective-permute-start(bf16[168,3584]{1,0:T(8,128)(2,1)S(1)} %split.98), channel_id=1, source_target_pairs={{0,6},{1,3},{2,4},{3,1},{4,2},{5,7},{6,0},{7,5},{8,14},{9,11},{10,... | collective-permute-start | bytes 3612680 | tf_op jit(solution)/shard_map/ppermute | solution.py:166
  340.3 10.4 %collective-permute-start.41 = (bf16[84,3584]{1,0:T(8,128)(2,1)S(1)}, bf16[84,3584]{1,0:T(8,128)(2,1)S(1)}, u32[]{:S(2)}, u32[]{:S(2)}) collective-permute-start(bf16[84,3584]{1,0:T(8,128)(2,1)S(1)} %split.105), channel_id=1, source_target_pairs={{0,32},{1,97},{32,0},{33,65},{64,96},{65,33},{96,64},{97,1},{2,34}... | collective-permute-start | bytes 1806344 | tf_op jit(solution)/shard_map/ppermute | solution.py:166
  341.7 12.7 %collective-permute-start.39 = (bf16[88,3584]{1,0:T(8,128)(2,1)S(1)}, bf16[88,3584]{1,0:T(8,128)(2,1)S(1)}, u32[]{:S(2)}, u32[]{:S(2)}) collective-permute-start(bf16[88,3584]{1,0:T(8,128)(2,1)S(1)} %split.101), channel_id=1, source_target_pairs={{0,8},{1,25},{8,0},{9,17},{16,24},{17,9},{24,16},{25,1},{2,10},{3,... | collective-permute-start | bytes 1892360 | tf_op jit(solution)/shard_map/ppermute | solution.py:166
  343.3 11.0 %collective-permute-start.40 = (bf16[84,3584]{1,0:T(8,128)(2,1)S(1)}, bf16[84,3584]{1,0:T(8,128)(2,1)S(1)}, u32[]{:S(2)}, u32[]{:S(2)}) collective-permute-start(bf16[84,3584]{1,0:T(8,128)(2,1)S(1)} %split.103), channel_id=1, source_target_pairs={{0,2},{1,7},{2,0},{3,5},{4,6},{5,3},{6,4},{7,1},{8,10},{9,15},{10,... | collective-permute-start | bytes 1806344 | tf_op jit(solution)/shard_map/ppermute | solution.py:166
  354.6 7.3 %collective-permute-start.44 = (bf16[42,3584]{1,0:T(8,128)(2,1)S(1)}, bf16[42,3584]{1,0:T(8,128)(2,1)S(1)}, u32[]{:S(2)}, u32[]{:S(2)}) collective-permute-start(bf16[42,3584]{1,0:T(8,128)(2,1)S(1)} %split.111), channel_id=1, source_target_pairs={{0,6},{1,3},{2,4},{3,1},{4,2},{5,7},{6,0},{7,5},{8,14},{9,11},{10,... | collective-permute-start | bytes 903176 | tf_op jit(solution)/shard_map/ppermute | solution.py:166
  354.9 9.8 %collective-permute-start.42 = (bf16[44,3584]{1,0:T(8,128)(2,1)S(1)}, bf16[44,3584]{1,0:T(8,128)(2,1)S(1)}, u32[]{:S(2)}, u32[]{:S(2)}) collective-permute-start(bf16[44,3584]{1,0:T(8,128)(2,1)S(1)} %split.107), channel_id=1, source_target_pairs={{0,96},{1,33},{32,64},{33,1},{64,32},{65,97},{96,0},{97,65},{2,98}... | collective-permute-start | bytes 946184 | tf_op jit(solution)/shard_map/ppermute | solution.py:166
  356.2 8.5 %collective-permute-start.43 = (bf16[42,3584]{1,0:T(8,128)(2,1)S(1)}, bf16[42,3584]{1,0:T(8,128)(2,1)S(1)}, u32[]{:S(2)}, u32[]{:S(2)}) collective-permute-start(bf16[42,3584]{1,0:T(8,128)(2,1)S(1)} %split.109), channel_id=1, source_target_pairs={{0,24},{1,9},{8,16},{9,1},{16,8},{17,25},{24,0},{25,17},{2,26},{3,... | collective-permute-start | bytes 903176 | tf_op jit(solution)/shard_map/ppermute | solution.py:166
  364.9 5.8 %collective-permute-start.47 = (bf16[21,3584]{1,0:T(8,128)(2,1)S(1)}, bf16[21,3584]{1,0:T(8,128)(2,1)S(1)}, u32[]{:S(2)}, u32[]{:S(2)}) collective-permute-start(bf16[21,3584]{1,0:T(8,128)(2,1)S(1)} %split.117), channel_id=1, source_target_pairs={{0,2},{1,7},{2,0},{3,5},{4,6},{5,3},{6,4},{7,1},{8,10},{9,15},{10,... | collective-permute-start | bytes 451592 | tf_op jit(solution)/shard_map/ppermute | solution.py:166
  367.4 7.1 %collective-permute-start.45 = (bf16[22,3584]{1,0:T(8,128)(2,1)S(1)}, bf16[22,3584]{1,0:T(8,128)(2,1)S(1)}, u32[]{:S(2)}, u32[]{:S(2)}) collective-permute-start(bf16[22,3584]{1,0:T(8,128)(2,1)S(1)} %split.113), channel_id=1, source_target_pairs={{0,32},{1,97},{32,0},{33,65},{64,96},{65,33},{96,64},{97,1},{2,34}... | collective-permute-start | bytes 473096 | tf_op jit(solution)/shard_map/ppermute | solution.py:166
  369.0 5.5 %collective-permute-start.46 = (bf16[21,3584]{1,0:T(8,128)(2,1)S(1)}, bf16[21,3584]{1,0:T(8,128)(2,1)S(1)}, u32[]{:S(2)}, u32[]{:S(2)}) collective-permute-start(bf16[21,3584]{1,0:T(8,128)(2,1)S(1)} %split.115), channel_id=1, source_target_pairs={{0,8},{1,25},{8,0},{9,17},{16,24},{17,9},{24,16},{25,1},{2,10},{3,... | collective-permute-start | bytes 451592 | tf_op jit(solution)/shard_map/ppermute | solution.py:166
  (11 other events, 140.9 us)

commit v5 on v4

--- a/solution.py
+++ b/solution.py
@@ -176,12 +176,12 @@
     return (one.astype(jnp.float32) + other.astype(jnp.float32)).astype(one.dtype)
 
 
-def halve(totals, axes):
+def halve(totals, axes, hold):
     for first in (False, True):
         halves = [jnp.split(total, 2) for total in totals]
-        arrived = lax.optimization_barrier(
-            [meet(a, lax.axis_size(a), first)(sent) for a, (_, sent) in zip(axes, halves)]
-        )
+        arrived = [meet(a, lax.axis_size(a), first)(sent) for a, (_, sent) in zip(axes, halves)]
+        if hold:
+            arrived = lax.optimization_barrier(arrived)
         totals = [add(kept, other) for (kept, _), other in zip(halves, arrived)]
     return totals
 
@@ -229,7 +229,7 @@
             arrived = lax.optimization_barrier([back(t) for back, t in zip(backs, totals)])
         totals, arrived = [add(*pair) for pair in zip(arrived, pieces)], None
     for phase in (1, 0):
-        totals = halve(totals, [order[phase] for order in ORDERS])
+        totals = halve(totals, [order[phase] for order in ORDERS], phase == 1)
     return jnp.concatenate(totals, axis=0)
 
 

time: 382 us -> 382 us (level)
    convert_element_type x20 -> x21, other arithmetic: 10.4 us -> 10.4 us  [add(): (one.astype(jnp.float32) + other.astype(jnp.float32)).astype(one.dtype)]
where the time goes in v5:
time: 382 us; the launch traced here: 376 us
  waiting for transfers between devices  153 us (40%)
  Pallas kernels  128 us (34%)
  starting transfers between devices  71.6 us (19%)
  other arithmetic  16.1 us (4%)
  local copies, waits for them, and re-layouts  7.15 us (2%)
    pallas_call x5, Pallas kernels, ffn(): pl.pallas_call(functools.partial(ffn_kernel, experts, offsets, counts), i...  127 us
    ppermute x21, waiting for transfers between devices, ring(): return lambda block: lax.ppermute(block, (axis, 'core'), pairs)  78.6 us
    ppermute x24, waiting for transfers between devices, meet(): return lambda block: lax.ppermute(block, (axis, 'core'), pairs)  74.1 us
    ppermute x24, starting transfers between devices, meet(): return lambda block: lax.ppermute(block, (axis, 'core'), pairs)  39.9 us
    ppermute x21, starting transfers between devices, ring(): return lambda block: lax.ppermute(block, (axis, 'core'), pairs)  31.2 us
    convert_element_type x21, other arithmetic, add(): (one.astype(jnp.float32) + other.astype(jnp.float32)).astype(one.dtype)  10.4 us
  transfers between devices with their start and end apart: 48, of which 25 were waited for; matrix products, arithmetic and copies ran while one was open for 3% of the time, Pallas kernels for 29%

profile of v5, /device:TPU:32, one launch (start us, length us, event | category | flops | bytes accessed | tf_op | source)
XLA Modules:
  0.0 376.2 jit_solution(5029979572047017562)
XLA Ops:
  4.9 1.7 collective-permute-start.2
  6.5 3.8 %collective-permute-done.4 = bf16[21,3712]{1,0:T(8,128)(2,1)S(1)} collective-permute-done((bf16[21,3712]{1,0:T(8,128)(2,1)S(1)}, bf16[21,3712]{1,0:T(8,128)(2,1)S(1)}, u32[]{:S(2)}, u32[]{:S(2)}) %collective-permute-start.4) | collective-permute-done | bytes 155936 | tf_op jit(solution)/shard_map/ppermute | solution.py:166
  11.9 2.0 collective-permute-start.5
  13.9 1.8 collective-permute-done
  15.8 3.0 collective-permute-start.3
  19.3 2.6 collective-permute-start.1
  22.1 2.2 collective-permute-done.3
  24.5 3.4 collective-permute-done.1
  28.3 2.1 collective-permute-start.11
  32.0 6.8 %collective-permute-done.13 = bf16[84,3712]{1,0:T(8,128)(2,1)S(1)} collective-permute-done((bf16[84,3712]{1,0:T(8,128)(2,1)S(1)}, bf16[84,3712]{1,0:T(8,128)(2,1)S(1)}, u32[]{:S(2)}, u32[]{:S(2)}) %collective-permute-start.13) | collective-permute-done | bytes 623648 | tf_op jit(solution)/shard_map/ppermute | solution.py:166
  38.9 2.7 collective-permute-start.14
  41.8 2.9 collective-permute-start.12
  44.8 3.1 collective-permute-start.10
  47.9 9.3 %collective-permute-done.14 = bf16[168,3712]{1,0:T(8,128)(2,1)S(1)} collective-permute-done((bf16[168,3712]{1,0:T(8,128)(2,1)S(1)}, bf16[168,3712]{1,0:T(8,128)(2,1)S(1)}, u32[]{:S(2)}, u32[]{:S(2)}) %collective-permute-start.14) | collective-permute-done | bytes 1247264 | tf_op jit(solution)/shard_map/ppermute | solution.py:166
  57.2 1.7 pad_maximum_fusion.2.refs_2_
  59.6 1.7 pad_maximum_fusion.1.refs_1_
  61.3 2.4 collective-permute-done.10
  65.7 30.6 %shard_map.74 = (bf16[352,3584]{1,0:T(8,128)(2,1)}, bf16[336,3584]{1,0:T(8,128)(2,1)S(1)}, bf16[336,3584]{1,0:T(8,128)(2,1)}) custom-call(s32[2]{0:T(128)S(1)} %pad_add_fusion.ids, bf16[352,3712]{1,0:T(8,128)(2,1)} %copy-done.2, bf16[336,3712]{1,0:T(8,128)(2,1)} %pad_maximum_fusion.1.refs_1_, bf16[336,3712]{1,0:T(8,128)(2,1)} %pad_maximum_fusion.2.refs_2_, ...), custom_call_target="tpu_custom_call" | custom-call | flops 22548578304 | bytes 36700160 | tf_op jit(solution)/shard_map/pallas_call | solution.py:128
  96.9 4.5 %collective-permute-start.18 = (bf16[352,3712]{1,0:T(8,128)(2,1)}, bf16[352,3712]{1,0:T(8,128)(2,1)S(1)}, u32[]{:S(2)}, u32[]{:S(2)}) collective-permute-start(bf16[352,3712]{1,0:T(8,128)(2,1)} %collective-permute-done.15.refs_0_), channel_id=1, source_target_pairs={{0,2},{1,7},{2,4},{3,1},{4,6},{5,3},{6,0},{7,5},{8,10},{9,15},{10,... | collective-permute-start | bytes 7839752 | tf_op jit(solution)/shard_map/ppermute | solution.py:157
  102.0 1.7 collective-permute-start.20
  103.7 30.3 %shard_map.75 = (bf16[352,3584]{1,0:T(8,128)(2,1)}, bf16[336,3584]{1,0:T(8,128)(2,1)S(1)}, bf16[336,3584]{1,0:T(8,128)(2,1)}) custom-call(s32[2]{0:T(128)S(1)} %pad_add_fusion.ids, bf16[352,3712]{1,0:T(8,128)(2,1)} %collective-permute-done.15.refs_0_, bf16[336,3712]{1,0:T(8,128)(2,1)} %collective-permute-done.16.refs_1_, ...), custom_call_target="tpu_custom_call" | custom-call | flops 22548578304 | bytes 36700160 | tf_op jit(solution)/shard_map/pallas_call | solution.py:128
  136.9 2.0 collective-permute-start.23
  138.8 30.5 %shard_map.76 = (bf16[352,3584]{1,0:T(8,128)(2,1)}, bf16[336,3584]{1,0:T(8,128)(2,1)S(1)}, bf16[336,3584]{1,0:T(8,128)(2,1)}) custom-call(s32[2]{0:T(128)S(1)} %pad_add_fusion.ids, bf16[352,3712]{1,0:T(8,128)(2,1)} %copy-done.9, bf16[336,3712]{1,0:T(8,128)(2,1)} %copy-done.10, bf16[336,3712]{1,0:T(8,128)(2,1)} %collective-permute-done.20.refs_2_, ...), custom_call_target="tpu_custom_call" | custom-call | flops 22548578304 | bytes 36700160 | tf_op jit(solution)/shard_map/pallas_call | solution.py:128
  170.8 18.4 %shard_map.77 = (bf16[176,3584]{1,0:T(8,128)(2,1)}, bf16[176,3584]{1,0:T(8,128)(2,1)S(1)}, bf16[176,3584]{1,0:T(8,128)(2,1)S(1)}) custom-call(s32[2]{0:T(128)S(1)} %pad_add_fusion.ids, bf16[352,3712]{1,0:T(8,128)(2,1)} %copy-done.8, bf16[336,3712]{1,0:T(8,128)(2,1)} %collective-permute-done.22.refs_1_, bf16[336,3712]{1,0:T(8,128)(2,1)} %collective-permute-done.23.refs_2_, ...), custom_call_target="tpu_custom_call" | custom-call | flops 11626610688 | bytes 29589504 | tf_op jit(solution)/shard_map/pallas_call | solution.py:128
  190.8 1.9 collective-permute-start.25
  192.7 2.0 collective-permute-start.26
  194.7 17.1 %shard_map.78 = (bf16[176,3584]{1,0:T(8,128)(2,1)S(1)}, bf16[160,3584]{1,0:T(8,128)(2,1)S(1)}, bf16[160,3584]{1,0:T(8,128)(2,1)S(1)}) custom-call(s32[2]{0:T(128)S(1)} %pad_add_fusion.ids, bf16[352,3712]{1,0:T(8,128)(2,1)} %copy-done.8, bf16[336,3712]{1,0:T(8,128)(2,1)} %collective-permute-done.22.refs_1_, ...), custom_call_target="tpu_custom_call" | custom-call | flops 10921967616 | bytes 29130752 | tf_op jit(solution)/shard_map/pallas_call | solution.py:128
  214.6 13.7 %collective-permute-done.28 = bf16[160,3584]{1,0:T(8,128)(2,1)S(1)} collective-permute-done((bf16[160,3584]{1,0:T(8,128)(2,1)S(1)}, bf16[160,3584]{1,0:T(8,128)(2,1)S(1)}, u32[]{:S(2)}, u32[]{:S(2)}) %collective-permute-start.28) | collective-permute-done | bytes 1146912 | tf_op jit(solution)/shard_map/ppermute | solution.py:157
  229.2 2.6 add_convert_fusion.7
  231.8 2.7 collective-permute-start.32
  234.5 1.9 add_convert_fusion.2
  238.1 1.9 collective-permute-start.31
  240.0 21.4 %collective-permute-done.32 = bf16[336,3584]{1,0:T(8,128)(2,1)S(1)} collective-permute-done((bf16[336,3584]{1,0:T(8,128)(2,1)S(1)}, bf16[336,3584]{1,0:T(8,128)(2,1)S(1)}, u32[]{:S(2)}, u32[]{:S(2)}) %collective-permute-start.32) | collective-permute-done | bytes 2408480 | tf_op jit(solution)/shard_map/ppermute | solution.py:157
  261.4 6.1 %collective-permute-done.31 = bf16[336,3584]{1,0:T(8,128)(2,1)S(1)} collective-permute-done((bf16[336,3584]{1,0:T(8,128)(2,1)S(1)}, bf16[336,3584]{1,0:T(8,128)(2,1)S(1)}, u32[]{:S(2)}, u32[]{:S(2)}) %collective-permute-start.31) | collective-permute-done | bytes 2408480 | tf_op jit(solution)/shard_map/ppermute | solution.py:157
  271.3 3.3 collective-permute-start.34
  274.6 27.9 %collective-permute-done.35 = bf16[336,3584]{1,0:T(8,128)(2,1)S(1)} collective-permute-done((bf16[336,3584]{1,0:T(8,128)(2,1)S(1)}, bf16[336,3584]{1,0:T(8,128)(2,1)S(1)}, u32[]{:S(2)}, u32[]{:S(2)}) %collective-permute-start.35) | collective-permute-done | bytes 2408480 | tf_op jit(solution)/shard_map/ppermute | solution.py:157
  302.5 8.1 %collective-permute-done.34 = bf16[336,3584]{1,0:T(8,128)(2,1)S(1)} collective-permute-done((bf16[336,3584]{1,0:T(8,128)(2,1)S(1)}, bf16[336,3584]{1,0:T(8,128)(2,1)S(1)}, u32[]{:S(2)}, u32[]{:S(2)}) %collective-permute-start.34) | collective-permute-done | bytes 2408480 | tf_op jit(solution)/shard_map/ppermute | solution.py:157
  311.2 3.3 collective-permute-start.38
  316.1 19.6 %collective-permute-done.38 = bf16[168,3584]{1,0:T(8,128)(2,1)S(1)} collective-permute-done((bf16[168,3584]{1,0:T(8,128)(2,1)S(1)}, bf16[168,3584]{1,0:T(8,128)(2,1)S(1)}, u32[]{:S(2)}, u32[]{:S(2)}) %collective-permute-start.38) | collective-permute-done | bytes 1204256 | tf_op jit(solution)/shard_map/ppermute | solution.py:166
  335.7 3.6 collective-permute-done.37
  343.4 2.8 collective-permute-start.40
  346.1 4.6 %collective-permute-done.41 = bf16[84,3584]{1,0:T(8,128)(2,1)S(1)} collective-permute-done((bf16[84,3584]{1,0:T(8,128)(2,1)S(1)}, bf16[84,3584]{1,0:T(8,128)(2,1)S(1)}, u32[]{:S(2)}, u32[]{:S(2)}) %collective-permute-start.41) | collective-permute-done | bytes 602144 | tf_op jit(solution)/shard_map/ppermute | solution.py:166
  350.7 3.7 collective-permute-done.40
  355.9 2.4 collective-permute-start.44
  358.7 5.8 %collective-permute-done.44 = bf16[42,3584]{1,0:T(8,128)(2,1)S(1)} collective-permute-done((bf16[42,3584]{1,0:T(8,128)(2,1)S(1)}, bf16[42,3584]{1,0:T(8,128)(2,1)S(1)}, u32[]{:S(2)}, u32[]{:S(2)}) %collective-permute-start.44) | collective-permute-done | bytes 301088 | tf_op jit(solution)/shard_map/ppermute | solution.py:166
  366.0 3.3 collective-permute-start.47
  370.8 2.0 collective-permute-done.47
  372.8 2.2 collective-permute-done.43
  (127 shorter events, 40.6 us)
Async XLA Ops:
  0.0 28.1 %collective-permute-start.6 = (bf16[3584,512]{1,0:T(8,128)(2,1)}, bf16[3584,512]{1,0:T(8,128)(2,1)}, u32[]{:S(2)}, u32[]{:S(2)}) collective-permute-start(bf16[3584,512]{1,0:T(8,128)(2,1)} %bitcast.5), channel_id=1, source_target_pairs={{0,1},{1,0},{2,3},{3,2},{4,5},{5,4},{6,7},{7,6},{8,9},{9,8},{10,11... | collective-permute-start | bytes 11010056 | tf_op jit(solution)/shard_map/ppermute | solution.py:197
  0.0 28.1 %collective-permute-start.7 = (bf16[3584,512]{1,0:T(8,128)(2,1)}, bf16[3584,512]{1,0:T(8,128)(2,1)}, u32[]{:S(2)}, u32[]{:S(2)}) collective-permute-start(bf16[3584,512]{1,0:T(8,128)(2,1)} %bitcast.11), channel_id=1, source_target_pairs={{0,1},{1,0},{2,3},{3,2},{4,5},{5,4},{6,7},{7,6},{8,9},{9,8},{10,11... | collective-permute-start | bytes 11010056 | tf_op jit(solution)/shard_map/ppermute | solution.py:197
  0.5 27.6 %collective-permute-start.8 = (bf16[512,3584]{1,0:T(8,128)(2,1)}, bf16[512,3584]{1,0:T(8,128)(2,1)}, u32[]{:S(2)}, u32[]{:S(2)}) collective-permute-start(bf16[512,3584]{1,0:T(8,128)(2,1)} %bitcast.17), channel_id=1, source_target_pairs={{0,1},{1,0},{2,3},{3,2},{4,5},{5,4},{6,7},{7,6},{8,9},{9,8},{10,11... | collective-permute-start | bytes 11010056 | tf_op jit(solution)/shard_map/ppermute | solution.py:197
  4.7 5.6 %collective-permute-start.4 = (bf16[21,3712]{1,0:T(8,128)(2,1)S(1)}, bf16[21,3712]{1,0:T(8,128)(2,1)S(1)}, u32[]{:S(2)}, u32[]{:S(2)}) collective-permute-start(bf16[21,3712]{1,0:T(8,128)(2,1)S(1)} %get-tuple-element.137), channel_id=1, source_target_pairs={{0,2},{1,7},{2,0},{3,5},{4,6},{5,3},{6,4},{7,1},{8,10},{9,15},{10,... | collective-permute-start | bytes 467720 | tf_op jit(solution)/shard_map/ppermute | solution.py:166
  4.9 7.0 %collective-permute-start.2 = (bf16[21,3712]{1,0:T(8,128)(2,1)S(1)}, bf16[21,3712]{1,0:T(8,128)(2,1)S(1)}, u32[]{:S(2)}, u32[]{:S(2)}) collective-permute-start(bf16[21,3712]{1,0:T(8,128)(2,1)S(1)} %get-tuple-element.138), channel_id=1, source_target_pairs={{0,8},{1,25},{8,0},{9,17},{16,24},{17,9},{24,16},{25,1},{2,10},{3,... | collective-permute-start | bytes 467720 | tf_op jit(solution)/shard_map/ppermute | solution.py:166
  10.3 5.5 %collective-permute-start = (bf16[22,3712]{1,0:T(8,128)(2,1)S(1)}, bf16[22,3712]{1,0:T(8,128)(2,1)S(1)}, u32[]{:S(2)}, u32[]{:S(2)}) collective-permute-start(bf16[22,3712]{1,0:T(8,128)(2,1)S(1)} %slice.12), channel_id=1, source_target_pairs={{0,32},{1,97},{32,0},{33,65},{64,96},{65,33},{96,64},{97,1},{2,34}... | collective-permute-start | bytes 489992 | tf_op jit(solution)/shard_map/ppermute | solution.py:166
  11.9 7.5 %collective-permute-start.5 = (bf16[42,3712]{1,0:T(8,128)(2,1)S(1)}, bf16[42,3712]{1,0:T(8,128)(2,1)S(1)}, u32[]{:S(2)}, u32[]{:S(2)}) collective-permute-start(bf16[42,3712]{1,0:T(8,128)(2,1)S(1)} %pad_maximum_fusion.12), channel_id=1, source_target_pairs={{0,6},{1,3},{2,4},{3,1},{4,2},{5,7},{6,0},{7,5},{8,14},{9,11},{10,... | collective-permute-start | bytes 935432 | tf_op jit(solution)/shard_map/ppermute | solution.py:166
  15.8 8.6 %collective-permute-start.3 = (bf16[42,3712]{1,0:T(8,128)(2,1)S(1)}, bf16[42,3712]{1,0:T(8,128)(2,1)S(1)}, u32[]{:S(2)}, u32[]{:S(2)}) collective-permute-start(bf16[42,3712]{1,0:T(8,128)(2,1)S(1)} %pad_maximum_fusion.11), channel_id=1, source_target_pairs={{0,24},{1,9},{8,16},{9,1},{16,8},{17,25},{24,0},{25,17},{2,26},{3,... | collective-permute-start | bytes 935432 | tf_op jit(solution)/shard_map/ppermute | solution.py:166
  19.3 8.6 %collective-permute-start.1 = (bf16[44,3712]{1,0:T(8,128)(2,1)S(1)}, bf16[44,3712]{1,0:T(8,128)(2,1)S(1)}, u32[]{:S(2)}, u32[]{:S(2)}) collective-permute-start(bf16[44,3712]{1,0:T(8,128)(2,1)S(1)} %pad_maximum_fusion.10), channel_id=1, source_target_pairs={{0,96},{1,33},{32,64},{33,1},{64,32},{65,97},{96,0},{97,65},{2,98}... | collective-permute-start | bytes 979976 | tf_op jit(solution)/shard_map/ppermute | solution.py:166
  28.1 10.6 %collective-permute-start.13 = (bf16[84,3712]{1,0:T(8,128)(2,1)S(1)}, bf16[84,3712]{1,0:T(8,128)(2,1)S(1)}, u32[]{:S(2)}, u32[]{:S(2)}) collective-permute-start(bf16[84,3712]{1,0:T(8,128)(2,1)S(1)} %pad_maximum_fusion.8), channel_id=1, source_target_pairs={{0,32},{1,97},{32,0},{33,65},{64,96},{65,33},{96,64},{97,1},{2,34}... | collective-permute-start | bytes 1870856 | tf_op jit(solution)/shard_map/ppermute | solution.py:166
  28.3 13.3 %collective-permute-start.11 = (bf16[84,3712]{1,0:T(8,128)(2,1)S(1)}, bf16[84,3712]{1,0:T(8,128)(2,1)S(1)}, u32[]{:S(2)}, u32[]{:S(2)}) collective-permute-start(bf16[84,3712]{1,0:T(8,128)(2,1)S(1)} %pad_maximum_fusion.7), channel_id=1, source_target_pairs={{0,2},{1,7},{2,0},{3,5},{4,6},{5,3},{6,4},{7,1},{8,10},{9,15},{10,... | collective-permute-start | bytes 1870856 | tf_op jit(solution)/shard_map/ppermute | solution.py:166
  30.4 14.3 %collective-permute-start.9 = (bf16[88,3712]{1,0:T(8,128)(2,1)S(1)}, bf16[88,3712]{1,0:T(8,128)(2,1)S(1)}, u32[]{:S(2)}, u32[]{:S(2)}) collective-permute-start(bf16[88,3712]{1,0:T(8,128)(2,1)S(1)} %pad_maximum_fusion.6), channel_id=1, source_target_pairs={{0,8},{1,25},{8,0},{9,17},{16,24},{17,9},{24,16},{25,1},{2,10},{3,... | collective-permute-start | bytes 1959944 | tf_op jit(solution)/shard_map/ppermute | solution.py:166
  38.9 18.2 %collective-permute-start.14 = (bf16[168,3712]{1,0:T(8,128)(2,1)S(1)}, bf16[168,3712]{1,0:T(8,128)(2,1)S(1)}, u32[]{:S(2)}, u32[]{:S(2)}) collective-permute-start(bf16[168,3712]{1,0:T(8,128)(2,1)S(1)} %pad_maximum_fusion.5), channel_id=1, source_target_pairs={{0,96},{1,33},{32,64},{33,1},{64,32},{65,97},{96,0},{97,65},{2,98}... | collective-permute-start | bytes 3741704 | tf_op jit(solution)/shard_map/ppermute | solution.py:166
  41.8 17.8 %collective-permute-start.12 = (bf16[168,3712]{1,0:T(8,128)(2,1)S(1)}, bf16[168,3712]{1,0:T(8,128)(2,1)S(1)}, u32[]{:S(2)}, u32[]{:S(2)}) collective-permute-start(bf16[168,3712]{1,0:T(8,128)(2,1)S(1)} %pad_maximum_fusion.4), channel_id=1, source_target_pairs={{0,6},{1,3},{2,4},{3,1},{4,2},{5,7},{6,0},{7,5},{8,14},{9,11},{10,... | collective-permute-start | bytes 3741704 | tf_op jit(solution)/shard_map/ppermute | solution.py:166
  44.8 18.9 %collective-permute-start.10 = (bf16[176,3712]{1,0:T(8,128)(2,1)S(1)}, bf16[176,3712]{1,0:T(8,128)(2,1)S(1)}, u32[]{:S(2)}, u32[]{:S(2)}) collective-permute-start(bf16[176,3712]{1,0:T(8,128)(2,1)S(1)} %pad_maximum_fusion.3), channel_id=1, source_target_pairs={{0,24},{1,9},{8,16},{9,1},{16,8},{17,25},{24,0},{25,17},{2,26},{3,... | collective-permute-start | bytes 3919880 | tf_op jit(solution)/shard_map/ppermute | solution.py:166
  63.8 33.0 %collective-permute-start.15 = (bf16[352,3712]{1,0:T(8,128)(2,1)S(1)}, bf16[352,3712]{1,0:T(8,128)(2,1)}, u32[]{:S(2)}, u32[]{:S(2)}) collective-permute-start(bf16[352,3712]{1,0:T(8,128)(2,1)S(1)} %pad_maximum_fusion.refs_0_), channel_id=1, source_target_pairs={{0,2},{1,7},{2,4},{3,1},{4,6},{5,3},{6,0},{7,5},{8,10},{9,15},{10,... | collective-permute-start | bytes 7839752 | tf_op jit(solution)/shard_map/ppermute | solution.py:157
  63.9 32.4 %collective-permute-start.16 = (bf16[336,3712]{1,0:T(8,128)(2,1)}, bf16[336,3712]{1,0:T(8,128)(2,1)}, u32[]{:S(2)}, u32[]{:S(2)}) collective-permute-start(bf16[336,3712]{1,0:T(8,128)(2,1)} %pad_maximum_fusion.1.refs_1_), channel_id=1, source_target_pairs={{0,32},{1,97},{32,64},{33,1},{64,96},{65,33},{96,0},{97,65},{2,34}... | collective-permute-start | bytes 7483400 | tf_op jit(solution)/shard_map/ppermute | solution.py:157
  64.8 32.1 %collective-permute-start.17 = (bf16[336,3712]{1,0:T(8,128)(2,1)}, bf16[336,3712]{1,0:T(8,128)(2,1)}, u32[]{:S(2)}, u32[]{:S(2)}) collective-permute-start(bf16[336,3712]{1,0:T(8,128)(2,1)} %pad_maximum_fusion.2.refs_2_), channel_id=1, source_target_pairs={{0,8},{1,25},{8,16},{9,1},{16,24},{17,9},{24,0},{25,17},{2,10},{3,... | collective-permute-start | bytes 7483400 | tf_op jit(solution)/shard_map/ppermute | solution.py:157
  96.9 37.2 %collective-permute-start.18 = (bf16[352,3712]{1,0:T(8,128)(2,1)}, bf16[352,3712]{1,0:T(8,128)(2,1)S(1)}, u32[]{:S(2)}, u32[]{:S(2)}) collective-permute-start(bf16[352,3712]{1,0:T(8,128)(2,1)} %collective-permute-done.15.refs_0_), channel_id=1, source_target_pairs={{0,2},{1,7},{2,4},{3,1},{4,6},{5,3},{6,0},{7,5},{8,10},{9,15},{10,... | collective-permute-start | bytes 7839752 | tf_op jit(solution)/shard_map/ppermute | solution.py:157
  101.4 32.6 %collective-permute-start.19 = (bf16[336,3712]{1,0:T(8,128)(2,1)}, bf16[336,3712]{1,0:T(8,128)(2,1)S(1)}, u32[]{:S(2)}, u32[]{:S(2)}) collective-permute-start(bf16[336,3712]{1,0:T(8,128)(2,1)} %collective-permute-done.16.refs_1_), channel_id=1, source_target_pairs={{0,32},{1,97},{32,64},{33,1},{64,96},{65,33},{96,0},{97,65},{2,34}... | collective-permute-start | bytes 7483400 | tf_op jit(solution)/shard_map/ppermute | solution.py:157
  102.0 32.0 %collective-permute-start.20 = (bf16[336,3712]{1,0:T(8,128)(2,1)}, bf16[336,3712]{1,0:T(8,128)(2,1)}, u32[]{:S(2)}, u32[]{:S(2)}) collective-permute-start(bf16[336,3712]{1,0:T(8,128)(2,1)} %collective-permute-done.17.refs_2_), channel_id=1, source_target_pairs={{0,8},{1,25},{8,16},{9,1},{16,24},{17,9},{24,0},{25,17},{2,10},{3,... | collective-permute-start | bytes 7483400 | tf_op jit(solution)/shard_map/ppermute | solution.py:157
  135.4 33.9 %collective-permute-start.21 = (bf16[352,3712]{1,0:T(8,128)(2,1)S(1)}, bf16[352,3712]{1,0:T(8,128)(2,1)S(1)}, u32[]{:S(2)}, u32[]{:S(2)}) collective-permute-start(bf16[352,3712]{1,0:T(8,128)(2,1)S(1)} %collective-permute-done.18.refs_0_), channel_id=1, source_target_pairs={{0,2},{1,7},{2,4},{3,1},{4,6},{5,3},{6,0},{7,5},{8,10},{9,15},{10,... | collective-permute-start | bytes 7839752 | tf_op jit(solution)/shard_map/ppermute | solution.py:157
  136.2 33.2 %collective-permute-start.22 = (bf16[336,3712]{1,0:T(8,128)(2,1)}, bf16[336,3712]{1,0:T(8,128)(2,1)}, u32[]{:S(2)}, u32[]{:S(2)}) collective-permute-start(bf16[336,3712]{1,0:T(8,128)(2,1)} %copy-done.10), channel_id=1, source_target_pairs={{0,32},{1,97},{32,64},{33,1},{64,96},{65,33},{96,0},{97,65},{2,34}... | collective-permute-start | bytes 7483400 | tf_op jit(solution)/shard_map/ppermute | solution.py:157
  136.9 32.5 %collective-permute-start.23 = (bf16[336,3712]{1,0:T(8,128)(2,1)}, bf16[336,3712]{1,0:T(8,128)(2,1)}, u32[]{:S(2)}, u32[]{:S(2)}) collective-permute-start(bf16[336,3712]{1,0:T(8,128)(2,1)} %collective-permute-done.20.refs_2_), channel_id=1, source_target_pairs={{0,8},{1,25},{8,16},{9,1},{16,24},{17,9},{24,0},{25,17},{2,10},{3,... | collective-permute-start | bytes 7483400 | tf_op jit(solution)/shard_map/ppermute | solution.py:157
  189.2 22.5 %collective-permute-start.24 = (bf16[176,3584]{1,0:T(8,128)(2,1)}, bf16[176,3584]{1,0:T(8,128)(2,1)}, u32[]{:S(2)}, u32[]{:S(2)}) collective-permute-start(bf16[176,3584]{1,0:T(8,128)(2,1)} %get-tuple-element.101), channel_id=1, source_target_pairs={{0,6},{1,3},{2,0},{3,5},{4,2},{5,7},{6,4},{7,1},{8,14},{9,11},{10,... | collective-permute-start | bytes 3784712 | tf_op jit(solution)/shard_map/ppermute | solution.py:157
  190.8 20.9 %collective-permute-start.25 = (bf16[176,3584]{1,0:T(8,128)(2,1)S(1)}, bf16[176,3584]{1,0:T(8,128)(2,1)S(1)}, u32[]{:S(2)}, u32[]{:S(2)}) collective-permute-start(bf16[176,3584]{1,0:T(8,128)(2,1)S(1)} %get-tuple-element.102), channel_id=1, source_target_pairs={{0,96},{1,33},{32,0},{33,65},{64,32},{65,97},{96,64},{97,1},{2,98}... | collective-permute-start | bytes 3784712 | tf_op jit(solution)/shard_map/ppermute | solution.py:157
  192.7 19.0 %collective-permute-start.26 = (bf16[176,3584]{1,0:T(8,128)(2,1)S(1)}, bf16[176,3584]{1,0:T(8,128)(2,1)}, u32[]{:S(2)}, u32[]{:S(2)}) collective-permute-start(bf16[176,3584]{1,0:T(8,128)(2,1)S(1)} %get-tuple-element.103), channel_id=1, source_target_pairs={{0,24},{1,9},{8,0},{9,17},{16,8},{17,25},{24,16},{25,1},{2,26},{3,... | collective-permute-start | bytes 3784712 | tf_op jit(solution)/shard_map/ppermute | solution.py:157
  211.8 17.4 %collective-permute-start.27 = (bf16[176,3584]{1,0:T(8,128)(2,1)S(1)}, bf16[176,3584]{1,0:T(8,128)(2,1)S(1)}, u32[]{:S(2)}, u32[]{:S(2)}) collective-permute-start(bf16[176,3584]{1,0:T(8,128)(2,1)S(1)} %get-tuple-element.108), channel_id=1, source_target_pairs={{0,6},{1,3},{2,0},{3,5},{4,2},{5,7},{6,4},{7,1},{8,14},{9,11},{10,... | collective-permute-start | bytes 3784712 | tf_op jit(solution)/shard_map/ppermute | solution.py:157
  212.4 15.9 %collective-permute-start.28 = (bf16[160,3584]{1,0:T(8,128)(2,1)S(1)}, bf16[160,3584]{1,0:T(8,128)(2,1)S(1)}, u32[]{:S(2)}, u32[]{:S(2)}) collective-permute-start(bf16[160,3584]{1,0:T(8,128)(2,1)S(1)} %get-tuple-element.109), channel_id=1, source_target_pairs={{0,96},{1,33},{32,0},{33,65},{64,32},{65,97},{96,64},{97,1},{2,98}... | collective-permute-start | bytes 3440648 | tf_op jit(solution)/shard_map/ppermute | solution.py:157
  213.3 15.9 %collective-permute-start.29 = (bf16[160,3584]{1,0:T(8,128)(2,1)S(1)}, bf16[160,3584]{1,0:T(8,128)(2,1)S(1)}, u32[]{:S(2)}, u32[]{:S(2)}) collective-permute-start(bf16[160,3584]{1,0:T(8,128)(2,1)S(1)} %get-tuple-element.110), channel_id=1, source_target_pairs={{0,24},{1,9},{8,0},{9,17},{16,8},{17,25},{24,16},{25,1},{2,26},{3,... | collective-permute-start | bytes 3440648 | tf_op jit(solution)/shard_map/ppermute | solution.py:157
  231.8 29.7 %collective-permute-start.32 = (bf16[336,3584]{1,0:T(8,128)(2,1)S(1)}, bf16[336,3584]{1,0:T(8,128)(2,1)S(1)}, u32[]{:S(2)}, u32[]{:S(2)}) collective-permute-start(bf16[336,3584]{1,0:T(8,128)(2,1)S(1)} %add_convert_fusion.7), channel_id=1, source_target_pairs={{0,24},{1,9},{8,0},{9,17},{16,8},{17,25},{24,16},{25,1},{2,26},{3,... | collective-permute-start | bytes 7225352 | tf_op jit(solution)/shard_map/ppermute | solution.py:157
  236.4 31.1 %collective-permute-start.30 = (bf16[352,3584]{1,0:T(8,128)(2,1)S(1)}, bf16[352,3584]{1,0:T(8,128)(2,1)S(1)}, u32[]{:S(2)}, u32[]{:S(2)}) collective-permute-start(bf16[352,3584]{1,0:T(8,128)(2,1)S(1)} %add_convert_fusion.2), channel_id=1, source_target_pairs={{0,6},{1,3},{2,0},{3,5},{4,2},{5,7},{6,4},{7,1},{8,14},{9,11},{10,... | collective-permute-start | bytes 7569416 | tf_op jit(solution)/shard_map/ppermute | solution.py:157
  238.1 29.4 %collective-permute-start.31 = (bf16[336,3584]{1,0:T(8,128)(2,1)S(1)}, bf16[336,3584]{1,0:T(8,128)(2,1)S(1)}, u32[]{:S(2)}, u32[]{:S(2)}) collective-permute-start(bf16[336,3584]{1,0:T(8,128)(2,1)S(1)} %add_convert_fusion.8), channel_id=1, source_target_pairs={{0,96},{1,33},{32,0},{33,65},{64,32},{65,97},{96,64},{97,1},{2,98}... | collective-permute-start | bytes 7225352 | tf_op jit(solution)/shard_map/ppermute | solution.py:157
  268.2 34.3 %collective-permute-start.35 = (bf16[336,3584]{1,0:T(8,128)(2,1)S(1)}, bf16[336,3584]{1,0:T(8,128)(2,1)S(1)}, u32[]{:S(2)}, u32[]{:S(2)}) collective-permute-start(bf16[336,3584]{1,0:T(8,128)(2,1)S(1)} %add_convert_fusion.5), channel_id=1, source_target_pairs={{0,24},{1,9},{8,0},{9,17},{16,8},{17,25},{24,16},{25,1},{2,26},{3,... | collective-permute-start | bytes 7225352 | tf_op jit(solution)/shard_map/ppermute | solution.py:157
  269.5 41.0 %collective-permute-start.33 = (bf16[352,3584]{1,0:T(8,128)(2,1)S(1)}, bf16[352,3584]{1,0:T(8,128)(2,1)S(1)}, u32[]{:S(2)}, u32[]{:S(2)}) collective-permute-start(bf16[352,3584]{1,0:T(8,128)(2,1)S(1)} %add_convert_fusion.1), channel_id=1, source_target_pairs={{0,6},{1,3},{2,0},{3,5},{4,2},{5,7},{6,4},{7,1},{8,14},{9,11},{10,... | collective-permute-start | bytes 7569416 | tf_op jit(solution)/shard_map/ppermute | solution.py:157
  271.3 39.2 %collective-permute-start.34 = (bf16[336,3584]{1,0:T(8,128)(2,1)S(1)}, bf16[336,3584]{1,0:T(8,128)(2,1)S(1)}, u32[]{:S(2)}, u32[]{:S(2)}) collective-permute-start(bf16[336,3584]{1,0:T(8,128)(2,1)S(1)} %add_convert_fusion.6), channel_id=1, source_target_pairs={{0,96},{1,33},{32,0},{33,65},{64,32},{65,97},{96,64},{97,1},{2,98}... | collective-permute-start | bytes 7225352 | tf_op jit(solution)/shard_map/ppermute | solution.py:157
  311.2 24.5 %collective-permute-start.38 = (bf16[168,3584]{1,0:T(8,128)(2,1)S(1)}, bf16[168,3584]{1,0:T(8,128)(2,1)S(1)}, u32[]{:S(2)}, u32[]{:S(2)}) collective-permute-start(bf16[168,3584]{1,0:T(8,128)(2,1)S(1)} %split.99), channel_id=1, source_target_pairs={{0,96},{1,33},{32,64},{33,1},{64,32},{65,97},{96,0},{97,65},{2,98}... | collective-permute-start | bytes 3612680 | tf_op jit(solution)/shard_map/ppermute | solution.py:166
  315.2 24.7 %collective-permute-start.36 = (bf16[176,3584]{1,0:T(8,128)(2,1)S(1)}, bf16[176,3584]{1,0:T(8,128)(2,1)S(1)}, u32[]{:S(2)}, u32[]{:S(2)}) collective-permute-start(bf16[176,3584]{1,0:T(8,128)(2,1)S(1)} %split.97), channel_id=1, source_target_pairs={{0,24},{1,9},{8,16},{9,1},{16,8},{17,25},{24,0},{25,17},{2,26},{3,... | collective-permute-start | bytes 3784712 | tf_op jit(solution)/shard_map/ppermute | solution.py:166
  316.0 23.3 %collective-permute-start.37 = (bf16[168,3584]{1,0:T(8,128)(2,1)S(1)}, bf16[168,3584]{1,0:T(8,128)(2,1)S(1)}, u32[]{:S(2)}, u32[]{:S(2)}) collective-permute-start(bf16[168,3584]{1,0:T(8,128)(2,1)S(1)} %split.98), channel_id=1, source_target_pairs={{0,6},{1,3},{2,4},{3,1},{4,2},{5,7},{6,0},{7,5},{8,14},{9,11},{10,... | collective-permute-start | bytes 3612680 | tf_op jit(solution)/shard_map/ppermute | solution.py:166
  340.3 10.4 %collective-permute-start.41 = (bf16[84,3584]{1,0:T(8,128)(2,1)S(1)}, bf16[84,3584]{1,0:T(8,128)(2,1)S(1)}, u32[]{:S(2)}, u32[]{:S(2)}) collective-permute-start(bf16[84,3584]{1,0:T(8,128)(2,1)S(1)} %split.105), channel_id=1, source_target_pairs={{0,32},{1,97},{32,0},{33,65},{64,96},{65,33},{96,64},{97,1},{2,34}... | collective-permute-start | bytes 1806344 | tf_op jit(solution)/shard_map/ppermute | solution.py:166
  341.8 12.7 %collective-permute-start.39 = (bf16[88,3584]{1,0:T(8,128)(2,1)S(1)}, bf16[88,3584]{1,0:T(8,128)(2,1)S(1)}, u32[]{:S(2)}, u32[]{:S(2)}) collective-permute-start(bf16[88,3584]{1,0:T(8,128)(2,1)S(1)} %split.101), channel_id=1, source_target_pairs={{0,8},{1,25},{8,0},{9,17},{16,24},{17,9},{24,16},{25,1},{2,10},{3,... | collective-permute-start | bytes 1892360 | tf_op jit(solution)/shard_map/ppermute | solution.py:166
  343.4 11.1 %collective-permute-start.40 = (bf16[84,3584]{1,0:T(8,128)(2,1)S(1)}, bf16[84,3584]{1,0:T(8,128)(2,1)S(1)}, u32[]{:S(2)}, u32[]{:S(2)}) collective-permute-start(bf16[84,3584]{1,0:T(8,128)(2,1)S(1)} %split.103), channel_id=1, source_target_pairs={{0,2},{1,7},{2,0},{3,5},{4,6},{5,3},{6,4},{7,1},{8,10},{9,15},{10,... | collective-permute-start | bytes 1806344 | tf_op jit(solution)/shard_map/ppermute | solution.py:166
  354.7 14.7 %collective-permute-start.42 = (bf16[44,3584]{1,0:T(8,128)(2,1)S(1)}, bf16[44,3584]{1,0:T(8,128)(2,1)S(1)}, u32[]{:S(2)}, u32[]{:S(2)}) collective-permute-start(bf16[44,3584]{1,0:T(8,128)(2,1)S(1)} %split.107), channel_id=1, source_target_pairs={{0,96},{1,33},{32,64},{33,1},{64,32},{65,97},{96,0},{97,65},{2,98}... | collective-permute-start | bytes 946184 | tf_op jit(solution)/shard_map/ppermute | solution.py:166
  355.9 8.5 %collective-permute-start.44 = (bf16[42,3584]{1,0:T(8,128)(2,1)S(1)}, bf16[42,3584]{1,0:T(8,128)(2,1)S(1)}, u32[]{:S(2)}, u32[]{:S(2)}) collective-permute-start(bf16[42,3584]{1,0:T(8,128)(2,1)S(1)} %split.112), channel_id=1, source_target_pairs={{0,24},{1,9},{8,16},{9,1},{16,8},{17,25},{24,0},{25,17},{2,26},{3,... | collective-permute-start | bytes 903176 | tf_op jit(solution)/shard_map/ppermute | solution.py:166
  358.6 7.3 %collective-permute-start.46 = (bf16[42,3584]{1,0:T(8,128)(2,1)S(1)}, bf16[42,3584]{1,0:T(8,128)(2,1)S(1)}, u32[]{:S(2)}, u32[]{:S(2)}) collective-permute-start(bf16[42,3584]{1,0:T(8,128)(2,1)S(1)} %split.117), channel_id=1, source_target_pairs={{0,6},{1,3},{2,4},{3,1},{4,2},{5,7},{6,0},{7,5},{8,14},{9,11},{10,... | collective-permute-start | bytes 903176 | tf_op jit(solution)/shard_map/ppermute | solution.py:166
  364.6 6.1 %collective-permute-start.45 = (bf16[21,3584]{1,0:T(8,128)(2,1)S(1)}, bf16[21,3584]{1,0:T(8,128)(2,1)S(1)}, u32[]{:S(2)}, u32[]{:S(2)}) collective-permute-start(bf16[21,3584]{1,0:T(8,128)(2,1)S(1)} %split.114), channel_id=1, source_target_pairs={{0,8},{1,25},{8,0},{9,17},{16,24},{17,9},{24,16},{25,1},{2,10},{3,... | collective-permute-start | bytes 451592 | tf_op jit(solution)/shard_map/ppermute | solution.py:166
  366.0 6.7 %collective-permute-start.47 = (bf16[21,3584]{1,0:T(8,128)(2,1)S(1)}, bf16[21,3584]{1,0:T(8,128)(2,1)S(1)}, u32[]{:S(2)}, u32[]{:S(2)}) collective-permute-start(bf16[21,3584]{1,0:T(8,128)(2,1)S(1)} %split.119), channel_id=1, source_target_pairs={{0,2},{1,7},{2,0},{3,5},{4,6},{5,3},{6,4},{7,1},{8,10},{9,15},{10,... | collective-permute-start | bytes 451592 | tf_op jit(solution)/shard_map/ppermute | solution.py:166
  369.5 5.5 %collective-permute-start.43 = (bf16[22,3584]{1,0:T(8,128)(2,1)S(1)}, bf16[22,3584]{1,0:T(8,128)(2,1)S(1)}, u32[]{:S(2)}, u32[]{:S(2)}) collective-permute-start(bf16[22,3584]{1,0:T(8,128)(2,1)S(1)} %split.109), channel_id=1, source_target_pairs={{0,32},{1,97},{32,0},{33,65},{64,96},{65,33},{96,64},{97,1},{2,34}... | collective-permute-start | bytes 473096 | tf_op jit(solution)/shard_map/ppermute | solution.py:166
  (11 other events, 140.9 us)
